TPU v7x, 32 devices: a whole 2x2x4 slice. The times are simulated.
32 devices in a mesh: dp: 4 (over y, core), row: 2 (over x), col: 4 (over z).
Axes of the slice: x: 2, y: 2, z: 4, core: 2. Of those that a mesh axis runs over, the one named last changes fastest.
Arguments:
- tokens: bfloat16 [256, 6144], P(('dp', 'row', 'col')), may hold values from -6 to 6
- w_in: bfloat16 [6144, 4, 3072], P('row', 'col'), may hold values from -0.078125 to 0.078125
- w_out: bfloat16 [4, 3072, 6144], P('col', None, 'row'), may hold values from -0.0546875 to 0.0546875
- grad_out: bfloat16 [256, 6144], P(('dp', 'col'), 'row'), may hold values from -6 to 6
Outputs:
- block_out: bfloat16 [256, 6144], P(('dp', 'col'), 'row')
- grad_in: bfloat16 [256, 6144], P(('dp', 'col'), 'row')
- grad_w_in: bfloat16 [6144, 4, 3072], P('row', 'col', 'dp')
- grad_w_out: bfloat16 [4, 3072, 6144], P('col', 'dp', 'row')
All inputs are finite; a program needn't handle non-finite values.
Results may differ from a plain program's by a relative error of at most 0.015.
Values may be sent and summed in bfloat16 or wider, within the bound.
No kernel may reach another device: no remote copies, remote signals or barrier semaphores. Data moves between devices by JAX's collectives and lax.ppermute only.
A program may use at most 192 MiB of HBM per device.

v0:
```python
import jax
import jax.numpy as jnp
from jax import lax
from jax.sharding import PartitionSpec as P


def gelu_parts(preact):
    cdf = 0.5 * (1.0 + lax.erf(preact * 0.7071067811865476))
    slopes = cdf + preact * jnp.exp(-0.5 * preact * preact) * 0.3989422804014327
    return (preact * cdf, slopes)


def gather_cols(block):
    return lax.all_gather(block, "col", axis=0, tiled=True)


def gather_rows(block):
    return lax.all_gather(block, "row", axis=0, tiled=True)


def col_total(terms):
    return lax.psum_scatter(
        terms.astype(jnp.bfloat16), "col", scatter_dimension=0, tiled=True
    ).astype(jnp.float32)


def body(tokens, w_in, w_out, grad_out):
    w_first = w_in[:, 0, :]
    w_second = w_out[0]
    local_rows = gather_cols(tokens)
    across = lax.all_to_all(local_rows, "row", split_axis=1, concat_axis=0, tiled=True)
    rows_block = across
    preact = lax.psum_scatter(
        jnp.dot(rows_block, w_first, preferred_element_type=jnp.float32),
        "row",
        scatter_dimension=0,
        tiled=True,
    )
    gelu_out, slopes = gelu_parts(preact)
    hidden = gelu_out.astype(jnp.bfloat16)
    hid_full = gather_rows(hidden)
    block_out = col_total(jnp.dot(hid_full, w_second, preferred_element_type=jnp.float32)).astype(
        jnp.bfloat16
    )
    out_full = gather_cols(grad_out)
    rows_block = out_full
    back_hid = lax.psum_scatter(
        lax.dot_general(
            rows_block, w_second, (((1,), (1,)), ((), ())), preferred_element_type=jnp.float32
        ).astype(jnp.bfloat16),
        "row",
        scatter_dimension=0,
        tiled=True,
    ).astype(jnp.float32)
    grad_pre = (back_hid * slopes).astype(jnp.bfloat16)
    pre_full = gather_rows(grad_pre)
    input_terms = lax.dot_general(
        pre_full, w_first, (((1,), (1,)), ((), ())), preferred_element_type=jnp.float32
    )
    grad_in = col_total(input_terms).astype(jnp.bfloat16)
    hid_mine, pre_mine = (
        lax.all_to_all(hid_full, "dp", split_axis=1, concat_axis=0, tiled=True),
        lax.all_to_all(pre_full, "dp", split_axis=1, concat_axis=0, tiled=True),
    )
    tok_all, out_all = (
        lax.all_gather(across, "dp", axis=0, tiled=True),
        lax.all_gather(out_full, "dp", axis=0, tiled=True),
    )
    part_in = lax.dot_general(
        tok_all, pre_mine, (((0,), (0,)), ((), ())), preferred_element_type=jnp.float32
    )
    part_out = lax.dot_general(
        hid_mine, out_all, (((0,), (0,)), ((), ())), preferred_element_type=jnp.float32
    )
    summed_in = part_in[:, None, :]
    summed_out = part_out[None]
    return (block_out, grad_in, summed_in.astype(jnp.bfloat16), summed_out.astype(jnp.bfloat16))


def solution(mesh):
    in_specs = (
        P(("dp", "row", "col"), None),
        P("row", "col", None),
        P("col", None, "row"),
        P(("dp", "col"), "row"),
    )
    out_specs = (
        P(("dp", "col"), "row"),
        P(("dp", "col"), "row"),
        P("row", "col", "dp"),
        P("col", "dp", "row"),
    )
    return jax.shard_map(body, mesh=mesh, in_specs=in_specs, out_specs=out_specs, check_vma=False)
```

profile of v0, /device:TPU:0, one launch (start us, length us, event | category | flops | bytes accessed | tf_op | source)
XLA Modules:
  0.0 173.7 jit_solution(12806309776542190804)
XLA Ops:
  8.0 16.4 %all_gather.18 = bf16[32,6144]{1,0:T(8,128)(2,1)S(1)} all-gather(bf16[8,6144]{1,0:T(8,128)(2,1)} %param.4), channel_id=1, replica_groups=mesh['dp'=4,'row'=2,'col'=4] {'col'}, dimensions={0}, use_global_device_ids=true | all-gather | bytes 491520 | tf_op jit(solution)/shard_map/all_gather | solution.py:14
  24.4 0.8 copy.28
  25.2 3.5 %all-to-all-start = ((bf16[32,2,3072]{2,0,1:T(8,128)(2,1)}), bf16[32,2,3072]{2,0,1:T(8,128)(2,1)S(1)}, u32[]{:S(2)}, u32[]{:S(2)}) async-start(bf16[32,2,3072]{2,0,1:T(8,128)(2,1)} %bitcast.50), calls=%async_computation | async-start | bytes 786432 | tf_op jit(solution)/shard_map/all_to_all | solution.py:31
  28.7 0.0 reduce-scatter.9.cloned.1.call-start
  28.7 15.7 %all_gather.20 = bf16[64,3072]{1,0:T(8,128)(2,1)S(1)} all-gather(bf16[16,3072]{1,0:T(8,128)(2,1)} %param.7), channel_id=1, replica_groups=mesh['dp'=4,'row'=2,'col'=4] {'col'}, dimensions={0}, use_global_device_ids=true | all-gather | bytes 491520 | tf_op jit(solution)/shard_map/all_gather | solution.py:14
  44.5 13.1 %fusion.16 = bf16[64,3072]{1,0:T(8,128)(2,1)} fusion(bf16[64,3072]{1,0:T(8,128)(2,1)S(1)} %all_gather.20, bf16[1,3072,3072]{2,1,0:T(8,128)(2,1)} %param.6), kind=kOutput, calls=%fused_computation.14 | convolution fusion | flops 1208156160 | bytes 19660800 | tf_op jit(solution)/shard_map/dot_general | solution.py:48
  57.5 0.0 reduce-scatter.9.cloned.1.call-update
  57.6 0.0 reduce-scatter.5.cloned.1.call-start
  57.6 10.8 %fusion.6 = f32[64,3072]{1,0:T(8,128)} fusion(bf16[64,3072]{1,0:T(8,128)(2,1)S(1)} %bitcast.51, bf16[3072,1,3072]{2,0,1:T(8,128)(2,1)} %param.5), kind=kOutput, calls=%fused_computation.6 | convolution fusion | flops 1207959552 | bytes 20054016 | tf_op jit(solution)/shard_map/dot_general | solution.py:34
  68.4 0.0 all-gather.5.cloned.1.call-start
  68.5 0.5 all-gather.5.cloned.1.call-update
  69.0 0.0 all-gather.3.cloned.1.call-start
  69.1 0.5 all-gather.3.cloned.1.call-update
  69.6 2.6 %reduce-scatter.9.cloned.1.call-done = bf16[32,3072]{1,0:T(8,128)(2,1)} async-done(((bf16[64,3072]{1,0:T(8,128)(2,1)}), bf16[32,3072]{1,0:T(8,128)(2,1)}) %reduce-scatter.9.cloned.1.call-update) | async-done | bytes 196624 | tf_op jit(solution)/shard_map/reduce_scatter | solution.py:47
  72.2 20.4 %reduce-scatter.5.cloned.1.call-done = f32[32,3072]{1,0:T(8,128)} async-done(((f32[64,3072]{1,0:T(8,128)}), f32[32,3072]{1,0:T(8,128)}) %reduce-scatter.5.cloned.1.call-update) | async-done | bytes 393232 | tf_op jit(solution)/shard_map/reduce_scatter | solution.py:33
  92.6 1.2 fusion.24
  93.9 7.3 %all_gather.19 = bf16[64,3072]{1,0:T(8,128)(2,1)S(1)} all-gather(bf16[32,3072]{1,0:T(8,128)(2,1)S(1)} %get-tuple-element.21), channel_id=1, replica_groups=mesh['dp'=4,'row'=2,'col'=4] {'row'}, dimensions={0}, use_global_device_ids=true | all-gather | bytes 589824 | tf_op jit(solution)/shard_map/all_gather | solution.py:18
  101.2 0.8 copy.26
  102.0 3.5 %all-to-all-start.2 = ((bf16[64,4,768]{2,0,1:T(8,128)(2,1)}), bf16[64,4,768]{2,0,1:T(8,128)(2,1)S(1)}, u32[]{:S(2)}, u32[]{:S(2)}) async-start(bf16[64,4,768]{2,0,1:T(8,128)(2,1)} %bitcast.48), calls=%async_computation.6 | async-start | bytes 786432 | tf_op jit(solution)/shard_map/all_to_all | solution.py:62
  105.5 0.0 reduce-scatter.7.cloned.1.call-start
  105.5 7.9 %all_gather.21 = bf16[64,3072]{1,0:T(8,128)(2,1)S(1)} all-gather(bf16[32,3072]{1,0:T(8,128)(2,1)S(1)} %get-tuple-element.20), channel_id=1, replica_groups=mesh['dp'=4,'row'=2,'col'=4] {'row'}, dimensions={0}, use_global_device_ids=true | all-gather | bytes 589824 | tf_op jit(solution)/shard_map/all_gather | solution.py:18
  113.4 10.5 %fusion.13 = bf16[64,3072]{1,0:T(8,128)(2,1)} fusion(bf16[64,3072]{1,0:T(8,128)(2,1)S(1)} %all_gather.19, bf16[1,3072,3072]{2,1,0:T(8,128)(2,1)} %param.6), kind=kOutput, calls=%fused_computation.13 | convolution fusion | flops 1208156160 | bytes 19660800 | tf_op jit(solution)/shard_map/dot_general | solution.py:42
  124.0 0.2 reduce-scatter.11.cloned.1.call-start
  124.2 13.0 %fusion.10 = bf16[64,3072]{1,0:T(8,128)(2,1)} fusion(bf16[64,3072]{1,0:T(8,128)(2,1)S(1)} %all_gather.21, bf16[3072,1,3072]{2,0,1:T(8,128)(2,1)} %param.5), kind=kOutput, calls=%fused_computation.12 | convolution fusion | flops 1208156160 | bytes 19660800 | tf_op jit(solution)/shard_map/dot_general | solution.py:57
  137.2 0.8 copy.27
  138.0 3.5 %all-to-all-start.1 = ((bf16[64,4,768]{2,0,1:T(8,128)(2,1)}), bf16[64,4,768]{2,0,1:T(8,128)(2,1)S(1)}, u32[]{:S(2)}, u32[]{:S(2)}) async-start(bf16[64,4,768]{2,0,1:T(8,128)(2,1)} %bitcast.49), calls=%async_computation.5 | async-start | bytes 786432 | tf_op jit(solution)/shard_map/all_to_all | solution.py:63
  141.5 0.0 all-gather.5.cloned.1.call-done
  141.5 5.0 %fusion.9 = bf16[1,768,3072]{2,1,0:T(8,128)(2,1)} fusion(bf16[256,768]{1,0:T(8,128)(2,1)S(1)} %bitcast.55, bf16[256,3072]{1,0:T(8,128)(2,1)} %all-gather.5.cloned.1.call-done), kind=kOutput, calls=%fused_computation.11 | convolution fusion | flops 1210318848 | bytes 6684672 | tf_op jit(solution)/shard_map/dot_general | solution.py:72
  146.5 2.4 %all-to-all-done.1 = bf16[64,4,768]{2,0,1:T(8,128)(2,1)S(1)} async-done(((bf16[64,4,768]{2,0,1:T(8,128)(2,1)}), bf16[64,4,768]{2,0,1:T(8,128)(2,1)S(1)}, u32[]{:S(2)}, u32[]{:S(2)}) %all-to-all-start.1) | async-done | bytes 393248 | tf_op jit(solution)/shard_map/all_to_all | solution.py:63
  148.9 5.0 %fusion.8 = bf16[3072,1,768]{0,2,1:T(8,128)(2,1)} fusion(bf16[256,768]{1,0:T(8,128)(2,1)S(1)} %bitcast.56, bf16[256,3072]{1,0:T(8,128)(2,1)} %all-gather.3.cloned.1.call-done), kind=kOutput, calls=%fused_computation.10 | convolution fusion | flops 1210318848 | bytes 6684672 | tf_op jit(solution)/shard_map/dot_general | solution.py:69
  153.8 6.6 %copy.19 = bf16[3072,1,768]{2,0,1:T(8,128)(2,1)} copy(bf16[3072,1,768]{0,2,1:T(8,128)(2,1)} %fusion.8) | data formatting | bytes 9437184
  160.5 6.1 %reduce-scatter.11.cloned.1.call-done = bf16[16,3072]{1,0:T(8,128)(2,1)} async-done(((bf16[64,3072]{1,0:T(8,128)(2,1)}), bf16[16,3072]{1,0:T(8,128)(2,1)}) %reduce-scatter.11.cloned.1.call-update) | async-done | bytes 98320 | tf_op jit(solution)/shard_map/reduce_scatter | solution.py:22
  (11 shorter events, 0.1 us)
Async XLA Ops:
  25.2 32.4 %all-to-all-start = ((bf16[32,2,3072]{2,0,1:T(8,128)(2,1)}), bf16[32,2,3072]{2,0,1:T(8,128)(2,1)S(1)}, u32[]{:S(2)}, u32[]{:S(2)}) async-start(bf16[32,2,3072]{2,0,1:T(8,128)(2,1)} %bitcast.50), calls=%async_computation | async-start | bytes 786432 | tf_op jit(solution)/shard_map/all_to_all | solution.py:31
  28.7 43.5 %reduce-scatter.9.cloned.1.call-start = ((), (), s32[]{:S(2)}) async-start(), calls=%async_computation.9 | async-start | bytes 589824 | tf_op jit(solution)/shard_map/reduce_scatter | solution.py:47
  44.5 13.1 %copy-start.1 = (bf16[64,3072]{1,0:T(8,128)(2,1)}, bf16[64,3072]{1,0:T(8,128)(2,1)S(1)}, u32[]{:S(2)}) copy-start(bf16[64,3072]{1,0:T(8,128)(2,1)S(1)} %all_gather.20) | copy-start | bytes 1179652
  57.6 35.1 %reduce-scatter.5.cloned.1.call-start = ((), (), s32[]{:S(2)}) async-start(), calls=%async_computation.7 | async-start | bytes 1179648 | tf_op jit(solution)/shard_map/reduce_scatter | solution.py:33
  57.6 10.8 %copy-start = (bf16[32,2,3072]{2,0,1:T(8,128)(2,1)}, bf16[32,2,3072]{2,0,1:T(8,128)(2,1)S(1)}, u32[]{:S(2)}) copy-start(bf16[32,2,3072]{2,0,1:T(8,128)(2,1)S(1)} %all-to-all-done) | copy-start | bytes 1179652
  68.4 73.1 %all-gather.5.cloned.1.call-start = ((), (), s32[]{:S(2)}) async-start(), calls=%async_computation.12 | async-start | bytes 1966080 | tf_op jit(solution)/shard_map/all_gather | solution.py:67
  69.0 79.9 %all-gather.3.cloned.1.call-start = ((), (), s32[]{:S(2)}) async-start(), calls=%async_computation.11 | async-start | bytes 1966080 | tf_op jit(solution)/shard_map/all_gather | solution.py:66
  102.0 36.0 %all-to-all-start.2 = ((bf16[64,4,768]{2,0,1:T(8,128)(2,1)}), bf16[64,4,768]{2,0,1:T(8,128)(2,1)S(1)}, u32[]{:S(2)}, u32[]{:S(2)}) async-start(bf16[64,4,768]{2,0,1:T(8,128)(2,1)} %bitcast.48), calls=%async_computation.6 | async-start | bytes 786432 | tf_op jit(solution)/shard_map/all_to_all | solution.py:62
  105.5 55.0 %reduce-scatter.7.cloned.1.call-start = ((), (), s32[]{:S(2)}) async-start(), calls=%async_computation.8 | async-start | bytes 491520 | tf_op jit(solution)/shard_map/reduce_scatter | solution.py:22
  124.0 42.6 %reduce-scatter.11.cloned.1.call-start = ((), (), s32[]{:S(2)}) async-start(), calls=%async_computation.10 | async-start | bytes 491520 | tf_op jit(solution)/shard_map/reduce_scatter | solution.py:22
  138.0 10.9 %all-to-all-start.1 = ((bf16[64,4,768]{2,0,1:T(8,128)(2,1)}), bf16[64,4,768]{2,0,1:T(8,128)(2,1)S(1)}, u32[]{:S(2)}, u32[]{:S(2)}) async-start(bf16[64,4,768]{2,0,1:T(8,128)(2,1)} %bitcast.49), calls=%async_computation.5 | async-start | bytes 786432 | tf_op jit(solution)/shard_map/all_to_all | solution.py:63
Sparse Core Ops, SparseCore 0:
  57.7 14.4 reduce-scatter.8
  75.1 17.4 reduce-scatter.4
  124.1 20.7 reduce-scatter.6
  147.7 18.8 reduce-scatter.10
Sparse Core Ops, SparseCore 1:
  70.5 20.9 all-gather.4
  92.8 21.9 all-gather.2
where the time goes:
time: 174 us
  matrix products  57.3 us (33%)
  blocking collectives  47.4 us (27%)
  waiting for transfers between devices  32.7 us (19%)
  between operations  15.3 us (9%)
  starting transfers between devices  10.8 us (6%)
  local copies, waits for them, and re-layouts  8.94 us (5%)
    all_gather x2, blocking collectives, gather_cols(): return lax.all_gather(block, 'col', axis=0, tiled=True)  32.2 us
    reduce_scatter x1, waiting for transfers between devices, body(): lax.psum_scatter(jnp.dot(rows_block, w_first, preferred_element_type=jnp....  20.4 us
    all_gather x2, blocking collectives, gather_rows(): return lax.all_gather(block, 'row', axis=0, tiled=True)  15.2 us
    dot_general x1, matrix products, body(): lax.dot_general(rows_block, w_second, (((1,), (1,)), ((), ())), preferred...  13.1 us
    dot_general x1, matrix products, body(): lax.dot_general(pre_full, w_first, (((1,), (1,)), ((), ())), preferred_el...  13 us
    dot_general x1, matrix products, body(): jnp.dot(rows_block, w_first, preferred_element_type=jnp.float32)  10.8 us
    dot_general x1, matrix products, body(): jnp.dot(hid_full, w_second, preferred_element_type=jnp.float32)  10.5 us
    unnamed x5, local copies, waits for them, and re-layouts  6.62 us
  transfers between devices with their start and end apart: 9, of which 4 were waited for; matrix products, arithmetic and copies ran while one was open for 38% of the time, Pallas kernels for 0%

commit v1 on v0

v1 whole, which is shorter than its diff:
```python
import functools

import jax
import jax.numpy as jnp
from jax import lax
from jax.experimental import pallas as pl
from jax.experimental.pallas import tpu as pltpu
from jax.sharding import PartitionSpec as P

CORES = 2
VMEM_LIMIT = 60 * 1024 * 1024
NT = (((1,), (1,)), ((), ()))
NN = (((1,), (0,)), ((), ()))
TN = (((0,), (0,)), ((), ()))


def mm(a, b, dims):
    return lax.dot_general(a, b, dims, preferred_element_type=jnp.float32)


def tile_of(size, most):
    for tile in range(most, 0, -128):
        if size % tile == 0:
            return tile
    return size


def whole(*shape):
    return pl.BlockSpec(shape, lambda *_: (0,) * len(shape))


def call(kernel, grid, in_specs, out_specs, out_shape, scratch, name, flops, size, idx, *args):
    return pl.pallas_call(
        kernel,
        grid_spec=pltpu.PrefetchScalarGridSpec(
            num_scalar_prefetch=1,
            grid=grid,
            in_specs=in_specs,
            out_specs=out_specs,
            scratch_shapes=scratch,
        ),
        out_shape=out_shape,
        compiler_params=pltpu.CompilerParams(vmem_limit_bytes=VMEM_LIMIT),
        cost_estimate=pl.CostEstimate(flops=flops, bytes_accessed=size, transcendentals=0),
        name=name,
    )(idx, *args)


def first_kernel(dims, idx, own, other, w, total, sent, rows):
    half = own.shape[0]

    @pl.when((pl.program_id(0) == 0) & (pl.program_id(1) == 0))
    def _():
        rows[:half] = own[...]
        rows[half:] = other[...]

    part = mm(rows[...], w[...], dims)
    total[...] = part
    sent[...] = part.astype(jnp.bfloat16)


def first(idx, own, other, w, blocks, size, transposed, name):
    half, width = own.shape
    tile = tile_of(size, 256)
    per = size // tile
    n = 2 * half
    if transposed:
        w_spec = pl.BlockSpec((tile, width), lambda b, j, idx: (idx[b] * per + j, 0))
    else:
        w_spec = pl.BlockSpec((width, tile), lambda b, j, idx: (0, idx[b] * per + j))
    out_spec = pl.BlockSpec((n, tile), lambda b, j, idx: (0, b * per + j))
    return call(
        functools.partial(first_kernel, NT if transposed else NN),
        (blocks, per),
        [whole(half, width), whole(half, width), w_spec],
        [out_spec, out_spec],
        [
            jax.ShapeDtypeStruct((n, blocks * size), jnp.float32),
            jax.ShapeDtypeStruct((n, blocks * size), jnp.bfloat16),
        ],
        [pltpu.VMEM((n, width), jnp.bfloat16)],
        name,
        2 * n * width * blocks * size,
        2 * width * blocks * size,
        idx,
        own,
        other,
        w,
    )


def gelu_parts(preact):
    cdf = 0.5 * (1.0 + lax.erf(preact * 0.7071067811865476))
    slopes = cdf + preact * jnp.exp(-0.5 * preact * preact) * 0.3989422804014327
    return (preact * cdf, slopes)


def second_product(blocks, size, dims, vals, weights, keep, send):
    half = keep.shape[0]
    part = mm(vals[:, :size], weights[0][...], dims)
    for b in range(1, blocks):
        part += mm(vals[:, b * size : (b + 1) * size], weights[b][...], dims)
    keep[...] = part[:half]
    send[...] = part[half:].astype(jnp.bfloat16)


def forward_kernel(blocks, size, shares, idx, *refs):
    total, parts = refs[0], refs[1 : 1 + shares]
    weights = refs[1 + shares : 1 + shares + blocks]
    keep, send, slopes, *hidden, vals = refs[1 + shares + blocks :]

    @pl.when(pl.program_id(0) == 0)
    def _():
        for b in range(blocks):
            cut = slice(b * size, (b + 1) * size)
            preact = total[:, cut]
            for part in parts:
                preact = preact + part[:, cut].astype(jnp.float32)
            value, slope = gelu_parts(preact)
            value = value.astype(jnp.bfloat16)
            vals[:, cut] = value
            hidden[b][...] = value
            slopes[:, cut] = slope

    second_product(blocks, size, NN, vals, weights, keep, send)


def backward_kernel(blocks, size, shares, idx, *refs):
    total, parts = refs[0], refs[1 : 1 + shares]
    slopes = refs[1 + shares]
    weights = refs[2 + shares : 2 + shares + blocks]
    keep, send, *pre, vals = refs[2 + shares + blocks :]

    @pl.when(pl.program_id(0) == 0)
    def _():
        for b in range(blocks):
            cut = slice(b * size, (b + 1) * size)
            back = total[:, cut]
            for part in parts:
                back = back + part[:, cut].astype(jnp.float32)
            value = (back * slopes[:, cut]).astype(jnp.bfloat16)
            vals[:, cut] = value
            pre[b][...] = value

    second_product(blocks, size, NT, vals, weights, keep, send)


def second(idx, total, parts, slopes, w, blocks, size, width, name):
    n = total.shape[0]
    half = n // 2
    tile = tile_of(width, 512)
    forward = slopes is None
    if forward:
        w_specs = [
            pl.BlockSpec((size, tile), functools.partial(lambda b, j, idx: (idx[b], j), b))
            for b in range(blocks)
        ]
    else:
        w_specs = [
            pl.BlockSpec((tile, size), functools.partial(lambda b, j, idx: (j, idx[b]), b))
            for b in range(blocks)
        ]
    acts = whole(n, blocks * size)
    out_spec = pl.BlockSpec((half, tile), lambda j, idx: (0, j))
    out_specs = [out_spec, out_spec]
    out_shape = [
        jax.ShapeDtypeStruct((half, width), jnp.float32),
        jax.ShapeDtypeStruct((half, width), jnp.bfloat16),
    ]
    if forward:
        out_specs.append(acts)
        out_shape.append(jax.ShapeDtypeStruct((n, blocks * size), jnp.float32))
    out_specs += [whole(n, size)] * blocks
    out_shape += [jax.ShapeDtypeStruct((n, size), jnp.bfloat16)] * blocks
    extra = [] if forward else [slopes]
    return call(
        functools.partial(
            forward_kernel if forward else backward_kernel, blocks, size, len(parts)
        ),
        (width // tile,),
        [acts] * (1 + len(parts) + len(extra)) + w_specs,
        out_specs,
        out_shape,
        [pltpu.VMEM((n, blocks * size), jnp.bfloat16)],
        name,
        2 * n * width * blocks * size,
        2 * width * blocks * size,
        idx,
        total,
        *parts,
        *extra,
        *[w] * blocks,
    )


def weight_kernel(groups, idx, *refs):
    left, right, out = refs[:groups], refs[groups : 2 * groups], refs[2 * groups]
    total = None
    for a, b in zip(left, right):
        part = mm(a[...], b[...], TN)
        total = part if total is None else total + part
    out[...] = total.astype(jnp.bfloat16)


def weight_grad(idx, left, right, rows_tiled, name):
    n = left[0].shape[0]
    k, m = left[0].shape[1], right[0].shape[1]
    if rows_tiled:
        tile = tile_of(k, 512)
        grid = (k // tile,)
        left_spec = pl.BlockSpec((n, tile), lambda j, idx: (0, j))
        right_spec = whole(n, m)
        out_spec = pl.BlockSpec((tile, m), lambda j, idx: (j, 0))
    else:
        tile = tile_of(m, 512)
        grid = (m // tile,)
        left_spec = whole(n, k)
        right_spec = pl.BlockSpec((n, tile), lambda j, idx: (0, j))
        out_spec = pl.BlockSpec((k, tile), lambda j, idx: (0, j))
    groups = len(left)
    return call(
        functools.partial(weight_kernel, groups),
        grid,
        [left_spec] * groups + [right_spec] * groups,
        out_spec,
        jax.ShapeDtypeStruct((k, m), jnp.bfloat16),
        [],
        name,
        2 * n * groups * k * m,
        2 * k * m,
        idx,
        *left,
        *right,
    )


def body(dp, row, col, tokens, w_in, w_out, grad_out):
    blocks = dp // CORES
    w_first = w_in[:, 0, :]
    w_second = w_out[0]
    width = w_first.shape[0]
    size = w_first.shape[1] // dp
    mine = lax.axis_index("dp")
    idx = jnp.stack([(mine + CORES * b) % dp for b in range(blocks)]).astype(jnp.int32)

    other_core = [(i, i ^ 1) for i in range(dp)]

    def across_cores(x):
        return lax.ppermute(x, "dp", other_core)

    def across_y(x, step):
        return lax.ppermute(x, "dp", [(i, (i + CORES * step) % dp) for i in range(dp)])

    def across_rows(x):
        return [
            lax.ppermute(x, "row", [(i, (i + step) % row) for i in range(row)])
            for step in range(1, row)
        ]

    n = tokens.shape[0]
    spread = tokens.reshape(n, row, width).swapaxes(0, 1)
    spread = jnp.broadcast_to(spread[:, None], (row, col, n, width)).reshape(row * col, n, width)
    tok = lax.all_to_all(spread, ("row", "col"), 0, 0, tiled=True).reshape(row * col * n, width)
    m = grad_out.shape[0]
    spread_out = jnp.broadcast_to(grad_out[None], (col, m, width))
    cot = lax.all_to_all(spread_out, "col", 0, 0, tiled=True).reshape(col * m, width)

    tok_other = across_cores(tok)
    pre_total, pre_sent = first(
        idx, tok, tok_other, w_first, blocks, size, False, "preact_partial"
    )
    pre_parts = across_rows(pre_sent)
    cot_other = across_cores(cot)
    back_total, back_sent = first(
        idx, cot, cot_other, w_second, blocks, size, True, "back_partial"
    )
    back_parts = across_rows(back_sent)

    def col_total(keep, send):
        terms = (keep + across_cores(send).astype(jnp.float32)).astype(jnp.bfloat16)
        terms = lax.all_to_all(terms.reshape(col, m, width), "col", 0, 0, tiled=True)
        return jnp.sum(terms.astype(jnp.float32), axis=0).astype(jnp.bfloat16)

    keep, send, slopes, *hidden = second(
        idx, pre_total, pre_parts, None, w_second, blocks, size, width, "block_out_partial"
    )
    block_out = col_total(keep, send)
    keep, send, *grad_pre = second(
        idx, back_total, back_parts, slopes, w_first, blocks, size, width, "grad_in_partial"
    )
    grad_in = col_total(keep, send)

    def all_replicas(own, other):
        groups = [own, other]
        for b in range(1, blocks):
            there = across_y(own, b)
            groups += [there, across_cores(there)]
        return groups

    def halves(x):
        return [x[: x.shape[0] // 2], x[x.shape[0] // 2 :]]

    def to_owner(parts):
        out = halves(parts[0])
        for b in range(1, blocks):
            out += halves(across_y(parts[b], b))
        return out

    cot_all = all_replicas(cot, cot_other)
    tok_all = all_replicas(tok, tok_other)
    hid_mine = to_owner(hidden)
    pre_mine = to_owner(grad_pre)
    grad_out_w = weight_grad(idx, hid_mine, cot_all, False, "grad_w_out")
    grad_in_w = weight_grad(idx, tok_all, pre_mine, True, "grad_w_in")
    return block_out, grad_in, grad_in_w[:, None, :], grad_out_w[None]


def solution(mesh):
    in_specs = (
        P(("dp", "row", "col"), None),
        P("row", "col", None),
        P("col", None, "row"),
        P(("dp", "col"), "row"),
    )
    out_specs = (
        P(("dp", "col"), "row"),
        P(("dp", "col"), "row"),
        P("row", "col", "dp"),
        P("col", "dp", "row"),
    )
    sizes = (mesh.shape["dp"], mesh.shape["row"], mesh.shape["col"])
    return jax.shard_map(
        functools.partial(body, *sizes),
        mesh=mesh,
        in_specs=in_specs,
        out_specs=out_specs,
        check_vma=False,
    )
```

time: 174 us -> 129 us (0.74)
  matrix products: 57.3 us -> 0 us
  Pallas kernels: 0 us -> 53.2 us
  blocking collectives: 47.4 us -> 19.6 us
  between operations: 15.3 us -> 0.74 us
  waiting for transfers between devices: 32.7 us -> 20.5 us
  starting transfers between devices: 10.8 us -> 17.3 us
  other arithmetic: 1.24 us -> 4.81 us
  local copies, waits for them, and re-layouts: 8.94 us -> 10.9 us
    dot_general x6 -> x0, matrix products: 57.3 us -> none  [the longest x1 13.1 us: body(): lax.dot_general(rows_block, w_second, (((1,), (1,)), ((), ())), preferred...]
    pallas_call x0 -> x6, Pallas kernels: none -> 53.2 us  [call(): pl.pallas_call(kernel, grid_spec=pltpu.PrefetchScalarGridSpec(num_scalar_...]
    all_gather x4 -> x0, blocking collectives: 47.4 us -> none  [the longest x2 32.2 us: gather_cols(): return lax.all_gather(block, 'col', axis=0, tiled=True)]
    reduce_scatter x4 -> x0, waiting for transfers between devices: 29.2 us -> none  [the longest x1 20.4 us: body(): lax.psum_scatter(jnp.dot(rows_block, w_first, preferred_element_type=jnp....]
    all_to_all x0 -> x1, blocking collectives: none -> 19.6 us  [body(): lax.all_to_all(spread, ('row', 'col'), 0, 0, tiled=True)]
    all_to_all x3, waiting for transfers between devices: 2.36 us -> 20.4 us  [the longest x2 10.4 us: col_total(): lax.all_to_all(terms.reshape(col, m, width), 'col', 0, 0, tiled=True)]
    ppermute x0 -> x12, starting transfers between devices: none -> 6.95 us  [the longest x4 4.1 us: across_y(): lax.ppermute(x, 'dp', [(i, (i + CORES * step) % dp) for i in range(dp)])]
    slice x0 -> x4, local copies, waits for them, and re-layouts: none -> 3.72 us  [halves(): return [x[:x.shape[0] // 2], x[x.shape[0] // 2:]]]
  transfers between devices with their start and end apart: 9 -> 15, of which waited for: 4 -> 2; matrix products, arithmetic and copies ran while one was open for 38% -> 6% of each run, Pallas kernels for 0% -> 42%
where the time goes in v1:
time: 129 us; the launch traced here: 127 us
  Pallas kernels  53.2 us (41%)
  waiting for transfers between devices  20.5 us (16%)
  blocking collectives  19.6 us (15%)
  starting transfers between devices  17.3 us (13%)
  local copies, waits for them, and re-layouts  10.9 us (8%)
  other arithmetic  4.81 us (4%)
    pallas_call x6, Pallas kernels, call(): pl.pallas_call(kernel, grid_spec=pltpu.PrefetchScalarGridSpec(num_scalar_...  53.2 us
    all_to_all x1, blocking collectives, body(): lax.all_to_all(spread, ('row', 'col'), 0, 0, tiled=True)  19.6 us
    all_to_all x2, waiting for transfers between devices, col_total(): lax.all_to_all(terms.reshape(col, m, width), 'col', 0, 0, tiled=True)  10.4 us
    all_to_all x1, waiting for transfers between devices, body(): lax.all_to_all(spread_out, 'col', 0, 0, tiled=True).reshape(col * m, width)  10 us
    all_to_all x2, starting transfers between devices, col_total(): lax.all_to_all(terms.reshape(col, m, width), 'col', 0, 0, tiled=True)  6.92 us
    unnamed x24, local copies, waits for them, and re-layouts  4.54 us
    ppermute x4, starting transfers between devices, across_y(): lax.ppermute(x, 'dp', [(i, (i + CORES * step) % dp) for i in range(dp)])  4.1 us
    slice x4, local copies, waits for them, and re-layouts, halves(): return [x[:x.shape[0] // 2], x[x.shape[0] // 2:]]  3.72 us
  transfers between devices with their start and end apart: 15, of which 2 were waited for; matrix products, arithmetic and copies ran while one was open for 6% of the time, Pallas kernels for 42%

profile of v1, /device:TPU:0, one launch (start us, length us, event | category | flops | bytes accessed | tf_op | source)
XLA Modules:
  0.0 127.1 jit_solution(17586668566440604223)
XLA Ops:
  0.6 0.9 broadcast_in_dim.8
  1.6 19.6 %all_to_all.20 = bf16[8,8,3072]{2,1,0:T(8,128)(2,1)S(1)} all-to-all(bf16[8,8,3072]{2,1,0:T(8,128)(2,1)S(1)} %bitcast.30), channel_id=1, replica_groups=mesh['dp'=4,'row'=2,'col'=4] {'row','col'}, dimensions={0} | all-to-all | bytes 786432 | tf_op jit(solution)/shard_map/all_to_all | solution.py:263
  21.2 1.7 %broadcast_in_dim.9 = bf16[4,16,3072]{2,1,0:T(8,128)(2,1)} broadcast(bf16[16,3072]{1,0:T(8,128)(2,1)} %param.7), dimensions={1,2} | broadcast | bytes 491520 | tf_op jit(solution)/shard_map/broadcast_in_dim | solution.py:265
  22.9 3.5 %all-to-all-start.2 = ((bf16[4,16,3072]{2,1,0:T(8,128)(2,1)}), bf16[4,16,3072]{2,1,0:T(8,128)(2,1)S(1)}, u32[]{:S(2)}, u32[]{:S(2)}) async-start(bf16[4,16,3072]{2,1,0:T(8,128)(2,1)} %broadcast_in_dim.9), calls=%async_computation.2 | async-start | bytes 786432 | tf_op jit(solution)/shard_map/all_to_all | solution.py:266
  26.5 10.0 %all-to-all-done.2 = bf16[4,16,3072]{2,1,0:T(8,128)(2,1)S(1)} async-done(((bf16[4,16,3072]{2,1,0:T(8,128)(2,1)}), bf16[4,16,3072]{2,1,0:T(8,128)(2,1)S(1)}, u32[]{:S(2)}, u32[]{:S(2)}) %all-to-all-start.2) | async-done | bytes 393248 | tf_op jit(solution)/shard_map/all_to_all | solution.py:266
  37.1 1.5 %collective-permute-start.10 = (bf16[64,3072]{1,0:T(8,128)(2,1)S(1)}, bf16[64,3072]{1,0:T(8,128)(2,1)S(1)}, u32[]{:S(2)}, u32[]{:S(2)}) collective-permute-start(bf16[64,3072]{1,0:T(8,128)(2,1)S(1)} %bitcast.23), channel_id=1, source_target_pairs={{0,16},{8,24},{16,0},{24,8},{1,17},{9,25},{17,1},{25,9},{2,18},{10... | collective-permute-start | bytes 1179656 | tf_op jit(solution)/shard_map/ppermute | solution.py:252
  39.2 0.7 copy-done.3
  39.9 8.0 %preact_partial.1 = (f32[128,1536]{1,0:T(8,128)}, bf16[128,1536]{1,0:T(8,128)(2,1)}) custom-call(s32[2]{0:T(128)} %pad_add_fusion.idx, bf16[64,3072]{1,0:T(8,128)(2,1)} %bitcast.28, bf16[64,3072]{1,0:T(8,128)(2,1)} %copy-done.3, bf16[3072,3072]{1,0:T(8,128)(2,1)} %bitcast.17), custom_call_target="tpu_custom_call" | custom-call | flops 1207959552 | bytes 9437184 | tf_op jit(solution)/shard_map/preact_partial/pallas_call | solution.py:33
  47.9 0.9 collective-permute-start.1
  48.8 0.7 copy-done.2
  49.5 8.9 %back_partial.1 = (f32[128,1536]{1,0:T(8,128)}, bf16[128,1536]{1,0:T(8,128)(2,1)}) custom-call(s32[2]{0:T(128)} %pad_add_fusion.idx, bf16[64,3072]{1,0:T(8,128)(2,1)} %bitcast.24, bf16[64,3072]{1,0:T(8,128)(2,1)} %copy-done.2, bf16[3072,3072]{1,0:T(8,128)(2,1)} %bitcast.14), custom_call_target="tpu_custom_call" | custom-call | flops 1207959552 | bytes 9437184 | tf_op jit(solution)/shard_map/back_partial/pallas_call | solution.py:33
  58.4 1.1 collective-permute-start.4
  60.1 0.8 copy-done.6
  60.8 8.4 %block_out_partial.1 = (f32[64,3072]{1,0:T(8,128)}, bf16[64,3072]{1,0:T(8,128)(2,1)}, f32[128,1536]{1,0:T(8,128)}, bf16[128,768]{1,0:T(8,128)(2,1)}, bf16[128,768]{1,0:T(8,128)(2,1)}) custom-call(s32[2]{0:T(128)} %pad_add_fusion.idx, f32[128,1536]{1,0:T(8,128)} %get-tuple-element.17.refs_0_, bf16[128,1536]{1,0:T(8,128)(2,1)} %copy-done.6, ...), custom_call_target="tpu_custom_call" | custom-call | flops 1207959552 | bytes 9437184 | tf_op jit(solution)/shard_map/block_out_partial/pallas_call | solution.py:33
  69.2 1.6 %collective-permute-start.9 = (bf16[128,768]{1,0:T(8,128)(2,1)}, bf16[128,768]{1,0:T(8,128)(2,1)S(1)}, u32[]{:S(2)}, u32[]{:S(2)}) collective-permute-start(bf16[128,768]{1,0:T(8,128)(2,1)} %get-tuple-element.29), channel_id=1, source_target_pairs={{0,16},{8,24},{16,0},{24,8},{1,17},{9,25},{17,1},{25,9},{2,18},{10... | collective-permute-start | bytes 589832 | tf_op jit(solution)/shard_map/ppermute | solution.py:252
  70.8 0.8 copy-done.5
  71.6 9.3 %grad_in_partial.1 = (f32[64,3072]{1,0:T(8,128)}, bf16[64,3072]{1,0:T(8,128)(2,1)}, bf16[128,768]{1,0:T(8,128)(2,1)}, bf16[128,768]{1,0:T(8,128)(2,1)}) custom-call(s32[2]{0:T(128)} %pad_add_fusion.idx, f32[128,1536]{1,0:T(8,128)} %get-tuple-element.21.refs_0_, bf16[128,1536]{1,0:T(8,128)(2,1)} %copy-done.5, f32[128,1536]{1,0:T(8,128)} %get-tuple-element.23.refs_2_, ...), custom_call_target="tpu_custom_call" | custom-call | flops 1207959552 | bytes 9437184 | tf_op jit(solution)/shard_map/grad_in_partial/pallas_call | solution.py:33
  81.4 0.7 fusion.1
  82.1 1.6 %fusion.3 = (bf16[64,768]{1,0:T(8,128)(2,1)}, bf16[64,768]{1,0:T(8,128)(2,1)}) fusion(bf16[128,768]{1,0:T(8,128)(2,1)} %get-tuple-element.26), kind=kLoop, calls=%fused_computation.6 | loop fusion | bytes 393216 | tf_op jit(solution)/shard_map/slice | solution.py:301
  84.0 0.8 add_convert_fusion.1
  84.8 3.5 %all-to-all-start.1 = ((bf16[4,16,3072]{2,1,0:T(8,128)(2,1)}), bf16[4,16,3072]{2,1,0:T(8,128)(2,1)S(1)}, u32[]{:S(2)}, u32[]{:S(2)}) async-start(bf16[4,16,3072]{2,1,0:T(8,128)(2,1)} %bitcast.8), calls=%async_computation.1 | async-start | bytes 786432 | tf_op jit(solution)/shard_map/all_to_all | solution.py:281
  88.3 2.0 %add_convert_fusion = bf16[64,3072]{1,0:T(8,128)(2,1)} fusion(f32[64,3072]{1,0:T(8,128)} %get-tuple-element.24, bf16[64,3072]{1,0:T(8,128)(2,1)S(1)} %collective-permute-done.5), kind=kLoop, calls=%fused_computation | loop fusion | flops 589824 | bytes 1572864 | tf_op jit(solution)/shard_map/convert_element_type | solution.py:280
  90.2 10.4 %all-to-all-done.1 = bf16[4,16,3072]{2,1,0:T(8,128)(2,1)S(1)} async-done(((bf16[4,16,3072]{2,1,0:T(8,128)(2,1)}), bf16[4,16,3072]{2,1,0:T(8,128)(2,1)S(1)}, u32[]{:S(2)}, u32[]{:S(2)}) %all-to-all-start.1) | async-done | bytes 393248 | tf_op jit(solution)/shard_map/all_to_all | solution.py:281
  100.6 3.5 %all-to-all-start.3 = ((bf16[4,16,3072]{2,1,0:T(8,128)(2,1)}), bf16[4,16,3072]{2,1,0:T(8,128)(2,1)S(1)}, u32[]{:S(2)}, u32[]{:S(2)}) async-start(bf16[4,16,3072]{2,1,0:T(8,128)(2,1)} %bitcast.10), calls=%async_computation.3 | async-start | bytes 786432 | tf_op jit(solution)/shard_map/all_to_all | solution.py:281
  104.1 0.7 fusion.2
  104.8 0.7 copy-done.10
  105.5 9.3 %grad_w_in.1 = bf16[3072,768]{1,0:T(8,128)(2,1)} custom-call(s32[2]{0:T(128)} %pad_add_fusion.idx, bf16[64,3072]{1,0:T(8,128)(2,1)} %bitcast.29, bf16[64,3072]{1,0:T(8,128)(2,1)} %copy-done.3, bf16[64,3072]{1,0:T(8,128)(2,1)} %copy-done.8, bf16[64,3072]{1,0:T(8,128)(2,1)} %copy-done.10, bf16[64,768]{1,0:T(8,128)(2,1)} %get-tuple-element.37.refs_4_, ...), custom_call_target="tpu_custom_call" | custom-call | flops 1207959552 | bytes 4718592 | tf_op jit(solution)/shard_map/grad_w_in/pallas_call | solution.py:33
  114.9 0.7 fusion
  115.6 0.8 copy-done.9
  116.3 9.4 %grad_w_out.1 = bf16[768,3072]{1,0:T(8,128)(2,1)} custom-call(s32[2]{0:T(128)} %pad_add_fusion.idx, bf16[64,768]{1,0:T(8,128)(2,1)} %get-tuple-element.33.refs_0_, bf16[64,768]{1,0:T(8,128)(2,1)} %get-tuple-element.32.refs_1_, bf16[64,768]{1,0:T(8,128)(2,1)} %get-tuple-element.31.refs_2_, bf16[64,768]{1,0:T(8,128)(2,1)} %get-tuple-element.30.refs_3_, ...), custom_call_target="tpu_custom_call" | custom-call | flops 1207959552 | bytes 4718592 | tf_op jit(solution)/shard_map/grad_w_out/pallas_call | solution.py:33
  125.7 0.7 reduce_sum.24
  126.4 0.7 reduce_sum.25
  (40 shorter events, 2.5 us)
Async XLA Ops:
  21.2 18.0 %copy-start.1 = (bf16[8,8,3072]{2,1,0:T(8,128)(2,1)}, bf16[8,8,3072]{2,1,0:T(8,128)(2,1)S(1)}, u32[]{:S(2)}) copy-start(bf16[8,8,3072]{2,1,0:T(8,128)(2,1)S(1)} %all_to_all.20) | copy-start | bytes 1179652
  22.9 13.6 %all-to-all-start.2 = ((bf16[4,16,3072]{2,1,0:T(8,128)(2,1)}), bf16[4,16,3072]{2,1,0:T(8,128)(2,1)S(1)}, u32[]{:S(2)}, u32[]{:S(2)}) async-start(bf16[4,16,3072]{2,1,0:T(8,128)(2,1)} %broadcast_in_dim.9), calls=%async_computation.2 | async-start | bytes 786432 | tf_op jit(solution)/shard_map/all_to_all | solution.py:266
  26.4 12.8 %collective-permute-start = (bf16[64,3072]{1,0:T(8,128)(2,1)S(1)}, bf16[64,3072]{1,0:T(8,128)(2,1)S(1)}, u32[]{:S(2)}, u32[]{:S(2)}) collective-permute-start(bf16[64,3072]{1,0:T(8,128)(2,1)S(1)} %bitcast.26), channel_id=1, source_target_pairs={{0,8},{8,0},{16,24},{24,16},{1,9},{9,1},{17,25},{25,17},{2,10},{10... | collective-permute-start | bytes 1179656 | tf_op jit(solution)/shard_map/ppermute | solution.py:249
  36.5 12.3 %copy-start = (bf16[4,16,3072]{2,1,0:T(8,128)(2,1)}, bf16[4,16,3072]{2,1,0:T(8,128)(2,1)S(1)}, u32[]{:S(2)}) copy-start(bf16[4,16,3072]{2,1,0:T(8,128)(2,1)S(1)} %all-to-all-done.2) | copy-start | bytes 1179652
  36.5 12.3 %collective-permute-start.3 = (bf16[64,3072]{1,0:T(8,128)(2,1)S(1)}, bf16[64,3072]{1,0:T(8,128)(2,1)S(1)}, u32[]{:S(2)}, u32[]{:S(2)}) collective-permute-start(bf16[64,3072]{1,0:T(8,128)(2,1)S(1)} %bitcast.22), channel_id=1, source_target_pairs={{0,8},{8,0},{16,24},{24,16},{1,9},{9,1},{17,25},{25,17},{2,10},{10... | collective-permute-start | bytes 1179656 | tf_op jit(solution)/shard_map/ppermute | solution.py:249
  37.1 22.4 %collective-permute-start.10 = (bf16[64,3072]{1,0:T(8,128)(2,1)S(1)}, bf16[64,3072]{1,0:T(8,128)(2,1)S(1)}, u32[]{:S(2)}, u32[]{:S(2)}) collective-permute-start(bf16[64,3072]{1,0:T(8,128)(2,1)S(1)} %bitcast.23), channel_id=1, source_target_pairs={{0,16},{8,24},{16,0},{24,8},{1,17},{9,25},{17,1},{25,9},{2,18},{10... | collective-permute-start | bytes 1179656 | tf_op jit(solution)/shard_map/ppermute | solution.py:252
  38.7 20.9 %collective-permute-start.6 = (bf16[64,3072]{1,0:T(8,128)(2,1)S(1)}, bf16[64,3072]{1,0:T(8,128)(2,1)S(1)}, u32[]{:S(2)}, u32[]{:S(2)}) collective-permute-start(bf16[64,3072]{1,0:T(8,128)(2,1)S(1)} %bitcast.27), channel_id=1, source_target_pairs={{0,16},{8,24},{16,0},{24,8},{1,17},{9,25},{17,1},{25,9},{2,18},{10... | collective-permute-start | bytes 1179656 | tf_op jit(solution)/shard_map/ppermute | solution.py:252
  39.2 0.7 copy-start.3
  47.9 12.2 %collective-permute-start.1 = (bf16[128,1536]{1,0:T(8,128)(2,1)}, bf16[128,1536]{1,0:T(8,128)(2,1)S(1)}, u32[]{:S(2)}, u32[]{:S(2)}) collective-permute-start(bf16[128,1536]{1,0:T(8,128)(2,1)} %get-tuple-element.18), channel_id=1, source_target_pairs={{0,4},{4,0},{1,5},{5,1},{2,6},{6,2},{3,7},{7,3},{8,12},{12,8},{9,1... | collective-permute-start | bytes 1179656 | tf_op jit(solution)/shard_map/ppermute | solution.py:256
  48.8 0.8 copy-start.2
  58.4 12.4 %collective-permute-start.4 = (bf16[128,1536]{1,0:T(8,128)(2,1)}, bf16[128,1536]{1,0:T(8,128)(2,1)S(1)}, u32[]{:S(2)}, u32[]{:S(2)}) collective-permute-start(bf16[128,1536]{1,0:T(8,128)(2,1)} %get-tuple-element.22), channel_id=1, source_target_pairs={{0,4},{4,0},{1,5},{5,1},{2,6},{6,2},{3,7},{7,3},{8,12},{12,8},{9,1... | collective-permute-start | bytes 1179656 | tf_op jit(solution)/shard_map/ppermute | solution.py:256
  59.5 56.0 %copy-start.7 = (bf16[64,3072]{1,0:T(8,128)(2,1)}, bf16[64,3072]{1,0:T(8,128)(2,1)S(1)}, u32[]{:S(2)}) copy-start(bf16[64,3072]{1,0:T(8,128)(2,1)S(1)} %collective-permute-done.10.refs_6_) | copy-start | bytes 1179652
  59.5 56.0 %collective-permute-start.11 = (bf16[64,3072]{1,0:T(8,128)(2,1)S(1)}, bf16[64,3072]{1,0:T(8,128)(2,1)S(1)}, u32[]{:S(2)}, u32[]{:S(2)}) collective-permute-start(bf16[64,3072]{1,0:T(8,128)(2,1)S(1)} %collective-permute-done.10.refs_6_), channel_id=1, source_target_pairs={{0,8},{8,0},{16,24},{24,16},{1,9},{9,1},{17,25},{25,17},{2,10},{10... | collective-permute-start | bytes 1179656 | tf_op jit(solution)/shard_map/ppermute | solution.py:249
  59.6 45.2 %copy-start.8 = (bf16[64,3072]{1,0:T(8,128)(2,1)}, bf16[64,3072]{1,0:T(8,128)(2,1)S(1)}, u32[]{:S(2)}) copy-start(bf16[64,3072]{1,0:T(8,128)(2,1)S(1)} %collective-permute-done.6.refs_2_) | copy-start | bytes 1179652
  59.6 45.2 %collective-permute-start.7 = (bf16[64,3072]{1,0:T(8,128)(2,1)S(1)}, bf16[64,3072]{1,0:T(8,128)(2,1)S(1)}, u32[]{:S(2)}, u32[]{:S(2)}) collective-permute-start(bf16[64,3072]{1,0:T(8,128)(2,1)S(1)} %collective-permute-done.6.refs_2_), channel_id=1, source_target_pairs={{0,8},{8,0},{16,24},{24,16},{1,9},{9,1},{17,25},{25,17},{2,10},{10... | collective-permute-start | bytes 1179656 | tf_op jit(solution)/shard_map/ppermute | solution.py:249
  60.1 0.8 copy-start.6
  69.2 45.6 %collective-permute-start.9 = (bf16[128,768]{1,0:T(8,128)(2,1)}, bf16[128,768]{1,0:T(8,128)(2,1)S(1)}, u32[]{:S(2)}, u32[]{:S(2)}) collective-permute-start(bf16[128,768]{1,0:T(8,128)(2,1)} %get-tuple-element.29), channel_id=1, source_target_pairs={{0,16},{8,24},{16,0},{24,8},{1,17},{9,25},{17,1},{25,9},{2,18},{10... | collective-permute-start | bytes 589832 | tf_op jit(solution)/shard_map/ppermute | solution.py:252
  70.8 12.9 %collective-permute-start.2 = (bf16[64,3072]{1,0:T(8,128)(2,1)}, bf16[64,3072]{1,0:T(8,128)(2,1)S(1)}, u32[]{:S(2)}, u32[]{:S(2)}) collective-permute-start(bf16[64,3072]{1,0:T(8,128)(2,1)} %get-tuple-element.20), channel_id=1, source_target_pairs={{0,8},{8,0},{16,24},{24,16},{1,9},{9,1},{17,25},{25,17},{2,10},{10... | collective-permute-start | bytes 1179656 | tf_op jit(solution)/shard_map/ppermute | solution.py:249
  70.8 0.8 copy-start.5
  71.6 9.8 %copy-start.11 = (bf16[128,768]{1,0:T(8,128)(2,1)S(1)}, bf16[128,768]{1,0:T(8,128)(2,1)}, u32[]{:S(2)}) copy-start(bf16[128,768]{1,0:T(8,128)(2,1)} %get-tuple-element.28) | copy-start | bytes 589828
  71.6 12.4 %copy-start.4 = (f32[64,3072]{1,0:T(8,128)S(1)}, f32[64,3072]{1,0:T(8,128)}, u32[]{:S(2)}) copy-start(f32[64,3072]{1,0:T(8,128)} %get-tuple-element.19) | copy-start | bytes 2359300
  80.9 23.2 %collective-permute-start.8 = (bf16[128,768]{1,0:T(8,128)(2,1)}, bf16[128,768]{1,0:T(8,128)(2,1)S(1)}, u32[]{:S(2)}, u32[]{:S(2)}) collective-permute-start(bf16[128,768]{1,0:T(8,128)(2,1)} %get-tuple-element.27), channel_id=1, source_target_pairs={{0,16},{8,24},{16,0},{24,8},{1,17},{9,25},{17,1},{25,9},{2,18},{10... | collective-permute-start | bytes 589832 | tf_op jit(solution)/shard_map/ppermute | solution.py:252
  83.7 4.5 %collective-permute-start.5 = (bf16[64,3072]{1,0:T(8,128)(2,1)}, bf16[64,3072]{1,0:T(8,128)(2,1)S(1)}, u32[]{:S(2)}, u32[]{:S(2)}) collective-permute-start(bf16[64,3072]{1,0:T(8,128)(2,1)} %get-tuple-element.25), channel_id=1, source_target_pairs={{0,8},{8,0},{16,24},{24,16},{1,9},{9,1},{17,25},{25,17},{2,10},{10... | collective-permute-start | bytes 1179656 | tf_op jit(solution)/shard_map/ppermute | solution.py:249
  84.8 15.8 %all-to-all-start.1 = ((bf16[4,16,3072]{2,1,0:T(8,128)(2,1)}), bf16[4,16,3072]{2,1,0:T(8,128)(2,1)S(1)}, u32[]{:S(2)}, u32[]{:S(2)}) async-start(bf16[4,16,3072]{2,1,0:T(8,128)(2,1)} %bitcast.8), calls=%async_computation.1 | async-start | bytes 786432 | tf_op jit(solution)/shard_map/all_to_all | solution.py:281
  100.6 25.8 %all-to-all-start.3 = ((bf16[4,16,3072]{2,1,0:T(8,128)(2,1)}), bf16[4,16,3072]{2,1,0:T(8,128)(2,1)S(1)}, u32[]{:S(2)}, u32[]{:S(2)}) async-start(bf16[4,16,3072]{2,1,0:T(8,128)(2,1)} %bitcast.10), calls=%async_computation.3 | async-start | bytes 786432 | tf_op jit(solution)/shard_map/all_to_all | solution.py:281
  104.8 0.7 copy-start.10
  115.6 0.8 copy-start.9

commit v2 on v0

v2 whole, which is shorter than its diff:
```python
import functools

import jax
import jax.numpy as jnp
from jax import lax
from jax.experimental import pallas as pl
from jax.experimental.pallas import tpu as pltpu
from jax.sharding import PartitionSpec as P

CORES = 2
MIB = 1024 * 1024
NT = (((1,), (1,)), ((), ()))
NN = (((1,), (0,)), ((), ()))
TN = (((0,), (0,)), ((), ()))
VMEM = pl.BlockSpec(memory_space=pltpu.VMEM)
SMEM = pl.BlockSpec(memory_space=pltpu.SMEM)
HBM = pl.BlockSpec(memory_space=pltpu.HBM)


def mm(a, b, dims):
    return lax.dot_general(a, b, dims, preferred_element_type=jnp.float32)


def tile_of(size, most):
    for tile in range(most, 0, -128):
        if size % tile == 0:
            return tile
    return size


def call(kernel, in_specs, out_specs, out_shape, name, flops=0, size=0, scratch=(), limit=24):
    return pl.pallas_call(
        kernel,
        in_specs=in_specs,
        out_specs=out_specs,
        out_shape=out_shape,
        scratch_shapes=scratch,
        compiler_params=pltpu.CompilerParams(vmem_limit_bytes=limit * MIB),
        cost_estimate=pl.CostEstimate(flops=flops, bytes_accessed=size, transcendentals=0),
        name=name,
    )


def shape(dims, dtype=jnp.bfloat16):
    return jax.ShapeDtypeStruct(tuple(dims), dtype)


def load_kernel(blocks, size, pieces, place, w_first, w_second, first, second, sems):
    width = w_first.shape[0]
    copies = []
    for b in range(blocks):
        at = pl.multiple_of(place[b] * size, 128)
        for p in range(pieces):
            rows = pl.ds(p * (width // pieces), width // pieces)
            copies.append((w_first.at[rows, pl.ds(at, size)], first.at[b, rows]))
    for b in range(blocks):
        for p in range(pieces):
            rows = pl.ds(p * (size // pieces), size // pieces)
            at = pl.multiple_of(place[b] * size + p * (size // pieces), 16)
            copies.append((w_second.at[pl.ds(at, size // pieces)], second.at[b, rows]))
    copies = [pltpu.make_async_copy(a, b, sems.at[i]) for i, (a, b) in enumerate(copies)]
    for copy in copies:
        copy.start()
    for copy in copies:
        copy.wait()


def load(place, w_first, w_second, blocks, size):
    width = w_first.shape[0]
    pieces = 4
    return call(
        functools.partial(load_kernel, blocks, size, pieces),
        [SMEM, HBM, HBM],
        [VMEM, VMEM],
        [
            pltpu.VMEM((blocks, width, size), jnp.bfloat16),
            pltpu.VMEM((blocks, size, width), jnp.bfloat16),
        ],
        "load_weights",
        size=8 * blocks * width * size,
        scratch=[pltpu.SemaphoreType.DMA((2 * blocks * pieces,))],
        limit=20,
    )(place, w_first, w_second)


def order_kernel(place, *refs):
    parts, out = refs[:-1], refs[-1]
    count = len(parts)
    rows = parts[0].shape[0]
    me = place[0]
    for k, part in enumerate(parts):
        at = lax.rem(me + count - k, count) * rows
        out[pl.ds(pl.multiple_of(at, 16), rows)] = part[...]


def in_order(col_place, parts):
    rows, width = parts[0].shape
    return call(
        order_kernel,
        [SMEM] + [VMEM] * len(parts),
        VMEM,
        shape((rows * len(parts), width)),
        "order_rows",
        size=4 * rows * len(parts) * width,
    )(col_place, *parts)


def first_kernel(dims, own, other, w, total, sent, rows):
    half = own.shape[0]
    rows[:half] = own[...]
    rows[half:] = other[...]
    blocks = w.shape[0]
    size = total.shape[1] // blocks
    tile = tile_of(size, 256)
    for b in range(blocks):
        for at in range(0, size, tile):
            weight = w[b, :, at : at + tile] if dims is NN else w[b, at : at + tile, :]
            part = mm(rows[...], weight, dims)
            cut = slice(b * size + at, b * size + at + tile)
            total[:, cut] = part
            sent[:, cut] = part.astype(jnp.bfloat16)


def first(own, other, w, size, dims, name):
    half, width = own.shape
    n = 2 * half
    units = w.shape[0] * size
    return call(
        functools.partial(first_kernel, dims),
        [VMEM] * 3,
        [VMEM] * 2,
        [shape((n, units), jnp.float32), shape((n, units))],
        name,
        flops=2 * n * width * units,
        size=2 * width * units,
        scratch=[pltpu.VMEM((n, width), jnp.bfloat16)],
    )(own, other, w)


def gelu_parts(preact):
    cdf = 0.5 * (1.0 + lax.erf(preact * 0.7071067811865476))
    slopes = cdf + preact * jnp.exp(-0.5 * preact * preact) * 0.3989422804014327
    return (preact * cdf, slopes)


def second_product(dims, vals, w, keep, send):
    half, width = keep.shape
    blocks = w.shape[0]
    size = vals.shape[1] // blocks
    tile = tile_of(width, 512)
    for at in range(0, width, tile):
        cut = slice(at, at + tile)
        part = None
        for b in range(blocks):
            weight = w[b, :, cut] if dims is NN else w[b, cut, :]
            term = mm(vals[:, b * size : (b + 1) * size], weight, dims)
            part = term if part is None else part + term
        keep[:, cut] = part[:half]
        send[:, cut] = part[half:].astype(jnp.bfloat16)


def row_sum(total, parts, cut):
    whole = total[:, cut]
    for part in parts:
        whole = whole + part[:, cut].astype(jnp.float32)
    return whole


def forward_kernel(blocks, shares, *refs):
    total, parts, w = refs[0], refs[1 : 1 + shares], refs[1 + shares]
    keep, send, slopes, *hidden, vals = refs[2 + shares :]
    size = total.shape[1] // blocks
    for b in range(blocks):
        cut = slice(b * size, (b + 1) * size)
        value, slope = gelu_parts(row_sum(total, parts, cut))
        value = value.astype(jnp.bfloat16)
        vals[:, cut] = value
        hidden[b][...] = value
        slopes[:, cut] = slope
    second_product(NN, vals, w, keep, send)


def backward_kernel(blocks, shares, *refs):
    total, parts, slopes, w = refs[0], refs[1 : 1 + shares], refs[1 + shares], refs[2 + shares]
    keep, send, *pre, vals = refs[3 + shares :]
    size = total.shape[1] // blocks
    for b in range(blocks):
        cut = slice(b * size, (b + 1) * size)
        value = (row_sum(total, parts, cut) * slopes[:, cut]).astype(jnp.bfloat16)
        vals[:, cut] = value
        pre[b][...] = value
    second_product(NT, vals, w, keep, send)


def second(total, parts, slopes, w, size, name):
    n, units = total.shape
    half = n // 2
    blocks = w.shape[0]
    forward = slopes is None
    width = w.shape[2] if forward else w.shape[1]
    out_shape = [shape((half, width), jnp.float32), shape((half, width))]
    if forward:
        out_shape.append(shape((n, units), jnp.float32))
    out_shape += [shape((n, size))] * blocks
    extra = [] if forward else [slopes]
    return call(
        functools.partial(forward_kernel if forward else backward_kernel, blocks, len(parts)),
        [VMEM] * (2 + len(parts) + len(extra)),
        [VMEM] * len(out_shape),
        out_shape,
        name,
        flops=2 * n * width * units,
        size=2 * width * units,
        scratch=[pltpu.VMEM((n, units), jnp.bfloat16)],
    )(total, *parts, *extra, w)


def cores_kernel(place, keep, part, own, *sent):
    count = 1 + len(sent)
    rows = own.shape[0]
    me = place[0]
    for k in range(count):
        at = pl.ds(pl.multiple_of(lax.rem(me + k, count) * rows, 16), rows)
        whole = keep[at] + part[at].astype(jnp.float32)
        if k == 0:
            own[...] = whole
        else:
            sent[k - 1][...] = whole.astype(jnp.bfloat16)


def cores_sum(col_place, keep, part, count, name):
    rows, width = keep.shape[0] // count, keep.shape[1]
    return call(
        cores_kernel,
        [SMEM, VMEM, VMEM],
        [VMEM] * count,
        [shape((rows, width), jnp.float32)] + [shape((rows, width))] * (count - 1),
        name,
        size=8 * count * rows * width,
    )(col_place, keep, part)


def weight_kernel(lefts, tile, across, *refs):
    left, right, out = refs[:lefts], refs[lefts:-5], refs[-5]
    rows_left, rows_right, staged, sems = refs[-4:]
    for groups, rows in ((left, rows_left), (right, rows_right)):
        at = 0
        for group in groups:
            rows[at : at + group.shape[0]] = group[...]
            at += group.shape[0]
    copies = []
    for i, at in enumerate(range(0, out.shape[1 if across else 0], tile)):
        cut = slice(at, at + tile)
        if across:
            part, where = mm(rows_left[...], rows_right[:, cut], TN), (slice(None), cut)
        else:
            part, where = mm(rows_left[:, cut], rows_right[...], TN), (cut, slice(None))
        staged[where] = part.astype(jnp.bfloat16)
        copies.append(pltpu.make_async_copy(staged.at[where], out.at[where], sems.at[i]))
        copies[-1].start()
    for copy in copies:
        copy.wait()


def weight_grad(left, right, across, name):
    n = sum(group.shape[0] for group in left)
    k, m = left[0].shape[1], right[0].shape[1]
    long = m if across else k
    tile = tile_of(long, 512)
    return call(
        functools.partial(weight_kernel, len(left), tile, across),
        [VMEM] * (len(left) + len(right)),
        HBM,
        shape((k, m)),
        name,
        flops=2 * n * k * m,
        size=2 * k * m,
        scratch=[
            pltpu.VMEM((n, k), jnp.bfloat16),
            pltpu.VMEM((n, m), jnp.bfloat16),
            pltpu.VMEM((k, m), jnp.bfloat16),
            pltpu.SemaphoreType.DMA((long // tile,)),
        ],
    )(*left, *right)


def body(dp, row, col, tokens, w_in, w_out, grad_out):
    blocks = dp // CORES
    width, size = w_in.shape[0], w_in.shape[2] // dp
    mine = lax.axis_index("dp")
    place = jnp.stack([(mine + CORES * b) % dp for b in range(blocks)]).astype(jnp.int32)
    col_place = lax.axis_index("col").astype(jnp.int32)[None]

    def shifted(x, axis, step):
        count = {"dp": dp, "row": row, "col": col}[axis]
        return lax.ppermute(x, axis, [(i, (i + step) % count) for i in range(count)])

    def across_cores(x):
        return lax.ppermute(x, "dp", [(i, i ^ 1) for i in range(dp)])

    def across_rows(x):
        return [shifted(x, "row", step) for step in range(1, row)]

    n = tokens.shape[0]
    spread = tokens.reshape(n, row, width).swapaxes(0, 1)
    spread = jnp.broadcast_to(spread[:, None], (row, col, n, width)).reshape(row * col, n, width)
    tok = lax.all_to_all(spread, ("row", "col"), 0, 0, tiled=True).reshape(row * col * n, width)
    cots = [grad_out] + [shifted(grad_out, "col", step) for step in range(1, col)]
    w_first, w_second = load(place, w_in[:, 0, :], w_out[0], blocks, size)
    cot = in_order(col_place, cots)

    tok_other = across_cores(tok)
    pre_total, pre_sent = first(tok, tok_other, w_first, size, NN, "preact_partial")
    pre_parts = across_rows(pre_sent)
    cot_other = across_cores(cot)
    back_total, back_sent = first(cot, cot_other, w_second, size, NT, "back_partial")
    back_parts = across_rows(back_sent)

    def col_total(keep, send, name):
        own, *sent = cores_sum(col_place, keep, across_cores(send), col, name)
        for step, part in enumerate(sent):
            own = own + shifted(part, "col", step + 1).astype(jnp.float32)
        return own.astype(jnp.bfloat16)

    keep, send, slopes, *hidden = second(
        pre_total, pre_parts, None, w_second, size, "block_out_partial"
    )
    block_out = col_total(keep, send, "block_out_cores")
    keep, send, *grad_pre = second(
        back_total, back_parts, slopes, w_first, size, "grad_in_partial"
    )
    grad_in = col_total(keep, send, "grad_in_cores")

    def all_replicas(own, other):
        groups = [own, other]
        for b in range(1, blocks):
            there = shifted(own, "dp", CORES * b)
            groups += [there, across_cores(there)]
        return groups

    def to_owner(parts):
        return [parts[0]] + [shifted(parts[b], "dp", CORES * b) for b in range(1, blocks)]

    cot_all = all_replicas(cot, cot_other)
    tok_all = all_replicas(tok, tok_other)
    grad_out_w = weight_grad(to_owner(hidden), cot_all, True, "grad_w_out")
    grad_in_w = weight_grad(tok_all, to_owner(grad_pre), False, "grad_w_in")
    return block_out, grad_in, grad_in_w[:, None, :], grad_out_w[None]


def solution(mesh):
    in_specs = (
        P(("dp", "row", "col"), None),
        P("row", "col", None),
        P("col", None, "row"),
        P(("dp", "col"), "row"),
    )
    out_specs = (
        P(("dp", "col"), "row"),
        P(("dp", "col"), "row"),
        P("row", "col", "dp"),
        P("col", "dp", "row"),
    )
    sizes = (mesh.shape["dp"], mesh.shape["row"], mesh.shape["col"])
    return jax.shard_map(
        functools.partial(body, *sizes),
        mesh=mesh,
        in_specs=in_specs,
        out_specs=out_specs,
        check_vma=False,
    )
```

time: 174 us -> 97.1 us (0.56)
  matrix products: 57.3 us -> 0 us
  blocking collectives: 47.4 us -> 19.6 us
  Pallas kernels: 0 us -> 22.1 us
  between operations: 15.3 us -> 0.77 us
  starting transfers between devices: 10.8 us -> 18.9 us
  local copies, waits for them, and re-layouts: 8.94 us -> 1.81 us
    dot_general x6 -> x0, matrix products: 57.3 us -> none  [the longest x1 13.1 us: body(): lax.dot_general(rows_block, w_second, (((1,), (1,)), ((), ())), preferred...]
    all_gather x4 -> x0, blocking collectives: 47.4 us -> none  [the longest x2 32.2 us: gather_cols(): return lax.all_gather(block, 'col', axis=0, tiled=True)]
    ppermute x0 -> x21, waiting for transfers between devices: none -> 32.2 us  [the longest x15 32.2 us: shifted(): lax.ppermute(x, axis, [(i, (i + step) % count) for i in range(count)])]
    reduce_scatter x4 -> x0, waiting for transfers between devices: 29.2 us -> none  [the longest x1 20.4 us: body(): lax.psum_scatter(jnp.dot(rows_block, w_first, preferred_element_type=jnp....]
    pallas_call x0 -> x10, Pallas kernels: none -> 22.1 us  [the longest x1 7.13 us: load(): call(functools.partial(load_kernel, blocks, size, pieces), [SMEM, HBM, HB...]
    all_to_all x0 -> x1, blocking collectives: none -> 19.6 us  [body(): lax.all_to_all(spread, ('row', 'col'), 0, 0, tiled=True)]
    ppermute x0 -> x21, starting transfers between devices: none -> 18.9 us  [the longest x15 18.2 us: shifted(): lax.ppermute(x, axis, [(i, (i + step) % count) for i in range(count)])]
    all_to_all x3 -> x0, starting transfers between devices: 10.4 us -> none  [the longest x1 3.47 us: body(): lax.all_to_all(local_rows, 'row', split_axis=1, concat_axis=0, tiled=True)]
  transfers between devices with their start and end apart: 9 -> 21, of which waited for: 4 -> 7; matrix products, arithmetic and copies ran while one was open for 38% -> 1% of each run, Pallas kernels for 0% -> 23%
where the time goes in v2:
time: 97.1 us; the launch traced here: 96.9 us
  waiting for transfers between devices  32.2 us (33%)
  Pallas kernels  22.1 us (23%)
  blocking collectives  19.6 us (20%)
  starting transfers between devices  18.9 us (19%)
  local copies, waits for them, and re-layouts  1.81 us (2%)
  other arithmetic  1.45 us (1%)
    ppermute x15, waiting for transfers between devices, shifted(): lax.ppermute(x, axis, [(i, (i + step) % count) for i in range(count)])  32.2 us
    all_to_all x1, blocking collectives, body(): lax.all_to_all(spread, ('row', 'col'), 0, 0, tiled=True)  19.6 us
    ppermute x15, starting transfers between devices, shifted(): lax.ppermute(x, axis, [(i, (i + step) % count) for i in range(count)])  18.2 us
    pallas_call x1, Pallas kernels, load(): call(functools.partial(load_kernel, blocks, size, pieces), [SMEM, HBM, HB...  7.13 us
    pallas_call x2, Pallas kernels, weight_grad(): call(functools.partial(weight_kernel, len(left), tile, across), [VMEM] *...  5.33 us
    pallas_call x2, Pallas kernels, second(): call(functools.partial(forward_kernel if forward else backward_kernel, bl...  4.81 us
    pallas_call x2, Pallas kernels, first(): call(functools.partial(first_kernel, dims), [VMEM] * 3, [VMEM] * 2, [shap...  4.64 us
  transfers between devices with their start and end apart: 21, of which 7 were waited for; matrix products, arithmetic and copies ran while one was open for 1% of the time, Pallas kernels for 23%

profile of v2, /device:TPU:0, one launch (start us, length us, event | category | flops | bytes accessed | tf_op | source)
XLA Modules:
  0.0 96.9 jit_solution(12679493132282710667)
XLA Ops:
  0.6 0.9 broadcast_in_dim.16
  1.6 19.6 %all_to_all.5 = bf16[8,8,3072]{2,1,0:T(8,128)(2,1)S(1)} all-to-all(bf16[8,8,3072]{2,1,0:T(8,128)(2,1)S(1)} %bitcast.20), channel_id=1, replica_groups=mesh['dp'=4,'row'=2,'col'=4] {'row','col'}, dimensions={0} | all-to-all | bytes 786432 | tf_op jit(solution)/shard_map/all_to_all | solution.py:307
  21.4 0.9 collective-permute-start.7
  22.3 2.7 %collective-permute-start.8 = (bf16[16,3072]{1,0:T(8,128)(2,1)}, bf16[16,3072]{1,0:T(8,128)(2,1)S(1)}, u32[]{:S(2)}, u32[]{:S(2)}) collective-permute-start(bf16[16,3072]{1,0:T(8,128)(2,1)} %refs_0_.1), channel_id=1, source_target_pairs={{0,3},{1,0},{2,1},{3,2},{4,7},{5,4},{6,5},{7,6},{8,11},{9,8},{10,9... | collective-permute-start | bytes 294920 | tf_op jit(solution)/shard_map/ppermute | solution.py:296
  25.0 3.9 %collective-permute-done.6.refs_1_ = bf16[16,3072]{1,0:T(8,128)(2,1)S(1)} collective-permute-done((bf16[16,3072]{1,0:T(8,128)(2,1)}, bf16[16,3072]{1,0:T(8,128)(2,1)S(1)}, u32[]{:S(2)}, u32[]{:S(2)}) %collective-permute-start.6) | collective-permute-done | bytes 98336 | tf_op jit(solution)/shard_map/ppermute | solution.py:296
  28.9 3.5 %collective-permute-done.7.refs_2_ = bf16[16,3072]{1,0:T(8,128)(2,1)S(1)} collective-permute-done((bf16[16,3072]{1,0:T(8,128)(2,1)}, bf16[16,3072]{1,0:T(8,128)(2,1)S(1)}, u32[]{:S(2)}, u32[]{:S(2)}) %collective-permute-start.7) | collective-permute-done | bytes 98336 | tf_op jit(solution)/shard_map/ppermute | solution.py:296
  32.3 0.9 copy-done
  33.4 7.1 %load_weights.1 = (bf16[2,3072,768]{2,1,0:T(8,128)(2,1)S(1)}, bf16[2,768,3072]{2,1,0:T(8,128)(2,1)S(1)}) custom-call(s32[2]{0:T(128)S(1)} %pad_add_fusion.place, bf16[3072,3072]{1,0:T(8,128)(2,1)} %bitcast.16, bf16[3072,3072]{1,0:T(8,128)(2,1)} %bitcast.17), custom_call_target="tpu_custom_call" | custom-call | bytes 37748736 | tf_op jit(solution)/shard_map/load_weights/pallas_call | solution.py:71
  40.6 1.6 %collective-permute-start.19 = (bf16[64,3072]{1,0:T(8,128)(2,1)S(1)}, bf16[64,3072]{1,0:T(8,128)(2,1)S(1)}, u32[]{:S(2)}, u32[]{:S(2)}) collective-permute-start(bf16[64,3072]{1,0:T(8,128)(2,1)S(1)} %order_rows.1.own.refs_2_), channel_id=1, source_target_pairs={{0,16},{8,24},{16,0},{24,8},{1,17},{9,25},{17,1},{25,9},{2,18},{10... | collective-permute-start | bytes 1179656 | tf_op jit(solution)/shard_map/ppermute | solution.py:296
  42.2 0.5 collective-permute-start.15
  42.7 1.4 %preact_partial.1 = (f32[128,1536]{1,0:T(8,128)S(1)}, bf16[128,1536]{1,0:T(8,128)(2,1)S(1)}) custom-call(bf16[64,3072]{1,0:T(8,128)(2,1)S(1)} %bitcast.14, bf16[64,3072]{1,0:T(8,128)(2,1)S(1)} %collective-permute-done.other.refs_1_, bf16[2,3072,768]{2,1,0:T(8,128)(2,1)S(1)} %get-tuple-element.27.w.refs_3_), custom_call_target="tpu_custom_call" | custom-call | flops 1207959552 | bytes 9437184 | tf_op jit(solution)/shard_map/preact_partial/pallas_call | solution.py:128
  44.1 0.6 collective-permute-start.1
  44.8 3.2 %back_partial.1 = (f32[128,1536]{1,0:T(8,128)S(1)}, bf16[128,1536]{1,0:T(8,128)(2,1)S(1)}) custom-call(bf16[64,3072]{1,0:T(8,128)(2,1)S(1)} %order_rows.1.own.refs_2_, bf16[64,3072]{1,0:T(8,128)(2,1)S(1)} %collective-permute-done.9.other.refs_3_, bf16[2,768,3072]{2,1,0:T(8,128)(2,1)S(1)} %get-tuple-element.30.refs_2_.w), custom_call_target="tpu_custom_call" | custom-call | flops 1207959552 | bytes 9437184 | tf_op jit(solution)/shard_map/back_partial/pallas_call | solution.py:128
  48.0 1.5 %collective-permute-start.10 = (bf16[128,1536]{1,0:T(8,128)(2,1)S(1)}, bf16[128,1536]{1,0:T(8,128)(2,1)S(1)}, u32[]{:S(2)}, u32[]{:S(2)}) collective-permute-start(bf16[128,1536]{1,0:T(8,128)(2,1)S(1)} %get-tuple-element.38), channel_id=1, source_target_pairs={{0,4},{4,0},{1,5},{5,1},{2,6},{6,2},{3,7},{7,3},{8,12},{12,8},{9,1... | collective-permute-start | bytes 1179656 | tf_op jit(solution)/shard_map/ppermute | solution.py:296
  49.5 11.1 %collective-permute-done.15.refs_2_ = bf16[64,3072]{1,0:T(8,128)(2,1)S(1)} collective-permute-done((bf16[64,3072]{1,0:T(8,128)(2,1)S(1)}, bf16[64,3072]{1,0:T(8,128)(2,1)S(1)}, u32[]{:S(2)}, u32[]{:S(2)}) %collective-permute-start.15) | collective-permute-done | bytes 393248 | tf_op jit(solution)/shard_map/ppermute | solution.py:296
  60.6 0.5 collective-permute-start.20
  61.1 1.7 %block_out_partial.1 = (f32[64,3072]{1,0:T(8,128)S(1)}, bf16[64,3072]{1,0:T(8,128)(2,1)S(1)}, f32[128,1536]{1,0:T(8,128)S(1)}, bf16[128,768]{1,0:T(8,128)(2,1)S(1)}, bf16[128,768]{1,0:T(8,128)(2,1)S(1)}) custom-call(f32[128,1536]{1,0:T(8,128)S(1)} %get-tuple-element.28.refs_0_, bf16[128,1536]{1,0:T(8,128)(2,1)S(1)} %collective-permute-done.1.refs_1_, ...), custom_call_target="tpu_custom_call" | custom-call | flops 1207959552 | bytes 9437184 | tf_op jit(solution)/shard_map/block_out_partial/pallas_call | solution.py:206
  62.9 0.7 collective-permute-done.10.refs_1_
  63.6 3.1 %grad_in_partial.1 = (f32[64,3072]{1,0:T(8,128)S(1)}, bf16[64,3072]{1,0:T(8,128)(2,1)S(1)}, bf16[128,768]{1,0:T(8,128)(2,1)S(1)}, bf16[128,768]{1,0:T(8,128)(2,1)S(1)}) custom-call(f32[128,1536]{1,0:T(8,128)S(1)} %get-tuple-element.37.refs_0_, bf16[128,1536]{1,0:T(8,128)(2,1)S(1)} %collective-permute-done.10.refs_1_, ...), custom_call_target="tpu_custom_call" | custom-call | flops 1207959552 | bytes 9437184 | tf_op jit(solution)/shard_map/grad_in_partial/pallas_call | solution.py:206
  66.8 1.6 %collective-permute-start.17 = (bf16[128,768]{1,0:T(8,128)(2,1)S(1)}, bf16[128,768]{1,0:T(8,128)(2,1)S(1)}, u32[]{:S(2)}, u32[]{:S(2)}) collective-permute-start(bf16[128,768]{1,0:T(8,128)(2,1)S(1)} %get-tuple-element.47), channel_id=1, source_target_pairs={{0,16},{8,24},{16,0},{24,8},{1,17},{9,25},{17,1},{25,9},{2,18},{10... | collective-permute-start | bytes 589832 | tf_op jit(solution)/shard_map/ppermute | solution.py:296
  68.3 0.5 collective-permute-start.18
  68.9 5.8 %collective-permute-done.17.refs_5_ = bf16[128,768]{1,0:T(8,128)(2,1)S(1)} collective-permute-done((bf16[128,768]{1,0:T(8,128)(2,1)S(1)}, bf16[128,768]{1,0:T(8,128)(2,1)S(1)}, u32[]{:S(2)}, u32[]{:S(2)}) %collective-permute-start.17) | collective-permute-done | bytes 196640 | tf_op jit(solution)/shard_map/ppermute | solution.py:296
  74.6 2.7 %grad_w_in.1 = bf16[3072,768]{1,0:T(8,128)(2,1)} custom-call(bf16[64,3072]{1,0:T(8,128)(2,1)S(1)} %bitcast.15, bf16[64,3072]{1,0:T(8,128)(2,1)S(1)} %collective-permute-done.other.refs_1_, bf16[64,3072]{1,0:T(8,128)(2,1)S(1)} %collective-permute-done.15.refs_2_, bf16[64,3072]{1,0:T(8,128)(2,1)S(1)} %collective-permute-done.16.refs_3_, ...), custom_call_target="tpu_custom_call" | custom-call | flops 1207959552 | bytes 4718592 | tf_op jit(solution)/shard_map/grad_w_in/pallas_call | solution.py:270
  77.4 2.7 %collective-permute-start.5 = (bf16[16,3072]{1,0:T(8,128)(2,1)S(1)}, bf16[16,3072]{1,0:T(8,128)(2,1)S(1)}, u32[]{:S(2)}, u32[]{:S(2)}) collective-permute-start(bf16[16,3072]{1,0:T(8,128)(2,1)S(1)} %get-tuple-element.36), channel_id=1, source_target_pairs={{0,3},{1,0},{2,1},{3,2},{4,7},{5,4},{6,5},{7,6},{8,11},{9,8},{10,9... | collective-permute-start | bytes 294920 | tf_op jit(solution)/shard_map/ppermute | solution.py:296
  80.1 0.9 collective-permute-start.4
  81.0 2.6 %grad_w_out.1 = bf16[768,3072]{1,0:T(8,128)(2,1)} custom-call(bf16[128,768]{1,0:T(8,128)(2,1)S(1)} %get-tuple-element.48.refs_0_, bf16[128,768]{1,0:T(8,128)(2,1)S(1)} %collective-permute-done.18.refs_1_, bf16[64,3072]{1,0:T(8,128)(2,1)S(1)} %order_rows.1.own.refs_2_, bf16[64,3072]{1,0:T(8,128)(2,1)S(1)} %collective-permute-done.9.other.refs_3_, ...), custom_call_target="tpu_custom_call" | custom-call | flops 1207959552 | bytes 4718592 | tf_op jit(solution)/shard_map/grad_w_out/pallas_call | solution.py:270
  83.8 3.9 %collective-permute-start.14 = (bf16[16,3072]{1,0:T(8,128)(2,1)S(1)}, bf16[16,3072]{1,0:T(8,128)(2,1)S(1)}, u32[]{:S(2)}, u32[]{:S(2)}) collective-permute-start(bf16[16,3072]{1,0:T(8,128)(2,1)S(1)} %get-tuple-element.45), channel_id=1, source_target_pairs={{0,3},{1,0},{2,1},{3,2},{4,7},{5,4},{6,5},{7,6},{8,11},{9,8},{10,9... | collective-permute-start | bytes 294920 | tf_op jit(solution)/shard_map/ppermute | solution.py:296
  87.9 0.4 collective-permute-start.12
  88.3 4.0 %collective-permute-done.4 = bf16[16,3072]{1,0:T(8,128)(2,1)S(1)} collective-permute-done((bf16[16,3072]{1,0:T(8,128)(2,1)S(1)}, bf16[16,3072]{1,0:T(8,128)(2,1)S(1)}, u32[]{:S(2)}, u32[]{:S(2)}) %collective-permute-start.4) | collective-permute-done | bytes 98336 | tf_op jit(solution)/shard_map/ppermute | solution.py:296
  92.3 0.7 add_convert_fusion.1
  93.0 3.2 %collective-permute-done.13 = bf16[16,3072]{1,0:T(8,128)(2,1)S(1)} collective-permute-done((bf16[16,3072]{1,0:T(8,128)(2,1)S(1)}, bf16[16,3072]{1,0:T(8,128)(2,1)S(1)}, u32[]{:S(2)}, u32[]{:S(2)}) %collective-permute-start.13) | collective-permute-done | bytes 98336 | tf_op jit(solution)/shard_map/ppermute | solution.py:296
  96.2 0.7 add_convert_fusion
  (27 shorter events, 1.0 us)
Async XLA Ops:
  21.2 21.5 %collective-permute-start = (bf16[64,3072]{1,0:T(8,128)(2,1)S(1)}, bf16[64,3072]{1,0:T(8,128)(2,1)S(1)}, u32[]{:S(2)}, u32[]{:S(2)}) collective-permute-start(bf16[64,3072]{1,0:T(8,128)(2,1)S(1)} %bitcast.12), channel_id=1, source_target_pairs={{0,8},{8,0},{16,24},{24,16},{1,9},{9,1},{17,25},{25,17},{2,10},{10... | collective-permute-start | bytes 1179656 | tf_op jit(solution)/shard_map/ppermute | solution.py:299
  21.2 7.7 %collective-permute-start.6 = (bf16[16,3072]{1,0:T(8,128)(2,1)}, bf16[16,3072]{1,0:T(8,128)(2,1)S(1)}, u32[]{:S(2)}, u32[]{:S(2)}) collective-permute-start(bf16[16,3072]{1,0:T(8,128)(2,1)} %refs_0_.1), channel_id=1, source_target_pairs={{0,1},{1,2},{2,3},{3,0},{4,5},{5,6},{6,7},{7,4},{8,9},{9,10},{10,1... | collective-permute-start | bytes 294920 | tf_op jit(solution)/shard_map/ppermute | solution.py:296
  21.4 10.9 %collective-permute-start.7 = (bf16[16,3072]{1,0:T(8,128)(2,1)}, bf16[16,3072]{1,0:T(8,128)(2,1)S(1)}, u32[]{:S(2)}, u32[]{:S(2)}) collective-permute-start(bf16[16,3072]{1,0:T(8,128)(2,1)} %refs_0_.1), channel_id=1, source_target_pairs={{0,2},{1,3},{2,0},{3,1},{4,6},{5,7},{6,4},{7,5},{8,10},{9,11},{10,... | collective-permute-start | bytes 294920 | tf_op jit(solution)/shard_map/ppermute | solution.py:296
  22.3 10.0 %collective-permute-start.8 = (bf16[16,3072]{1,0:T(8,128)(2,1)}, bf16[16,3072]{1,0:T(8,128)(2,1)S(1)}, u32[]{:S(2)}, u32[]{:S(2)}) collective-permute-start(bf16[16,3072]{1,0:T(8,128)(2,1)} %refs_0_.1), channel_id=1, source_target_pairs={{0,3},{1,0},{2,1},{3,2},{4,7},{5,4},{6,5},{7,6},{8,11},{9,8},{10,9... | collective-permute-start | bytes 294920 | tf_op jit(solution)/shard_map/ppermute | solution.py:296
  32.3 0.9 copy-start
  33.3 11.5 %collective-permute-start.9 = (bf16[64,3072]{1,0:T(8,128)(2,1)S(1)}, bf16[64,3072]{1,0:T(8,128)(2,1)S(1)}, u32[]{:S(2)}, u32[]{:S(2)}) collective-permute-start(bf16[64,3072]{1,0:T(8,128)(2,1)S(1)} %order_rows.1.own.refs_2_), channel_id=1, source_target_pairs={{0,8},{8,0},{16,24},{24,16},{1,9},{9,1},{17,25},{25,17},{2,10},{10... | collective-permute-start | bytes 1179656 | tf_op jit(solution)/shard_map/ppermute | solution.py:299
  40.6 20.0 %collective-permute-start.19 = (bf16[64,3072]{1,0:T(8,128)(2,1)S(1)}, bf16[64,3072]{1,0:T(8,128)(2,1)S(1)}, u32[]{:S(2)}, u32[]{:S(2)}) collective-permute-start(bf16[64,3072]{1,0:T(8,128)(2,1)S(1)} %order_rows.1.own.refs_2_), channel_id=1, source_target_pairs={{0,16},{8,24},{16,0},{24,8},{1,17},{9,25},{17,1},{25,9},{2,18},{10... | collective-permute-start | bytes 1179656 | tf_op jit(solution)/shard_map/ppermute | solution.py:296
  42.2 18.4 %collective-permute-start.15 = (bf16[64,3072]{1,0:T(8,128)(2,1)S(1)}, bf16[64,3072]{1,0:T(8,128)(2,1)S(1)}, u32[]{:S(2)}, u32[]{:S(2)}) collective-permute-start(bf16[64,3072]{1,0:T(8,128)(2,1)S(1)} %bitcast.13), channel_id=1, source_target_pairs={{0,16},{8,24},{16,0},{24,8},{1,17},{9,25},{17,1},{25,9},{2,18},{10... | collective-permute-start | bytes 1179656 | tf_op jit(solution)/shard_map/ppermute | solution.py:296
  44.1 17.0 %collective-permute-start.1 = (bf16[128,1536]{1,0:T(8,128)(2,1)S(1)}, bf16[128,1536]{1,0:T(8,128)(2,1)S(1)}, u32[]{:S(2)}, u32[]{:S(2)}) collective-permute-start(bf16[128,1536]{1,0:T(8,128)(2,1)S(1)} %get-tuple-element.29), channel_id=1, source_target_pairs={{0,4},{4,0},{1,5},{5,1},{2,6},{6,2},{3,7},{7,3},{8,12},{12,8},{9,1... | collective-permute-start | bytes 1179656 | tf_op jit(solution)/shard_map/ppermute | solution.py:296
  48.0 15.6 %collective-permute-start.10 = (bf16[128,1536]{1,0:T(8,128)(2,1)S(1)}, bf16[128,1536]{1,0:T(8,128)(2,1)S(1)}, u32[]{:S(2)}, u32[]{:S(2)}) collective-permute-start(bf16[128,1536]{1,0:T(8,128)(2,1)S(1)} %get-tuple-element.38), channel_id=1, source_target_pairs={{0,4},{4,0},{1,5},{5,1},{2,6},{6,2},{3,7},{7,3},{8,12},{12,8},{9,1... | collective-permute-start | bytes 1179656 | tf_op jit(solution)/shard_map/ppermute | solution.py:296
  60.6 7.7 %collective-permute-start.16 = (bf16[64,3072]{1,0:T(8,128)(2,1)S(1)}, bf16[64,3072]{1,0:T(8,128)(2,1)S(1)}, u32[]{:S(2)}, u32[]{:S(2)}) collective-permute-start(bf16[64,3072]{1,0:T(8,128)(2,1)S(1)} %collective-permute-done.15.refs_2_), channel_id=1, source_target_pairs={{0,8},{8,0},{16,24},{24,16},{1,9},{9,1},{17,25},{25,17},{2,10},{10... | collective-permute-start | bytes 1179656 | tf_op jit(solution)/shard_map/ppermute | solution.py:299
  60.6 20.4 %collective-permute-start.20 = (bf16[64,3072]{1,0:T(8,128)(2,1)S(1)}, bf16[64,3072]{1,0:T(8,128)(2,1)S(1)}, u32[]{:S(2)}, u32[]{:S(2)}) collective-permute-start(bf16[64,3072]{1,0:T(8,128)(2,1)S(1)} %collective-permute-done.19.refs_4_), channel_id=1, source_target_pairs={{0,8},{8,0},{16,24},{24,16},{1,9},{9,1},{17,25},{25,17},{2,10},{10... | collective-permute-start | bytes 1179656 | tf_op jit(solution)/shard_map/ppermute | solution.py:299
  62.8 14.5 %collective-permute-start.2 = (bf16[64,3072]{1,0:T(8,128)(2,1)S(1)}, bf16[64,3072]{1,0:T(8,128)(2,1)S(1)}, u32[]{:S(2)}, u32[]{:S(2)}) collective-permute-start(bf16[64,3072]{1,0:T(8,128)(2,1)S(1)} %get-tuple-element.32), channel_id=1, source_target_pairs={{0,8},{8,0},{16,24},{24,16},{1,9},{9,1},{17,25},{25,17},{2,10},{10... | collective-permute-start | bytes 1179656 | tf_op jit(solution)/shard_map/ppermute | solution.py:299
  66.8 7.9 %collective-permute-start.17 = (bf16[128,768]{1,0:T(8,128)(2,1)S(1)}, bf16[128,768]{1,0:T(8,128)(2,1)S(1)}, u32[]{:S(2)}, u32[]{:S(2)}) collective-permute-start(bf16[128,768]{1,0:T(8,128)(2,1)S(1)} %get-tuple-element.47), channel_id=1, source_target_pairs={{0,16},{8,24},{16,0},{24,8},{1,17},{9,25},{17,1},{25,9},{2,18},{10... | collective-permute-start | bytes 589832 | tf_op jit(solution)/shard_map/ppermute | solution.py:296
  68.3 15.3 %collective-permute-start.11 = (bf16[64,3072]{1,0:T(8,128)(2,1)S(1)}, bf16[64,3072]{1,0:T(8,128)(2,1)S(1)}, u32[]{:S(2)}, u32[]{:S(2)}) collective-permute-start(bf16[64,3072]{1,0:T(8,128)(2,1)S(1)} %get-tuple-element.41), channel_id=1, source_target_pairs={{0,8},{8,0},{16,24},{24,16},{1,9},{9,1},{17,25},{25,17},{2,10},{10... | collective-permute-start | bytes 1179656 | tf_op jit(solution)/shard_map/ppermute | solution.py:299
  68.3 12.7 %collective-permute-start.18 = (bf16[128,768]{1,0:T(8,128)(2,1)S(1)}, bf16[128,768]{1,0:T(8,128)(2,1)S(1)}, u32[]{:S(2)}, u32[]{:S(2)}) collective-permute-start(bf16[128,768]{1,0:T(8,128)(2,1)S(1)} %get-tuple-element.49), channel_id=1, source_target_pairs={{0,16},{8,24},{16,0},{24,8},{1,17},{9,25},{17,1},{25,9},{2,18},{10... | collective-permute-start | bytes 589832 | tf_op jit(solution)/shard_map/ppermute | solution.py:296
  77.4 10.5 %collective-permute-start.5 = (bf16[16,3072]{1,0:T(8,128)(2,1)S(1)}, bf16[16,3072]{1,0:T(8,128)(2,1)S(1)}, u32[]{:S(2)}, u32[]{:S(2)}) collective-permute-start(bf16[16,3072]{1,0:T(8,128)(2,1)S(1)} %get-tuple-element.36), channel_id=1, source_target_pairs={{0,3},{1,0},{2,1},{3,2},{4,7},{5,4},{6,5},{7,6},{8,11},{9,8},{10,9... | collective-permute-start | bytes 294920 | tf_op jit(solution)/shard_map/ppermute | solution.py:296
  80.1 12.2 %collective-permute-start.4 = (bf16[16,3072]{1,0:T(8,128)(2,1)S(1)}, bf16[16,3072]{1,0:T(8,128)(2,1)S(1)}, u32[]{:S(2)}, u32[]{:S(2)}) collective-permute-start(bf16[16,3072]{1,0:T(8,128)(2,1)S(1)} %get-tuple-element.35), channel_id=1, source_target_pairs={{0,2},{1,3},{2,0},{3,1},{4,6},{5,7},{6,4},{7,5},{8,10},{9,11},{10,... | collective-permute-start | bytes 294920 | tf_op jit(solution)/shard_map/ppermute | solution.py:296
  81.0 11.3 %collective-permute-start.3 = (bf16[16,3072]{1,0:T(8,128)(2,1)S(1)}, bf16[16,3072]{1,0:T(8,128)(2,1)S(1)}, u32[]{:S(2)}, u32[]{:S(2)}) collective-permute-start(bf16[16,3072]{1,0:T(8,128)(2,1)S(1)} %get-tuple-element.34), channel_id=1, source_target_pairs={{0,1},{1,2},{2,3},{3,0},{4,5},{5,6},{6,7},{7,4},{8,9},{9,10},{10,1... | collective-permute-start | bytes 294920 | tf_op jit(solution)/shard_map/ppermute | solution.py:296
  83.8 9.2 %collective-permute-start.14 = (bf16[16,3072]{1,0:T(8,128)(2,1)S(1)}, bf16[16,3072]{1,0:T(8,128)(2,1)S(1)}, u32[]{:S(2)}, u32[]{:S(2)}) collective-permute-start(bf16[16,3072]{1,0:T(8,128)(2,1)S(1)} %get-tuple-element.45), channel_id=1, source_target_pairs={{0,3},{1,0},{2,1},{3,2},{4,7},{5,4},{6,5},{7,6},{8,11},{9,8},{10,9... | collective-permute-start | bytes 294920 | tf_op jit(solution)/shard_map/ppermute | solution.py:296
  87.6 8.6 %collective-permute-start.13 = (bf16[16,3072]{1,0:T(8,128)(2,1)S(1)}, bf16[16,3072]{1,0:T(8,128)(2,1)S(1)}, u32[]{:S(2)}, u32[]{:S(2)}) collective-permute-start(bf16[16,3072]{1,0:T(8,128)(2,1)S(1)} %get-tuple-element.44), channel_id=1, source_target_pairs={{0,2},{1,3},{2,0},{3,1},{4,6},{5,7},{6,4},{7,5},{8,10},{9,11},{10,... | collective-permute-start | bytes 294920 | tf_op jit(solution)/shard_map/ppermute | solution.py:296
  87.9 8.3 %collective-permute-start.12 = (bf16[16,3072]{1,0:T(8,128)(2,1)S(1)}, bf16[16,3072]{1,0:T(8,128)(2,1)S(1)}, u32[]{:S(2)}, u32[]{:S(2)}) collective-permute-start(bf16[16,3072]{1,0:T(8,128)(2,1)S(1)} %get-tuple-element.43), channel_id=1, source_target_pairs={{0,1},{1,2},{2,3},{3,0},{4,5},{5,6},{6,7},{7,4},{8,9},{9,10},{10,1... | collective-permute-start | bytes 294920 | tf_op jit(solution)/shard_map/ppermute | solution.py:296

commit v3 on v2

--- a/solution.py
+++ b/solution.py
@@ -8,6 +8,7 @@
 from jax.sharding import PartitionSpec as P
 
 CORES = 2
+PIECES = 2
 MIB = 1024 * 1024
 NT = (((1,), (1,)), ((), ()))
 NN = (((1,), (0,)), ((), ()))
@@ -15,6 +16,7 @@
 VMEM = pl.BlockSpec(memory_space=pltpu.VMEM)
 SMEM = pl.BlockSpec(memory_space=pltpu.SMEM)
 HBM = pl.BlockSpec(memory_space=pltpu.HBM)
+ANY = pl.BlockSpec(memory_space=pl.ANY)
 
 
 def mm(a, b, dims):
@@ -28,17 +30,25 @@
     return size
 
 
-def call(kernel, in_specs, out_specs, out_shape, name, flops=0, size=0, scratch=(), limit=24):
-    return pl.pallas_call(
-        kernel,
-        in_specs=in_specs,
+def call(
+    kernel, in_specs, out_specs, out_shape, name, scratch=(), limit=24, after=(), cost=0
+):
+    reads = len(in_specs)
+
+    def run(*refs):
+        kernel(*refs[:reads], *refs[reads + len(after) :])
+
+    kernel_call = pl.pallas_call(
+        run,
+        in_specs=list(in_specs) + [ANY] * len(after),
         out_specs=out_specs,
         out_shape=out_shape,
         scratch_shapes=scratch,
         compiler_params=pltpu.CompilerParams(vmem_limit_bytes=limit * MIB),
-        cost_estimate=pl.CostEstimate(flops=flops, bytes_accessed=size, transcendentals=0),
+        cost_estimate=pl.CostEstimate(flops=0, bytes_accessed=cost * MIB, transcendentals=0),
         name=name,
     )
+    return lambda *args: kernel_call(*args, *after)
 
 
 def shape(dims, dtype=jnp.bfloat16):
@@ -65,7 +75,7 @@
         copy.wait()
 
 
-def load(place, w_first, w_second, blocks, size):
+def load(place, w_first, w_second, blocks, size, after):
     width = w_first.shape[0]
     pieces = 4
     return call(
@@ -77,10 +87,83 @@
             pltpu.VMEM((blocks, size, width), jnp.bfloat16),
         ],
         "load_weights",
-        size=8 * blocks * width * size,
         scratch=[pltpu.SemaphoreType.DMA((2 * blocks * pieces,))],
         limit=20,
+        after=after,
     )(place, w_first, w_second)
+
+
+def split_kernel(place, tokens, cots, cot, *rest):
+    *outs, sems = rest
+    count, width = len(outs), outs[0].shape[1]
+    copies = [pltpu.make_async_copy(cots, cot, sems.at[count])]
+    for k in reversed(range(count)):
+        at = lax.rem(place[0] + k, count) * width
+        source = tokens.at[:, pl.ds(pl.multiple_of(at, 128), width)]
+        copies.append(pltpu.make_async_copy(source, outs[k], sems.at[k]))
+    for copy in reversed(copies):
+        copy.start()
+    for copy in copies:
+        copy.wait()
+
+
+def split(row_place, tokens, cots, count):
+    rows, width = tokens.shape[0], tokens.shape[1] // count
+    return call(
+        split_kernel,
+        [SMEM, HBM, HBM],
+        [VMEM] * (1 + count),
+        [shape(cots.shape)] + [shape((rows, width))] * count,
+        "split_width",
+        scratch=[pltpu.SemaphoreType.DMA((1 + count,))],
+    )(row_place, tokens, cots)
+
+
+def stack_kernel(*refs):
+    *parts, cot, out, cot_out = refs
+    out[...] = jnp.concatenate([r[...].astype(jnp.float32) for r in parts]).astype(out.dtype)
+    cot_out[...] = cot[...]
+
+
+def stack(parts, cot):
+    rows, width = parts[0].shape
+    return call(
+        stack_kernel,
+        [VMEM] * (1 + len(parts)),
+        [VMEM] * 2,
+        [shape((rows * len(parts), width)), shape(cot.shape)],
+        "stack_rows",
+    )(*parts, cot)
+
+
+def tokens_kernel(row, places, *refs):
+    stacks, outs, held = refs[: -1 - PIECES], refs[-1 - PIECES : -1], refs[-1]
+    col, n = len(stacks), held.shape[1]
+    rows_out = outs[0].shape[0]
+    my_row, my_col = places[0], places[1]
+    for k, part in enumerate(stacks):
+        rows = part[...].astype(jnp.float32)
+        for r in range(row):
+            at = lax.rem(my_row + row - r, row) * col + lax.rem(my_col + col - k, col)
+            held[at] = rows[r * n : (r + 1) * n]
+    for at in range(0, row * col, 2):
+        pair = jnp.concatenate([held[at], held[at + 1]])
+        piece, start = divmod(at * n, rows_out)
+        outs[piece][start : start + 2 * n] = pair.astype(jnp.bfloat16)
+
+
+def tokens_in_order(places, stacks, row, after):
+    rows, width = stacks[0].shape
+    col = len(stacks)
+    return call(
+        functools.partial(tokens_kernel, row),
+        [SMEM] + [VMEM] * col,
+        [VMEM] * PIECES,
+        [shape((rows * col // PIECES, width))] * PIECES,
+        "order_tokens",
+        scratch=[pltpu.VMEM((row * col, rows // row, width), jnp.float32)],
+        after=after,
+    )(places, *stacks)
 
 
 def order_kernel(place, *refs):
@@ -93,7 +176,7 @@
         out[pl.ds(pl.multiple_of(at, 16), rows)] = part[...]
 
 
-def in_order(col_place, parts):
+def in_order(col_place, parts, after):
     rows, width = parts[0].shape
     return call(
         order_kernel,
@@ -101,14 +184,19 @@
         VMEM,
         shape((rows * len(parts), width)),
         "order_rows",
-        size=4 * rows * len(parts) * width,
+        after=after,
+        cost=0,
     )(col_place, *parts)
 
 
-def first_kernel(dims, own, other, w, total, sent, rows):
-    half = own.shape[0]
-    rows[:half] = own[...]
-    rows[half:] = other[...]
+def first_kernel(dims, pieces, *refs):
+    groups, w = refs[: 2 * pieces], refs[2 * pieces]
+    total, sent, own_out, rows = refs[2 * pieces + 1 :]
+    step = groups[0].shape[0]
+    for i, group in enumerate(groups):
+        rows[i * step : (i + 1) * step] = group[...]
+        if i < pieces:
+            own_out[i * step : (i + 1) * step] = group[...]
     blocks = w.shape[0]
     size = total.shape[1] // blocks
     tile = tile_of(size, 256)
@@ -121,20 +209,19 @@
             sent[:, cut] = part.astype(jnp.bfloat16)
 
 
-def first(own, other, w, size, dims, name):
-    half, width = own.shape
+def first(own, other, w, size, dims, name, after):
+    half, width = len(own) * own[0].shape[0], own[0].shape[1]
     n = 2 * half
     units = w.shape[0] * size
     return call(
-        functools.partial(first_kernel, dims),
+        functools.partial(first_kernel, dims, len(own)),
+        [VMEM] * (2 * len(own) + 1),
         [VMEM] * 3,
-        [VMEM] * 2,
-        [shape((n, units), jnp.float32), shape((n, units))],
+        [shape((n, units), jnp.float32), shape((n, units)), shape((half, width))],
         name,
-        flops=2 * n * width * units,
-        size=2 * width * units,
         scratch=[pltpu.VMEM((n, width), jnp.bfloat16)],
-    )(own, other, w)
+        after=after,
+    )(*own, *other, w)
 
 
 def gelu_parts(preact):
@@ -143,7 +230,7 @@
     return (preact * cdf, slopes)
 
 
-def second_product(dims, vals, w, keep, send):
+def second_product(dims, vals, w, keep, sends):
     half, width = keep.shape
     blocks = w.shape[0]
     size = vals.shape[1] // blocks
@@ -156,7 +243,9 @@
             term = mm(vals[:, b * size : (b + 1) * size], weight, dims)
             part = term if part is None else part + term
         keep[:, cut] = part[:half]
-        send[:, cut] = part[half:].astype(jnp.bfloat16)
+        for i, send in enumerate(sends):
+            rows = send.shape[0]
+            send[:, cut] = part[half + i * rows : half + (i + 1) * rows].astype(jnp.bfloat16)
 
 
 def row_sum(total, parts, cut):
@@ -168,7 +257,8 @@
 
 def forward_kernel(blocks, shares, *refs):
     total, parts, w = refs[0], refs[1 : 1 + shares], refs[1 + shares]
-    keep, send, slopes, *hidden, vals = refs[2 + shares :]
+    keep, *sends = refs[2 + shares : 3 + shares + PIECES]
+    slopes, *hidden, vals = refs[3 + shares + PIECES :]
     size = total.shape[1] // blocks
     for b in range(blocks):
         cut = slice(b * size, (b + 1) * size)
@@ -177,28 +267,29 @@
         vals[:, cut] = value
         hidden[b][...] = value
         slopes[:, cut] = slope
-    second_product(NN, vals, w, keep, send)
+    second_product(NN, vals, w, keep, sends)
 
 
 def backward_kernel(blocks, shares, *refs):
     total, parts, slopes, w = refs[0], refs[1 : 1 + shares], refs[1 + shares], refs[2 + shares]
-    keep, send, *pre, vals = refs[3 + shares :]
+    keep, *sends = refs[3 + shares : 4 + shares + PIECES]
+    *pre, vals = refs[4 + shares + PIECES :]
     size = total.shape[1] // blocks
     for b in range(blocks):
         cut = slice(b * size, (b + 1) * size)
         value = (row_sum(total, parts, cut) * slopes[:, cut]).astype(jnp.bfloat16)
         vals[:, cut] = value
         pre[b][...] = value
-    second_product(NT, vals, w, keep, send)
-
-
-def second(total, parts, slopes, w, size, name):
+    second_product(NT, vals, w, keep, sends)
+
+
+def second(total, parts, slopes, w, size, name, after=()):
     n, units = total.shape
     half = n // 2
     blocks = w.shape[0]
     forward = slopes is None
     width = w.shape[2] if forward else w.shape[1]
-    out_shape = [shape((half, width), jnp.float32), shape((half, width))]
+    out_shape = [shape((half, width), jnp.float32)] + [shape((half // PIECES, width))] * PIECES
     if forward:
         out_shape.append(shape((n, units), jnp.float32))
     out_shape += [shape((n, size))] * blocks
@@ -209,35 +300,50 @@
         [VMEM] * len(out_shape),
         out_shape,
         name,
-        flops=2 * n * width * units,
-        size=2 * width * units,
         scratch=[pltpu.VMEM((n, units), jnp.bfloat16)],
+        after=after,
+        cost=0,
     )(total, *parts, *extra, w)
 
 
-def cores_kernel(place, keep, part, own, *sent):
+def cores_kernel(place, keep, *refs):
+    parts, own = refs[:PIECES], refs[PIECES]
+    *sent, held = refs[PIECES + 1 :]
+    rows = own.shape[0]
+    at = 0
+    for part in parts:
+        cut = slice(at, at + part.shape[0])
+        held[cut] = keep[cut] + part[...].astype(jnp.float32)
+        at += part.shape[0]
     count = 1 + len(sent)
-    rows = own.shape[0]
     me = place[0]
     for k in range(count):
         at = pl.ds(pl.multiple_of(lax.rem(me + k, count) * rows, 16), rows)
-        whole = keep[at] + part[at].astype(jnp.float32)
         if k == 0:
-            own[...] = whole
+            own[...] = held[at]
         else:
-            sent[k - 1][...] = whole.astype(jnp.bfloat16)
-
-
-def cores_sum(col_place, keep, part, count, name):
+            sent[k - 1][...] = held[at].astype(jnp.bfloat16)
+
+
+def cores_sum(col_place, keep, parts, count, name, after=()):
     rows, width = keep.shape[0] // count, keep.shape[1]
     return call(
         cores_kernel,
-        [SMEM, VMEM, VMEM],
+        [SMEM, VMEM] + [VMEM] * PIECES,
         [VMEM] * count,
         [shape((rows, width), jnp.float32)] + [shape((rows, width))] * (count - 1),
         name,
-        size=8 * count * rows * width,
-    )(col_place, keep, part)
+        scratch=[pltpu.VMEM(keep.shape, jnp.float32)],
+        after=after,
+    )(col_place, keep, *parts)
+
+
+def mark_kernel(*refs):
+    refs[-1][...] = refs[0][:16, :128]
+
+
+def mark(parts):
+    return call(mark_kernel, [VMEM] * len(parts), VMEM, shape((16, 128)), "mark")(*parts)
 
 
 def weight_kernel(lefts, tile, across, *refs):
@@ -262,7 +368,7 @@
         copy.wait()
 
 
-def weight_grad(left, right, across, name):
+def weight_grad(left, right, across, name, after):
     n = sum(group.shape[0] for group in left)
     k, m = left[0].shape[1], right[0].shape[1]
     long = m if across else k
@@ -273,14 +379,14 @@
         HBM,
         shape((k, m)),
         name,
-        flops=2 * n * k * m,
-        size=2 * k * m,
         scratch=[
             pltpu.VMEM((n, k), jnp.bfloat16),
             pltpu.VMEM((n, m), jnp.bfloat16),
             pltpu.VMEM((k, m), jnp.bfloat16),
             pltpu.SemaphoreType.DMA((long // tile,)),
         ],
+        after=after,
+        cost=0,
     )(*left, *right)
 
 
@@ -289,6 +395,7 @@
     width, size = w_in.shape[0], w_in.shape[2] // dp
     mine = lax.axis_index("dp")
     place = jnp.stack([(mine + CORES * b) % dp for b in range(blocks)]).astype(jnp.int32)
+    row_place = lax.axis_index("row").astype(jnp.int32)[None]
     col_place = lax.axis_index("col").astype(jnp.int32)[None]
 
     def shifted(x, axis, step):
@@ -301,50 +408,74 @@
     def across_rows(x):
         return [shifted(x, "row", step) for step in range(1, row)]
 
-    n = tokens.shape[0]
-    spread = tokens.reshape(n, row, width).swapaxes(0, 1)
-    spread = jnp.broadcast_to(spread[:, None], (row, col, n, width)).reshape(row * col, n, width)
-    tok = lax.all_to_all(spread, ("row", "col"), 0, 0, tiled=True).reshape(row * col * n, width)
-    cots = [grad_out] + [shifted(grad_out, "col", step) for step in range(1, col)]
-    w_first, w_second = load(place, w_in[:, 0, :], w_out[0], blocks, size)
-    cot = in_order(col_place, cots)
-
-    tok_other = across_cores(tok)
-    pre_total, pre_sent = first(tok, tok_other, w_first, size, NN, "preact_partial")
+    def all_replicas(own, other, there):
+        groups = [own, *other]
+        for part in there:
+            groups += [part, across_cores(part)]
+        return groups
+
+    cot_mine, own, *other_widths = split(row_place, tokens, grad_out, row)
+    stacked, cot_mine = stack(
+        [own] + [shifted(part, "row", step + 1) for step, part in enumerate(other_widths)],
+        cot_mine,
+    )
+    stacks = [stacked] + [shifted(stacked, "col", step) for step in range(1, col)]
+    cots = [cot_mine] + [shifted(cot_mine, "col", step) for step in range(1, col)]
+    w_first, w_second = load(place, w_in[:, 0, :], w_out[0], blocks, size, [stacked])
+    places = jnp.concatenate([row_place, col_place])
+    tok = tokens_in_order(places, stacks, row, [w_first])
+
+    tok_other = [across_cores(x) for x in tok]
+    cot = in_order(col_place, cots, [tok[0]])
+    cot_other = across_cores(cot)
+    cot_arrived = across_cores(mark([cot_other]))
+    pre_total, pre_sent, tok_later = first(
+        tok, tok_other, w_first, size, NN, "preact_partial", []
+    )
     pre_parts = across_rows(pre_sent)
-    cot_other = across_cores(cot)
-    back_total, back_sent = first(cot, cot_other, w_second, size, NT, "back_partial")
+    back_total, back_sent, cot_later = first(
+        [cot], [cot_other], w_second, size, NT, "back_partial", [pre_sent, cot_arrived]
+    )
     back_parts = across_rows(back_sent)
-
-    def col_total(keep, send, name):
-        own, *sent = cores_sum(col_place, keep, across_cores(send), col, name)
+    tok_there = [shifted(tok_later, "dp", CORES * b) for b in range(1, blocks)]
+    cot_there = [shifted(cot_later, "dp", CORES * b) for b in range(1, blocks)]
+
+    def col_total(own, sent):
         for step, part in enumerate(sent):
             own = own + shifted(part, "col", step + 1).astype(jnp.float32)
         return own.astype(jnp.bfloat16)
 
-    keep, send, slopes, *hidden = second(
-        pre_total, pre_parts, None, w_second, size, "block_out_partial"
-    )
-    block_out = col_total(keep, send, "block_out_cores")
-    keep, send, *grad_pre = second(
-        back_total, back_parts, slopes, w_first, size, "grad_in_partial"
-    )
-    grad_in = col_total(keep, send, "grad_in_cores")
-
-    def all_replicas(own, other):
-        groups = [own, other]
-        for b in range(1, blocks):
-            there = shifted(own, "dp", CORES * b)
-            groups += [there, across_cores(there)]
-        return groups
+    out_keep, *rest = second(
+        pre_total, pre_parts, None, w_second, size, "block_out_partial", [back_sent]
+    )
+    out_sends, (slopes, *hidden) = rest[:PIECES], rest[PIECES:]
+    out_own, *out_sent = cores_sum(
+        col_place, out_keep, [across_cores(x) for x in out_sends], col, "block_out_cores"
+    )
+    block_out = col_total(out_own, out_sent)
+    tok_all = all_replicas(tok_later, tok_other, tok_there)
+    cot_all = all_replicas(cot_later, [cot_other], cot_there)
+    arrived = across_cores(mark(back_parts))
+    in_keep, *rest = second(
+        back_total, back_parts, slopes, w_first, size, "grad_in_partial", [out_own, tok_all[-1], arrived]
+    )
+    in_sends, grad_pre = rest[:PIECES], rest[PIECES:]
+    in_own, *in_sent = cores_sum(
+        col_place,
+        in_keep,
+        [across_cores(x) for x in in_sends],
+        col,
+        "grad_in_cores",
+        [block_out, cot_all[-1]],
+    )
+    grad_in = col_total(in_own, in_sent)
 
     def to_owner(parts):
         return [parts[0]] + [shifted(parts[b], "dp", CORES * b) for b in range(1, blocks)]
 
-    cot_all = all_replicas(cot, cot_other)
-    tok_all = all_replicas(tok, tok_other)
-    grad_out_w = weight_grad(to_owner(hidden), cot_all, True, "grad_w_out")
-    grad_in_w = weight_grad(tok_all, to_owner(grad_pre), False, "grad_w_in")
+    after = [in_own, block_out]
+    grad_out_w = weight_grad(to_owner(hidden), cot_all, True, "grad_w_out", after)
+    grad_in_w = weight_grad(tok_all, to_owner(grad_pre), False, "grad_w_in", after)
     return block_out, grad_in, grad_in_w[:, None, :], grad_out_w[None]
 
 

time: 97.1 us -> 72.5 us (0.75)
  blocking collectives: 19.6 us -> 0 us
  waiting for transfers between devices: 32.2 us -> 14 us
  starting transfers between devices: 18.9 us -> 31.7 us
  Pallas kernels: 22.1 us -> 23.1 us
    ppermute x15 -> x19, waiting for transfers between devices: 32.2 us -> 9.8 us  [shifted(): lax.ppermute(x, axis, [(i, (i + step) % count) for i in range(count)])]
    all_to_all x1 -> x0, blocking collectives: 19.6 us -> none  [body(): lax.all_to_all(spread, ('row', 'col'), 0, 0, tiled=True)]
    ppermute x15 -> x19, starting transfers between devices: 18.2 us -> 29.8 us  [shifted(): lax.ppermute(x, axis, [(i, (i + step) % count) for i in range(count)])]
    ppermute x6 -> x11, waiting for transfers between devices: 0.02 us -> 4.21 us  [across_cores(): return lax.ppermute(x, 'dp', [(i, i ^ 1) for i in range(dp)])]
    ppermute x6 -> x11, starting transfers between devices: 0.66 us -> 1.87 us  [across_cores(): return lax.ppermute(x, 'dp', [(i, i ^ 1) for i in range(dp)])]
    pallas_call x10 -> x15, Pallas kernels: 22.1 us -> 23.1 us  [call(): return lambda *args: kernel_call(*args, *after)]
  transfers between devices with their start and end apart: 21 -> 30, of which waited for: 7 -> 12; matrix products, arithmetic and copies ran while one was open for 1% -> 0% of each run, Pallas kernels for 23% -> 32%
where the time goes in v3:
time: 72.5 us; the launch traced here: 72.4 us
  starting transfers between devices  31.7 us (44%)
  Pallas kernels  23.1 us (32%)
  waiting for transfers between devices  14 us (19%)
  local copies, waits for them, and re-layouts  1.78 us (2%)
  other arithmetic  0.89 us (1%)
  between operations  0.87 us (1%)
    ppermute x19, starting transfers between devices, shifted(): lax.ppermute(x, axis, [(i, (i + step) % count) for i in range(count)])  29.8 us
    pallas_call x15, Pallas kernels, call(): return lambda *args: kernel_call(*args, *after)  23.1 us
    ppermute x19, waiting for transfers between devices, shifted(): lax.ppermute(x, axis, [(i, (i + step) % count) for i in range(count)])  9.8 us
    ppermute x11, waiting for transfers between devices, across_cores(): return lax.ppermute(x, 'dp', [(i, i ^ 1) for i in range(dp)])  4.21 us
    ppermute x11, starting transfers between devices, across_cores(): return lax.ppermute(x, 'dp', [(i, i ^ 1) for i in range(dp)])  1.87 us
    unnamed x6, local copies, waits for them, and re-layouts  1.78 us
  transfers between devices with their start and end apart: 30, of which 12 were waited for; matrix products, arithmetic and copies ran while one was open for 0% of the time, Pallas kernels for 32%

profile of v3, /device:TPU:0, one launch (start us, length us, event | category | flops | bytes accessed | tf_op | source)
XLA Modules:
  0.0 72.4 jit_solution(15555228032125640398)
XLA Ops:
  0.6 0.9 %copy-done.1 = bf16[8,6144]{1,0:T(8,128)(2,1)S(1)} copy-done((bf16[8,6144]{1,0:T(8,128)(2,1)S(1)}, bf16[8,6144]{1,0:T(8,128)(2,1)}, u32[]{:S(2)}) %copy-start.1) | copy-done | bytes 98328
  1.5 0.9 %copy-done.2 = bf16[16,3072]{1,0:T(8,128)(2,1)S(1)} copy-done((bf16[16,3072]{1,0:T(8,128)(2,1)S(1)}, bf16[16,3072]{1,0:T(8,128)(2,1)}, u32[]{:S(2)}) %copy-start.2) | copy-done | bytes 98328
  2.7 3.0 %collective-permute-start = (bf16[8,3072]{1,0:T(8,128)(2,1)S(1)}, bf16[8,3072]{1,0:T(8,128)(2,1)S(1)}, u32[]{:S(2)}, u32[]{:S(2)}) collective-permute-start(bf16[8,3072]{1,0:T(8,128)(2,1)S(1)} %get-tuple-element.39), channel_id=1, source_target_pairs={{0,4},{4,0},{1,5},{5,1},{2,6},{6,2},{3,7},{7,3},{8,12},{12,8},{9,1... | collective-permute-start | bytes 147464 | tf_op jit(solution)/shard_map/ppermute | solution.py:403
  5.7 2.1 %collective-permute-done.refs_1_ = bf16[8,3072]{1,0:T(8,128)(2,1)S(1)} collective-permute-done((bf16[8,3072]{1,0:T(8,128)(2,1)S(1)}, bf16[8,3072]{1,0:T(8,128)(2,1)S(1)}, u32[]{:S(2)}, u32[]{:S(2)}) %collective-permute-start) | collective-permute-done | bytes 49184 | tf_op jit(solution)/shard_map/ppermute | solution.py:403
  7.8 2.2 %collective-permute-start.1 = (bf16[16,3072]{1,0:T(8,128)(2,1)S(1)}, bf16[16,3072]{1,0:T(8,128)(2,1)S(1)}, u32[]{:S(2)}, u32[]{:S(2)}) collective-permute-start(bf16[16,3072]{1,0:T(8,128)(2,1)S(1)} %get-tuple-element.41.refs_3_.refs_1_), channel_id=1, source_target_pairs={{0,1},{1,2},{2,3},{3,0},{4,5},{5,6},{6,7},{7,4},{8,9},{9,10},{10,1... | collective-permute-start | bytes 294920 | tf_op jit(solution)/shard_map/ppermute | solution.py:403
  10.0 2.6 %collective-permute-start.2 = (bf16[16,3072]{1,0:T(8,128)(2,1)S(1)}, bf16[16,3072]{1,0:T(8,128)(2,1)S(1)}, u32[]{:S(2)}, u32[]{:S(2)}) collective-permute-start(bf16[16,3072]{1,0:T(8,128)(2,1)S(1)} %get-tuple-element.41.refs_3_.refs_1_), channel_id=1, source_target_pairs={{0,2},{1,3},{2,0},{3,1},{4,6},{5,7},{6,4},{7,5},{8,10},{9,11},{10,... | collective-permute-start | bytes 294920 | tf_op jit(solution)/shard_map/ppermute | solution.py:403
  12.6 1.3 %collective-permute-start.3 = (bf16[16,3072]{1,0:T(8,128)(2,1)S(1)}, bf16[16,3072]{1,0:T(8,128)(2,1)S(1)}, u32[]{:S(2)}, u32[]{:S(2)}) collective-permute-start(bf16[16,3072]{1,0:T(8,128)(2,1)S(1)} %get-tuple-element.41.refs_3_.refs_1_), channel_id=1, source_target_pairs={{0,3},{1,0},{2,1},{3,2},{4,7},{5,4},{6,5},{7,6},{8,11},{9,8},{10,9... | collective-permute-start | bytes 294920 | tf_op jit(solution)/shard_map/ppermute | solution.py:403
  13.9 0.7 collective-permute-start.7
  15.0 0.6 collective-permute-done.1.refs_2_
  15.6 2.2 %collective-permute-start.9 = (bf16[16,3072]{1,0:T(8,128)(2,1)S(1)}, bf16[16,3072]{1,0:T(8,128)(2,1)S(1)}, u32[]{:S(2)}, u32[]{:S(2)}) collective-permute-start(bf16[16,3072]{1,0:T(8,128)(2,1)S(1)} %get-tuple-element.48.refs_1_), channel_id=1, source_target_pairs={{0,3},{1,0},{2,1},{3,2},{4,7},{5,4},{6,5},{7,6},{8,11},{9,8},{10,9... | collective-permute-start | bytes 294920 | tf_op jit(solution)/shard_map/ppermute | solution.py:403
  17.9 7.1 %load_weights.1 = (bf16[2,3072,768]{2,1,0:T(8,128)(2,1)S(1)}, bf16[2,768,3072]{2,1,0:T(8,128)(2,1)S(1)}) custom-call(s32[2]{0:T(128)S(1)} %pad_add_fusion.1.refs_0_, bf16[3072,3072]{1,0:T(8,128)(2,1)} %bitcast.8, bf16[3072,3072]{1,0:T(8,128)(2,1)} %bitcast.9, bf16[16,3072]{1,0:T(8,128)(2,1)S(1)} %get-tuple-element.41.refs_3_.refs_1_), custom_call_target="tpu_custom_call" | custom-call | tf_op jit(solution)/shard_map/load_weights/pallas_call | solution.py:51
  27.5 1.4 %preact_partial.1 = (f32[128,1536]{1,0:T(8,128)S(1)}, bf16[128,1536]{1,0:T(8,128)(2,1)S(1)}, bf16[64,3072]{1,0:T(8,128)(2,1)S(1)}) custom-call(bf16[32,3072]{1,0:T(8,128)(2,1)S(1)} %get-tuple-element.43.refs_0_.refs_5_, bf16[32,3072]{1,0:T(8,128)(2,1)S(1)} %get-tuple-element.44.refs_1_, bf16[32,3072]{1,0:T(8,128)(2,1)S(1)} %collective-permute-done.4.refs_2_.refs_1_, ...), custom_call_target="tpu_custom_call" | custom-call | tf_op jit(solution)/shard_map/preact_partial/pallas_call | solution.py:51
  28.9 1.6 %collective-permute-start.18 = (bf16[64,3072]{1,0:T(8,128)(2,1)S(1)}, bf16[64,3072]{1,0:T(8,128)(2,1)S(1)}, u32[]{:S(2)}, u32[]{:S(2)}) collective-permute-start(bf16[64,3072]{1,0:T(8,128)(2,1)S(1)} %get-tuple-element.59.refs_0_), channel_id=1, source_target_pairs={{0,16},{8,24},{16,0},{24,8},{1,17},{9,25},{17,1},{25,9},{2,18},{10... | collective-permute-start | bytes 1179656 | tf_op jit(solution)/shard_map/ppermute | solution.py:403
  30.5 1.5 %collective-permute-start.6 = (bf16[128,1536]{1,0:T(8,128)(2,1)S(1)}, bf16[128,1536]{1,0:T(8,128)(2,1)S(1)}, u32[]{:S(2)}, u32[]{:S(2)}) collective-permute-start(bf16[128,1536]{1,0:T(8,128)(2,1)S(1)} %get-tuple-element.46.refs_3_), channel_id=1, source_target_pairs={{0,4},{4,0},{1,5},{5,1},{2,6},{6,2},{3,7},{7,3},{8,12},{12,8},{9,1... | collective-permute-start | bytes 1179656 | tf_op jit(solution)/shard_map/ppermute | solution.py:403
  32.0 1.2 %collective-permute-done.11.refs_4_ = bf16[16,128]{1,0:T(8,128)(2,1)S(1)} collective-permute-done((bf16[16,128]{1,0:T(8,128)(2,1)S(1)}, bf16[16,128]{1,0:T(8,128)(2,1)S(1)}, u32[]{:S(2)}, u32[]{:S(2)}) %collective-permute-start.11) | collective-permute-done | bytes 4128 | tf_op jit(solution)/shard_map/ppermute | solution.py:406
  33.1 3.2 %back_partial.1 = (f32[128,1536]{1,0:T(8,128)S(1)}, bf16[128,1536]{1,0:T(8,128)(2,1)S(1)}, bf16[64,3072]{1,0:T(8,128)(2,1)S(1)}) custom-call(bf16[64,3072]{1,0:T(8,128)(2,1)S(1)} %order_rows.1.refs_0_, bf16[64,3072]{1,0:T(8,128)(2,1)S(1)} %collective-permute-done.10.refs_0_.refs_1_.refs_3_, bf16[2,768,3072]{2,1,0:T(8,128)(2,1)S(1)} %get-tuple-element.47.refs_2_, ...), custom_call_target="tpu_custom_call" | custom-call | tf_op jit(solution)/shard_map/back_partial/pallas_call | solution.py:51
  37.4 3.5 %collective-permute-done.18.refs_3_ = bf16[64,3072]{1,0:T(8,128)(2,1)S(1)} collective-permute-done((bf16[64,3072]{1,0:T(8,128)(2,1)S(1)}, bf16[64,3072]{1,0:T(8,128)(2,1)S(1)}, u32[]{:S(2)}, u32[]{:S(2)}) %collective-permute-start.18) | collective-permute-done | bytes 393248 | tf_op jit(solution)/shard_map/ppermute | solution.py:403
  40.9 1.6 %collective-permute-done.6.refs_1_ = bf16[128,1536]{1,0:T(8,128)(2,1)S(1)} collective-permute-done((bf16[128,1536]{1,0:T(8,128)(2,1)S(1)}, bf16[128,1536]{1,0:T(8,128)(2,1)S(1)}, u32[]{:S(2)}, u32[]{:S(2)}) %collective-permute-start.6) | collective-permute-done | bytes 393248 | tf_op jit(solution)/shard_map/ppermute | solution.py:403
  42.4 1.7 %block_out_partial.1 = (f32[64,3072]{1,0:T(8,128)S(1)}, bf16[32,3072]{1,0:T(8,128)(2,1)S(1)}, bf16[32,3072]{1,0:T(8,128)(2,1)S(1)}, f32[128,1536]{1,0:T(8,128)S(...) custom-call(f32[128,1536]{1,0:T(8,128)S(1)} %get-tuple-element.45.refs_0_, ...), custom_call_target="tpu_custom_call" | custom-call | tf_op jit(solution)/shard_map/block_out_partial/pallas_call | solution.py:51
  44.7 0.9 %collective-permute-done.12.refs_2_ = bf16[32,3072]{1,0:T(8,128)(2,1)S(1)} collective-permute-done((bf16[32,3072]{1,0:T(8,128)(2,1)S(1)}, bf16[32,3072]{1,0:T(8,128)(2,1)S(1)}, u32[]{:S(2)}, u32[]{:S(2)}) %collective-permute-start.12) | collective-permute-done | bytes 196640 | tf_op jit(solution)/shard_map/ppermute | solution.py:406
  46.0 1.6 %collective-permute-start.14 = (bf16[16,3072]{1,0:T(8,128)(2,1)S(1)}, bf16[16,3072]{1,0:T(8,128)(2,1)S(1)}, u32[]{:S(2)}, u32[]{:S(2)}) collective-permute-start(bf16[16,3072]{1,0:T(8,128)(2,1)S(1)} %get-tuple-element.54), channel_id=1, source_target_pairs={{0,1},{1,2},{2,3},{3,0},{4,5},{5,6},{6,7},{7,4},{8,9},{9,10},{10,1... | collective-permute-start | bytes 294920 | tf_op jit(solution)/shard_map/ppermute | solution.py:403
  47.7 2.6 %collective-permute-start.15 = (bf16[16,3072]{1,0:T(8,128)(2,1)S(1)}, bf16[16,3072]{1,0:T(8,128)(2,1)S(1)}, u32[]{:S(2)}, u32[]{:S(2)}) collective-permute-start(bf16[16,3072]{1,0:T(8,128)(2,1)S(1)} %get-tuple-element.55), channel_id=1, source_target_pairs={{0,2},{1,3},{2,0},{3,1},{4,6},{5,7},{6,4},{7,5},{8,10},{9,11},{10,... | collective-permute-start | bytes 294920 | tf_op jit(solution)/shard_map/ppermute | solution.py:403
  50.3 3.2 %collective-permute-start.16 = (bf16[16,3072]{1,0:T(8,128)(2,1)S(1)}, bf16[16,3072]{1,0:T(8,128)(2,1)S(1)}, u32[]{:S(2)}, u32[]{:S(2)}) collective-permute-start(bf16[16,3072]{1,0:T(8,128)(2,1)S(1)} %get-tuple-element.56), channel_id=1, source_target_pairs={{0,3},{1,0},{2,1},{3,2},{4,7},{5,4},{6,5},{7,6},{8,11},{9,8},{10,9... | collective-permute-start | bytes 294920 | tf_op jit(solution)/shard_map/ppermute | solution.py:403
  53.5 1.2 %collective-permute-done.20.refs_6_ = bf16[16,128]{1,0:T(8,128)(2,1)S(1)} collective-permute-done((bf16[16,128]{1,0:T(8,128)(2,1)S(1)}, bf16[16,128]{1,0:T(8,128)(2,1)S(1)}, u32[]{:S(2)}, u32[]{:S(2)}) %collective-permute-start.20) | collective-permute-done | bytes 4128 | tf_op jit(solution)/shard_map/ppermute | solution.py:406
  55.2 3.1 %grad_in_partial.1 = (f32[64,3072]{1,0:T(8,128)S(1)}, bf16[32,3072]{1,0:T(8,128)(2,1)S(1)}, bf16[32,3072]{1,0:T(8,128)(2,1)S(1)}, bf16[128,768]{1,0:T(8,128)(2,1)S(1)}, bf16[128,768]{1,0:T(8,128)(2,1)S(1)}) custom-call(f32[128,1536]{1,0:T(8,128)S(1)} %get-tuple-element.57.refs_0_, bf16[128,1536]{1,0:T(8,128)(2,1)S(1)} %collective-permute-done.17.refs_0_.refs_1_, ...), custom_call_target="tpu_custom_call" | custom-call | tf_op jit(solution)/shard_map/grad_in_partial/pallas_call | solution.py:51
  59.0 1.5 %collective-permute-start.28 = (bf16[128,768]{1,0:T(8,128)(2,1)S(1)}, bf16[128,768]{1,0:T(8,128)(2,1)S(1)}, u32[]{:S(2)}, u32[]{:S(2)}) collective-permute-start(bf16[128,768]{1,0:T(8,128)(2,1)S(1)} %get-tuple-element.69), channel_id=1, source_target_pairs={{0,16},{8,24},{16,0},{24,8},{1,17},{9,25},{17,1},{25,9},{2,18},{10... | collective-permute-start | bytes 589832 | tf_op jit(solution)/shard_map/ppermute | solution.py:403
  60.8 1.8 %collective-permute-start.26 = (bf16[16,3072]{1,0:T(8,128)(2,1)S(1)}, bf16[16,3072]{1,0:T(8,128)(2,1)S(1)}, u32[]{:S(2)}, u32[]{:S(2)}) collective-permute-start(bf16[16,3072]{1,0:T(8,128)(2,1)S(1)} %get-tuple-element.66), channel_id=1, source_target_pairs={{0,2},{1,3},{2,0},{3,1},{4,6},{5,7},{6,4},{7,5},{8,10},{9,11},{10,... | collective-permute-start | bytes 294920 | tf_op jit(solution)/shard_map/ppermute | solution.py:403
  62.6 2.0 %collective-permute-start.27 = (bf16[16,3072]{1,0:T(8,128)(2,1)S(1)}, bf16[16,3072]{1,0:T(8,128)(2,1)S(1)}, u32[]{:S(2)}, u32[]{:S(2)}) collective-permute-start(bf16[16,3072]{1,0:T(8,128)(2,1)S(1)} %get-tuple-element.67), channel_id=1, source_target_pairs={{0,3},{1,0},{2,1},{3,2},{4,7},{5,4},{6,5},{7,6},{8,11},{9,8},{10,9... | collective-permute-start | bytes 294920 | tf_op jit(solution)/shard_map/ppermute | solution.py:403
  64.7 2.6 %grad_w_out.1 = bf16[768,3072]{1,0:T(8,128)(2,1)} custom-call(bf16[128,768]{1,0:T(8,128)(2,1)S(1)} %get-tuple-element.70.refs_0_, bf16[128,768]{1,0:T(8,128)(2,1)S(1)} %collective-permute-done.29.refs_1_, bf16[64,3072]{1,0:T(8,128)(2,1)S(1)} %get-tuple-element.63.refs_2_, bf16[64,3072]{1,0:T(8,128)(2,1)S(1)} %collective-permute-done.10.refs_0_.refs_1_.refs_3_, ...), custom_call_target="tpu_custom_call" | custom-call | tf_op jit(solution)/shard_map/grad_w_out/pallas_call | solution.py:51
  67.3 2.7 %grad_w_in.1 = bf16[3072,768]{1,0:T(8,128)(2,1)} custom-call(bf16[64,3072]{1,0:T(8,128)(2,1)S(1)} %get-tuple-element.59.refs_0_, bf16[32,3072]{1,0:T(8,128)(2,1)S(1)} %collective-permute-done.4.refs_2_.refs_1_, bf16[32,3072]{1,0:T(8,128)(2,1)S(1)} %collective-permute-done.5.refs_3_.refs_2_, bf16[64,3072]{1,0:T(8,128)(2,1)S(1)} %collective-permute-done.18.refs_3_, ...), custom_call_target="tpu_custom_call" | custom-call | tf_op jit(solution)/shard_map/grad_w_in/pallas_call | solution.py:51
  70.0 1.6 %collective-permute-done.26 = bf16[16,3072]{1,0:T(8,128)(2,1)S(1)} collective-permute-done((bf16[16,3072]{1,0:T(8,128)(2,1)S(1)}, bf16[16,3072]{1,0:T(8,128)(2,1)S(1)}, u32[]{:S(2)}, u32[]{:S(2)}) %collective-permute-start.26) | collective-permute-done | bytes 98336 | tf_op jit(solution)/shard_map/ppermute | solution.py:403
  71.7 0.7 add_convert_fusion
  (53 shorter events, 6.7 us)
Async XLA Ops:
  0.6 0.9 %copy-start.1 = (bf16[8,6144]{1,0:T(8,128)(2,1)S(1)}, bf16[8,6144]{1,0:T(8,128)(2,1)}, u32[]{:S(2)}) copy-start(bf16[8,6144]{1,0:T(8,128)(2,1)} %refs_1_.1) | copy-start | bytes 294916
  2.7 5.1 %collective-permute-start = (bf16[8,3072]{1,0:T(8,128)(2,1)S(1)}, bf16[8,3072]{1,0:T(8,128)(2,1)S(1)}, u32[]{:S(2)}, u32[]{:S(2)}) collective-permute-start(bf16[8,3072]{1,0:T(8,128)(2,1)S(1)} %get-tuple-element.39), channel_id=1, source_target_pairs={{0,4},{4,0},{1,5},{5,1},{2,6},{6,2},{3,7},{7,3},{8,12},{12,8},{9,1... | collective-permute-start | bytes 147464 | tf_op jit(solution)/shard_map/ppermute | solution.py:403
  7.8 7.8 %collective-permute-start.1 = (bf16[16,3072]{1,0:T(8,128)(2,1)S(1)}, bf16[16,3072]{1,0:T(8,128)(2,1)S(1)}, u32[]{:S(2)}, u32[]{:S(2)}) collective-permute-start(bf16[16,3072]{1,0:T(8,128)(2,1)S(1)} %get-tuple-element.41.refs_3_.refs_1_), channel_id=1, source_target_pairs={{0,1},{1,2},{2,3},{3,0},{4,5},{5,6},{6,7},{7,4},{8,9},{9,10},{10,1... | collective-permute-start | bytes 294920 | tf_op jit(solution)/shard_map/ppermute | solution.py:403
  10.0 15.0 %collective-permute-start.2 = (bf16[16,3072]{1,0:T(8,128)(2,1)S(1)}, bf16[16,3072]{1,0:T(8,128)(2,1)S(1)}, u32[]{:S(2)}, u32[]{:S(2)}) collective-permute-start(bf16[16,3072]{1,0:T(8,128)(2,1)S(1)} %get-tuple-element.41.refs_3_.refs_1_), channel_id=1, source_target_pairs={{0,2},{1,3},{2,0},{3,1},{4,6},{5,7},{6,4},{7,5},{8,10},{9,11},{10,... | collective-permute-start | bytes 294920 | tf_op jit(solution)/shard_map/ppermute | solution.py:403
  12.6 12.4 %collective-permute-start.3 = (bf16[16,3072]{1,0:T(8,128)(2,1)S(1)}, bf16[16,3072]{1,0:T(8,128)(2,1)S(1)}, u32[]{:S(2)}, u32[]{:S(2)}) collective-permute-start(bf16[16,3072]{1,0:T(8,128)(2,1)S(1)} %get-tuple-element.41.refs_3_.refs_1_), channel_id=1, source_target_pairs={{0,3},{1,0},{2,1},{3,2},{4,7},{5,4},{6,5},{7,6},{8,11},{9,8},{10,9... | collective-permute-start | bytes 294920 | tf_op jit(solution)/shard_map/ppermute | solution.py:403
  13.9 12.3 %collective-permute-start.7 = (bf16[16,3072]{1,0:T(8,128)(2,1)S(1)}, bf16[16,3072]{1,0:T(8,128)(2,1)S(1)}, u32[]{:S(2)}, u32[]{:S(2)}) collective-permute-start(bf16[16,3072]{1,0:T(8,128)(2,1)S(1)} %get-tuple-element.48.refs_1_), channel_id=1, source_target_pairs={{0,1},{1,2},{2,3},{3,0},{4,5},{5,6},{6,7},{7,4},{8,9},{9,10},{10,1... | collective-permute-start | bytes 294920 | tf_op jit(solution)/shard_map/ppermute | solution.py:403
  14.6 12.1 %collective-permute-start.8 = (bf16[16,3072]{1,0:T(8,128)(2,1)S(1)}, bf16[16,3072]{1,0:T(8,128)(2,1)S(1)}, u32[]{:S(2)}, u32[]{:S(2)}) collective-permute-start(bf16[16,3072]{1,0:T(8,128)(2,1)S(1)} %get-tuple-element.48.refs_1_), channel_id=1, source_target_pairs={{0,2},{1,3},{2,0},{3,1},{4,6},{5,7},{6,4},{7,5},{8,10},{9,11},{10,... | collective-permute-start | bytes 294920 | tf_op jit(solution)/shard_map/ppermute | solution.py:403
  15.6 11.1 %collective-permute-start.9 = (bf16[16,3072]{1,0:T(8,128)(2,1)S(1)}, bf16[16,3072]{1,0:T(8,128)(2,1)S(1)}, u32[]{:S(2)}, u32[]{:S(2)}) collective-permute-start(bf16[16,3072]{1,0:T(8,128)(2,1)S(1)} %get-tuple-element.48.refs_1_), channel_id=1, source_target_pairs={{0,3},{1,0},{2,1},{3,2},{4,7},{5,4},{6,5},{7,6},{8,11},{9,8},{10,9... | collective-permute-start | bytes 294920 | tf_op jit(solution)/shard_map/ppermute | solution.py:403
  25.7 1.5 %collective-permute-start.4 = (bf16[32,3072]{1,0:T(8,128)(2,1)S(1)}, bf16[32,3072]{1,0:T(8,128)(2,1)S(1)}, u32[]{:S(2)}, u32[]{:S(2)}) collective-permute-start(bf16[32,3072]{1,0:T(8,128)(2,1)S(1)} %get-tuple-element.43.refs_0_.refs_5_), channel_id=1, source_target_pairs={{0,8},{8,0},{16,24},{24,16},{1,9},{9,1},{17,25},{25,17},{2,10},{10... | collective-permute-start | bytes 589832 | tf_op jit(solution)/shard_map/ppermute | solution.py:406
  25.7 1.7 %collective-permute-start.5 = (bf16[32,3072]{1,0:T(8,128)(2,1)S(1)}, bf16[32,3072]{1,0:T(8,128)(2,1)S(1)}, u32[]{:S(2)}, u32[]{:S(2)}) collective-permute-start(bf16[32,3072]{1,0:T(8,128)(2,1)S(1)} %get-tuple-element.44.refs_1_), channel_id=1, source_target_pairs={{0,8},{8,0},{16,24},{24,16},{1,9},{9,1},{17,25},{25,17},{2,10},{10... | collective-permute-start | bytes 589832 | tf_op jit(solution)/shard_map/ppermute | solution.py:406
  26.7 5.2 %collective-permute-start.10 = (bf16[64,3072]{1,0:T(8,128)(2,1)S(1)}, bf16[64,3072]{1,0:T(8,128)(2,1)S(1)}, u32[]{:S(2)}, u32[]{:S(2)}) collective-permute-start(bf16[64,3072]{1,0:T(8,128)(2,1)S(1)} %order_rows.1.refs_0_), channel_id=1, source_target_pairs={{0,8},{8,0},{16,24},{24,16},{1,9},{9,1},{17,25},{25,17},{2,10},{10... | collective-permute-start | bytes 1179656 | tf_op jit(solution)/shard_map/ppermute | solution.py:406
  28.9 12.0 %collective-permute-start.18 = (bf16[64,3072]{1,0:T(8,128)(2,1)S(1)}, bf16[64,3072]{1,0:T(8,128)(2,1)S(1)}, u32[]{:S(2)}, u32[]{:S(2)}) collective-permute-start(bf16[64,3072]{1,0:T(8,128)(2,1)S(1)} %get-tuple-element.59.refs_0_), channel_id=1, source_target_pairs={{0,16},{8,24},{16,0},{24,8},{1,17},{9,25},{17,1},{25,9},{2,18},{10... | collective-permute-start | bytes 1179656 | tf_op jit(solution)/shard_map/ppermute | solution.py:403
  30.5 12.0 %collective-permute-start.6 = (bf16[128,1536]{1,0:T(8,128)(2,1)S(1)}, bf16[128,1536]{1,0:T(8,128)(2,1)S(1)}, u32[]{:S(2)}, u32[]{:S(2)}) collective-permute-start(bf16[128,1536]{1,0:T(8,128)(2,1)S(1)} %get-tuple-element.46.refs_3_), channel_id=1, source_target_pairs={{0,4},{4,0},{1,5},{5,1},{2,6},{6,2},{3,7},{7,3},{8,12},{12,8},{9,1... | collective-permute-start | bytes 1179656 | tf_op jit(solution)/shard_map/ppermute | solution.py:403
  32.0 1.2 %collective-permute-start.11 = (bf16[16,128]{1,0:T(8,128)(2,1)S(1)}, bf16[16,128]{1,0:T(8,128)(2,1)S(1)}, u32[]{:S(2)}, u32[]{:S(2)}) collective-permute-start(bf16[16,128]{1,0:T(8,128)(2,1)S(1)} %mark.2), channel_id=1, source_target_pairs={{0,8},{8,0},{16,24},{24,16},{1,9},{9,1},{17,25},{25,17},{2,10},{10... | collective-permute-start | bytes 12296 | tf_op jit(solution)/shard_map/ppermute | solution.py:406
  36.3 14.0 %collective-permute-start.17 = (bf16[128,1536]{1,0:T(8,128)(2,1)S(1)}, bf16[128,1536]{1,0:T(8,128)(2,1)S(1)}, u32[]{:S(2)}, u32[]{:S(2)}) collective-permute-start(bf16[128,1536]{1,0:T(8,128)(2,1)S(1)} %get-tuple-element.49.refs_3_), channel_id=1, source_target_pairs={{0,4},{4,0},{1,5},{5,1},{2,6},{6,2},{3,7},{7,3},{8,12},{12,8},{9,1... | collective-permute-start | bytes 1179656 | tf_op jit(solution)/shard_map/ppermute | solution.py:403
  36.9 16.6 %collective-permute-start.23 = (bf16[64,3072]{1,0:T(8,128)(2,1)S(1)}, bf16[64,3072]{1,0:T(8,128)(2,1)S(1)}, u32[]{:S(2)}, u32[]{:S(2)}) collective-permute-start(bf16[64,3072]{1,0:T(8,128)(2,1)S(1)} %get-tuple-element.63.refs_2_), channel_id=1, source_target_pairs={{0,16},{8,24},{16,0},{24,8},{1,17},{9,25},{17,1},{25,9},{2,18},{10... | collective-permute-start | bytes 1179656 | tf_op jit(solution)/shard_map/ppermute | solution.py:403
  40.9 14.3 %collective-permute-start.19 = (bf16[64,3072]{1,0:T(8,128)(2,1)S(1)}, bf16[64,3072]{1,0:T(8,128)(2,1)S(1)}, u32[]{:S(2)}, u32[]{:S(2)}) collective-permute-start(bf16[64,3072]{1,0:T(8,128)(2,1)S(1)} %collective-permute-done.18.refs_3_), channel_id=1, source_target_pairs={{0,8},{8,0},{16,24},{24,16},{1,9},{9,1},{17,25},{25,17},{2,10},{10... | collective-permute-start | bytes 1179656 | tf_op jit(solution)/shard_map/ppermute | solution.py:406
  44.1 1.5 %collective-permute-start.12 = (bf16[32,3072]{1,0:T(8,128)(2,1)S(1)}, bf16[32,3072]{1,0:T(8,128)(2,1)S(1)}, u32[]{:S(2)}, u32[]{:S(2)}) collective-permute-start(bf16[32,3072]{1,0:T(8,128)(2,1)S(1)} %get-tuple-element.51), channel_id=1, source_target_pairs={{0,8},{8,0},{16,24},{24,16},{1,9},{9,1},{17,25},{25,17},{2,10},{10... | collective-permute-start | bytes 589832 | tf_op jit(solution)/shard_map/ppermute | solution.py:406
  44.2 1.7 %collective-permute-start.13 = (bf16[32,3072]{1,0:T(8,128)(2,1)S(1)}, bf16[32,3072]{1,0:T(8,128)(2,1)S(1)}, u32[]{:S(2)}, u32[]{:S(2)}) collective-permute-start(bf16[32,3072]{1,0:T(8,128)(2,1)S(1)} %get-tuple-element.52), channel_id=1, source_target_pairs={{0,8},{8,0},{16,24},{24,16},{1,9},{9,1},{17,25},{25,17},{2,10},{10... | collective-permute-start | bytes 589832 | tf_op jit(solution)/shard_map/ppermute | solution.py:406
  46.0 12.3 %collective-permute-start.14 = (bf16[16,3072]{1,0:T(8,128)(2,1)S(1)}, bf16[16,3072]{1,0:T(8,128)(2,1)S(1)}, u32[]{:S(2)}, u32[]{:S(2)}) collective-permute-start(bf16[16,3072]{1,0:T(8,128)(2,1)S(1)} %get-tuple-element.54), channel_id=1, source_target_pairs={{0,1},{1,2},{2,3},{3,0},{4,5},{5,6},{6,7},{7,4},{8,9},{9,10},{10,1... | collective-permute-start | bytes 294920 | tf_op jit(solution)/shard_map/ppermute | solution.py:403
  47.7 11.3 %collective-permute-start.15 = (bf16[16,3072]{1,0:T(8,128)(2,1)S(1)}, bf16[16,3072]{1,0:T(8,128)(2,1)S(1)}, u32[]{:S(2)}, u32[]{:S(2)}) collective-permute-start(bf16[16,3072]{1,0:T(8,128)(2,1)S(1)} %get-tuple-element.55), channel_id=1, source_target_pairs={{0,2},{1,3},{2,0},{3,1},{4,6},{5,7},{6,4},{7,5},{8,10},{9,11},{10,... | collective-permute-start | bytes 294920 | tf_op jit(solution)/shard_map/ppermute | solution.py:403
  50.3 8.7 %collective-permute-start.16 = (bf16[16,3072]{1,0:T(8,128)(2,1)S(1)}, bf16[16,3072]{1,0:T(8,128)(2,1)S(1)}, u32[]{:S(2)}, u32[]{:S(2)}) collective-permute-start(bf16[16,3072]{1,0:T(8,128)(2,1)S(1)} %get-tuple-element.56), channel_id=1, source_target_pairs={{0,3},{1,0},{2,1},{3,2},{4,7},{5,4},{6,5},{7,6},{8,11},{9,8},{10,9... | collective-permute-start | bytes 294920 | tf_op jit(solution)/shard_map/ppermute | solution.py:403
  53.5 1.2 %collective-permute-start.20 = (bf16[16,128]{1,0:T(8,128)(2,1)S(1)}, bf16[16,128]{1,0:T(8,128)(2,1)S(1)}, u32[]{:S(2)}, u32[]{:S(2)}) collective-permute-start(bf16[16,128]{1,0:T(8,128)(2,1)S(1)} %mark.3), channel_id=1, source_target_pairs={{0,8},{8,0},{16,24},{24,16},{1,9},{9,1},{17,25},{25,17},{2,10},{10... | collective-permute-start | bytes 12296 | tf_op jit(solution)/shard_map/ppermute | solution.py:406
  54.7 10.0 %collective-permute-start.29 = (bf16[128,768]{1,0:T(8,128)(2,1)S(1)}, bf16[128,768]{1,0:T(8,128)(2,1)S(1)}, u32[]{:S(2)}, u32[]{:S(2)}) collective-permute-start(bf16[128,768]{1,0:T(8,128)(2,1)S(1)} %get-tuple-element.71), channel_id=1, source_target_pairs={{0,16},{8,24},{16,0},{24,8},{1,17},{9,25},{17,1},{25,9},{2,18},{10... | collective-permute-start | bytes 589832 | tf_op jit(solution)/shard_map/ppermute | solution.py:403
  55.2 5.4 %collective-permute-start.24 = (bf16[64,3072]{1,0:T(8,128)(2,1)S(1)}, bf16[64,3072]{1,0:T(8,128)(2,1)S(1)}, u32[]{:S(2)}, u32[]{:S(2)}) collective-permute-start(bf16[64,3072]{1,0:T(8,128)(2,1)S(1)} %collective-permute-done.23.refs_4_), channel_id=1, source_target_pairs={{0,8},{8,0},{16,24},{24,16},{1,9},{9,1},{17,25},{25,17},{2,10},{10... | collective-permute-start | bytes 1179656 | tf_op jit(solution)/shard_map/ppermute | solution.py:406
  58.4 2.3 %collective-permute-start.21 = (bf16[32,3072]{1,0:T(8,128)(2,1)S(1)}, bf16[32,3072]{1,0:T(8,128)(2,1)S(1)}, u32[]{:S(2)}, u32[]{:S(2)}) collective-permute-start(bf16[32,3072]{1,0:T(8,128)(2,1)S(1)} %get-tuple-element.61), channel_id=1, source_target_pairs={{0,8},{8,0},{16,24},{24,16},{1,9},{9,1},{17,25},{25,17},{2,10},{10... | collective-permute-start | bytes 589832 | tf_op jit(solution)/shard_map/ppermute | solution.py:406
  58.9 1.7 %collective-permute-start.22 = (bf16[32,3072]{1,0:T(8,128)(2,1)S(1)}, bf16[32,3072]{1,0:T(8,128)(2,1)S(1)}, u32[]{:S(2)}, u32[]{:S(2)}) collective-permute-start(bf16[32,3072]{1,0:T(8,128)(2,1)S(1)} %get-tuple-element.62), channel_id=1, source_target_pairs={{0,8},{8,0},{16,24},{24,16},{1,9},{9,1},{17,25},{25,17},{2,10},{10... | collective-permute-start | bytes 589832 | tf_op jit(solution)/shard_map/ppermute | solution.py:406
  59.0 8.3 %collective-permute-start.28 = (bf16[128,768]{1,0:T(8,128)(2,1)S(1)}, bf16[128,768]{1,0:T(8,128)(2,1)S(1)}, u32[]{:S(2)}, u32[]{:S(2)}) collective-permute-start(bf16[128,768]{1,0:T(8,128)(2,1)S(1)} %get-tuple-element.69), channel_id=1, source_target_pairs={{0,16},{8,24},{16,0},{24,8},{1,17},{9,25},{17,1},{25,9},{2,18},{10... | collective-permute-start | bytes 589832 | tf_op jit(solution)/shard_map/ppermute | solution.py:403
  60.6 11.8 %copy-start = (bf16[16,3072]{1,0:T(8,128)(2,1)}, bf16[16,3072]{1,0:T(8,128)(2,1)S(1)}, u32[]{:S(2)}) copy-start(bf16[16,3072]{1,0:T(8,128)(2,1)S(1)} %add_convert_fusion.1.refs_4_.refs_8_.refs_7_) | copy-start | bytes 294916
  60.8 9.3 %collective-permute-start.25 = (bf16[16,3072]{1,0:T(8,128)(2,1)S(1)}, bf16[16,3072]{1,0:T(8,128)(2,1)S(1)}, u32[]{:S(2)}, u32[]{:S(2)}) collective-permute-start(bf16[16,3072]{1,0:T(8,128)(2,1)S(1)} %get-tuple-element.65), channel_id=1, source_target_pairs={{0,1},{1,2},{2,3},{3,0},{4,5},{5,6},{6,7},{7,4},{8,9},{9,10},{10,1... | collective-permute-start | bytes 294920 | tf_op jit(solution)/shard_map/ppermute | solution.py:403
  60.8 10.8 %collective-permute-start.26 = (bf16[16,3072]{1,0:T(8,128)(2,1)S(1)}, bf16[16,3072]{1,0:T(8,128)(2,1)S(1)}, u32[]{:S(2)}, u32[]{:S(2)}) collective-permute-start(bf16[16,3072]{1,0:T(8,128)(2,1)S(1)} %get-tuple-element.66), channel_id=1, source_target_pairs={{0,2},{1,3},{2,0},{3,1},{4,6},{5,7},{6,4},{7,5},{8,10},{9,11},{10,... | collective-permute-start | bytes 294920 | tf_op jit(solution)/shard_map/ppermute | solution.py:403
  62.6 9.0 %collective-permute-start.27 = (bf16[16,3072]{1,0:T(8,128)(2,1)S(1)}, bf16[16,3072]{1,0:T(8,128)(2,1)S(1)}, u32[]{:S(2)}, u32[]{:S(2)}) collective-permute-start(bf16[16,3072]{1,0:T(8,128)(2,1)S(1)} %get-tuple-element.67), channel_id=1, source_target_pairs={{0,3},{1,0},{2,1},{3,2},{4,7},{5,4},{6,5},{7,6},{8,11},{9,8},{10,9... | collective-permute-start | bytes 294920 | tf_op jit(solution)/shard_map/ppermute | solution.py:403
  (1 other events, 0.9 us)

commit v4 on v3

v4 whole, which is shorter than its diff:
```python
import functools

import jax
import jax.numpy as jnp
from jax import lax
from jax.experimental import pallas as pl
from jax.experimental.pallas import tpu as pltpu
from jax.sharding import PartitionSpec as P

CORES = 2
CFG = {'cot_early': 0, 'tok_pieces': 1, 'cot_pieces': 2, 'out_pieces': 2, 'in_pieces': 1, 'load2': 'pre', 'order2': 'load2', 'hop_cot': 0, 'hop_c': 0, 'hop_d': 0, 'back_pre': 0, 'tok_y': 'preact', 'cot_y': 'back', 'k3_back': 0, 'k3_toky': 0, 'se_d': 0, 'k4': ['E'], 'sf': ['bo'], 'wg_bo': 0, 'hid': 'merged'}
MIB = 1024 * 1024
NT = (((1,), (1,)), ((), ()))
NN = (((1,), (0,)), ((), ()))
TN = (((0,), (0,)), ((), ()))
VMEM = pl.BlockSpec(memory_space=pltpu.VMEM)
SMEM = pl.BlockSpec(memory_space=pltpu.SMEM)
HBM = pl.BlockSpec(memory_space=pltpu.HBM)
ANY = pl.BlockSpec(memory_space=pl.ANY)


def mm(a, b, dims):
    return lax.dot_general(a, b, dims, preferred_element_type=jnp.float32)


def tile_of(size, most):
    for tile in range(most, 0, -128):
        if size % tile == 0:
            return tile
    return size


def in_hbm(x):
    return pltpu.with_memory_space_constraint(x, pltpu.HBM)


def call(
    kernel, in_specs, out_specs, out_shape, name, scratch=(), limit=24, after=(), cost=0
):
    reads = len(in_specs)

    def run(*refs):
        kernel(*refs[:reads], *refs[reads + len(after) :])

    kernel_call = pl.pallas_call(
        run,
        in_specs=list(in_specs) + [ANY] * len(after),
        out_specs=out_specs,
        out_shape=out_shape,
        scratch_shapes=scratch,
        compiler_params=pltpu.CompilerParams(vmem_limit_bytes=limit * MIB),
        cost_estimate=pl.CostEstimate(flops=0, bytes_accessed=cost * MIB, transcendentals=0),
        name=name,
    )
    return lambda *args: kernel_call(*args, *after)


def shape(dims, dtype=jnp.bfloat16):
    return jax.ShapeDtypeStruct(tuple(dims), dtype)


def load_kernel(dp, size, pieces, columns, place, w, out, sems):
    blocks = dp // CORES
    rows = (w.shape[0] if columns else size) // pieces
    copies = []
    for b in range(blocks):
        for p in range(pieces):
            if columns:
                cut = pl.ds(p * rows, rows)
                source = w.at[cut, pl.ds(pl.multiple_of(lax.rem(place[0] + CORES * b, dp) * size, 128), size)]
                to = out.at[cut, pl.ds(b * size, size)]
            else:
                at = pl.multiple_of(lax.rem(place[0] + CORES * b, dp) * size + p * rows, 16)
                source = w.at[pl.ds(at, rows)]
                to = out.at[pl.ds(b * size + p * rows, rows)]
            copies.append(pltpu.make_async_copy(source, to, sems.at[b * pieces + p]))
    for copy in copies:
        copy.start()
    for copy in copies:
        copy.wait()


def load(place, w, dp, size, columns, name, after):
    blocks, pieces = dp // CORES, 8
    units = blocks * size
    return call(
        functools.partial(load_kernel, dp, size, pieces, columns),
        [SMEM, HBM],
        VMEM,
        pltpu.VMEM((w.shape[0], units) if columns else (units, w.shape[1]), jnp.bfloat16),
        name,
        scratch=[pltpu.SemaphoreType.DMA((blocks * pieces,))],
        after=after,
    )(place, in_hbm(w))


def split_kernel(place, tokens, cots, cot, *rest):
    *outs, sems = rest
    count, width = len(outs), outs[0].shape[1]
    copies = [pltpu.make_async_copy(cots, cot, sems.at[count])]
    for k in reversed(range(count)):
        at = lax.rem(place[0] + k, count) * width
        source = tokens.at[:, pl.ds(pl.multiple_of(at, 128), width)]
        copies.append(pltpu.make_async_copy(source, outs[k], sems.at[k]))
    for copy in reversed(copies):
        copy.start()
    for copy in copies:
        copy.wait()


def split(row_place, tokens, cots, count):
    rows, width = tokens.shape[0], tokens.shape[1] // count
    return call(
        split_kernel,
        [SMEM, HBM, HBM],
        [VMEM] * (1 + count),
        [shape(cots.shape)] + [shape((rows, width))] * count,
        "split_width",
        scratch=[pltpu.SemaphoreType.DMA((1 + count,))],
    )(row_place, tokens, cots)


def stack_kernel(*refs):
    *parts, cot, out, cot_out = refs
    out[...] = jnp.concatenate([r[...].astype(jnp.float32) for r in parts]).astype(out.dtype)
    cot_out[...] = cot[...]


def stack(parts, cot):
    rows, width = parts[0].shape
    return call(
        stack_kernel,
        [VMEM] * (1 + len(parts)),
        [VMEM] * 2,
        [shape((rows * len(parts), width)), shape(cot.shape)],
        "stack_rows",
    )(*parts, cot)


def tokens_kernel(row, pieces, row_place, col_place, *refs):
    stacks, outs, held = refs[: -1 - pieces], refs[-1 - pieces : -1], refs[-1]
    col, n = len(stacks), held.shape[1]
    rows_out = outs[0].shape[0]
    my_row, my_col = row_place[0], col_place[0]
    for k, part in enumerate(stacks):
        rows = part[...].astype(jnp.float32)
        for r in range(row):
            at = lax.rem(my_row + row - r, row) * col + lax.rem(my_col + col - k, col)
            held[at] = rows[r * n : (r + 1) * n]
    for at in range(0, row * col, 2):
        pair = jnp.concatenate([held[at], held[at + 1]])
        piece, start = divmod(at * n, rows_out)
        outs[piece][start : start + 2 * n] = pair.astype(jnp.bfloat16)


def tokens_in_order(row_place, col_place, stacks, row, after, pieces):
    rows, width = stacks[0].shape
    col = len(stacks)
    return call(
        functools.partial(tokens_kernel, row, pieces),
        [SMEM, SMEM] + [VMEM] * col,
        [VMEM] * pieces,
        [shape((rows * col // pieces, width))] * pieces,
        "order_tokens",
        scratch=[pltpu.VMEM((row * col, rows // row, width), jnp.float32)],
        after=after,
    )(row_place, col_place, *stacks)


def order_kernel(count, place, *refs):
    parts, outs, held = refs[:count], refs[count:-1], refs[-1]
    me, rows = place[0], parts[0].shape[0]
    for k, part in enumerate(parts):
        held[lax.rem(me + count - k, count)] = part[...]
    each = count // len(outs)
    for k in range(count):
        start = k % each * rows
        outs[k // each][start : start + rows] = held[k]


def in_order(col_place, parts, after, pieces):
    rows, width = parts[0].shape
    count = len(parts)
    return call(
        functools.partial(order_kernel, count),
        [SMEM] + [VMEM] * count,
        [VMEM] * pieces,
        [shape((rows * count // pieces, width))] * pieces,
        "order_rows",
        scratch=[pltpu.VMEM((count, rows, width), jnp.bfloat16)],
        after=after,
    )(col_place, *parts)


def first_kernel(dims, tile, mine, count, *refs):
    groups, w, refs = refs[:count], refs[count], refs[count + 1 :]
    if len(refs) == 6:
        refs[4][...] = refs[0][...]
        refs = refs[1:4] + refs[5:]
    total, sent, own_out, rows = refs
    at = 0
    for i, group in enumerate(groups):
        cut = slice(at, at + group.shape[0])
        rows[cut] = group[...]
        if i < mine:
            own_out[cut] = group[...]
        at += group.shape[0]
    for at in range(0, total.shape[1], tile):
        cut = slice(at, at + tile)
        part = mm(rows[...], w[:, cut] if dims is NN else w[cut, :], dims)
        total[:, cut] = part
        sent[:, cut] = part.astype(jnp.bfloat16)


def first(own, other, w, dims, name, after=(), passing=None):
    half, width = len(own) * own[0].shape[0], own[0].shape[1]
    n = 2 * half
    units = w.shape[1 if dims is NN else 0]
    extra = [] if passing is None else [passing]
    return call(
        functools.partial(first_kernel, dims, tile_of(units, 256), len(own), len(own) + len(other)),
        [VMEM] * (len(own) + len(other) + 1 + len(extra)),
        [VMEM] * (3 + len(extra)),
        [shape((n, units), jnp.float32), shape((n, units)), shape((half, width))]
        + [shape(x.shape) for x in extra],
        name,
        scratch=[pltpu.VMEM((n, width), jnp.bfloat16)],
        after=after,
    )(*own, *other, w, *extra)


def gelu_parts(preact):
    cdf = 0.5 * (1.0 + lax.erf(preact * 0.7071067811865476))
    slopes = cdf + preact * jnp.exp(-0.5 * preact * preact) * 0.3989422804014327
    return (preact * cdf, slopes)


def second_product(dims, vals, w, keep, sends):
    half, width = keep.shape
    tile = tile_of(width, 512)
    for at in range(0, width, tile):
        cut = slice(at, at + tile)
        part = mm(vals[...], w[:, cut] if dims is NN else w[cut, :], dims)
        keep[:, cut] = part[:half]
        for i, send in enumerate(sends):
            rows = send.shape[0]
            send[:, cut] = part[half + i * rows : half + (i + 1) * rows].astype(jnp.bfloat16)


def row_sum(total, parts, cut):
    whole = total[:, cut]
    for part in parts:
        whole = whole + part[:, cut].astype(jnp.float32)
    return whole


def forward_kernel(blocks, shares, pieces, passing, *refs):
    total, parts, w = refs[0], refs[1 : 1 + shares], refs[1 + shares]
    passed, refs = refs[2 + shares : 2 + shares + passing], refs[2 + shares + passing :]
    keep, *sends = refs[: 1 + pieces]
    slopes, *hidden, vals = refs[1 + pieces :]
    hidden, outs = hidden[:blocks], hidden[blocks:]
    for a, b in zip(passed, outs):
        b[...] = a[...]
    size = total.shape[1] // blocks
    for b in range(blocks):
        cut = slice(b * size, (b + 1) * size)
        value, slope = gelu_parts(row_sum(total, parts, cut))
        value = value.astype(jnp.bfloat16)
        vals[:, cut] = value
        hidden[b][...] = value
        slopes[:, cut] = slope
    second_product(NN, vals, w, keep, sends)


def backward_kernel(blocks, shares, pieces, passing, *refs):
    total, parts, slopes, w = refs[0], refs[1 : 1 + shares], refs[1 + shares], refs[2 + shares]
    hidden, refs = refs[3 + shares : 3 + shares + passing], refs[3 + shares + passing :]
    keep, *sends = refs[: 1 + pieces]
    *pre, vals = refs[1 + pieces :]
    n, size = total.shape[0], total.shape[1] // blocks
    for b in range(blocks):
        cut = slice(b * size, (b + 1) * size)
        value = (row_sum(total, parts, cut) * slopes[:, cut]).astype(jnp.bfloat16)
        vals[:, cut] = value
        pre[b][:n] = value
        if b > 0 and passing:
            pre[b][n:] = hidden[b - 1][...]
    second_product(NT, vals, w, keep, sends)


def second(total, parts, slopes, w, size, name, passing, after, pieces):
    n, units = total.shape
    half = n // 2
    blocks = units // size
    forward = slopes is None
    width = w.shape[1] if forward else w.shape[0]
    out_shape = [shape((half, width), jnp.float32)] + [shape((half // pieces, width))] * pieces
    if forward:
        out_shape.append(shape((n, units), jnp.float32))
        out_shape += [shape((n, size))] * blocks + [shape(x.shape) for x in passing]
    else:
        other = 2 * n if passing else n
        out_shape += [shape((n, size))] + [shape((other, size))] * (blocks - 1)
    extra = [] if forward else [slopes]
    kernel = forward_kernel if forward else backward_kernel
    return call(
        functools.partial(kernel, blocks, len(parts), pieces, len(passing)),
        [VMEM] * (2 + len(parts) + len(extra) + len(passing)),
        [VMEM] * len(out_shape),
        out_shape,
        name,
        scratch=[pltpu.VMEM((n, units), jnp.bfloat16)],
        after=after,
    )(total, *parts, *extra, w, *passing)


def cores_kernel(pieces, place, keep, *refs):
    parts, own = refs[:pieces], refs[pieces]
    *sent, held = refs[pieces + 1 :]
    rows = own.shape[0]
    at = 0
    for part in parts:
        cut = slice(at, at + part.shape[0])
        held[cut] = keep[cut] + part[...].astype(jnp.float32)
        at += part.shape[0]
    count = 1 + len(sent)
    me = place[0]
    for k in range(count):
        at = pl.ds(pl.multiple_of(lax.rem(me + k, count) * rows, 16), rows)
        if k == 0:
            own[...] = held[at]
        else:
            sent[k - 1][...] = held[at].astype(jnp.bfloat16)


def cores_sum(col_place, keep, parts, count, name, after=()):
    rows, width = keep.shape[0] // count, keep.shape[1]
    return call(
        functools.partial(cores_kernel, len(parts)),
        [SMEM, VMEM] + [VMEM] * len(parts),
        [VMEM] * count,
        [shape((rows, width), jnp.float32)] + [shape((rows, width))] * (count - 1),
        name,
        scratch=[pltpu.VMEM(keep.shape, jnp.float32)],
        after=after,
    )(col_place, keep, *parts)


def mark_kernel(*refs):
    refs[-1][...] = refs[0][:16, :128]


def mark(parts):
    return call(mark_kernel, [VMEM] * len(parts), VMEM, shape((16, 128)), "mark")(*parts)


def weight_kernel(left_cuts, right_cuts, tile, across, *refs):
    lefts = len(left_cuts)
    left, right, out = refs[:lefts], refs[lefts:-5], refs[-5]
    rows_left, rows_right, staged, sems = refs[-4:]
    for groups, cuts, rows in ((left, left_cuts, rows_left), (right, right_cuts, rows_right)):
        at = 0
        for group, (start, stop) in zip(groups, cuts):
            rows[at : at + stop - start] = group[start:stop]
            at += stop - start
    copies = []
    for i, at in enumerate(range(0, out.shape[1 if across else 0], tile)):
        cut = slice(at, at + tile)
        if across:
            part, where = mm(rows_left[...], rows_right[:, cut], TN), (slice(None), cut)
        else:
            part, where = mm(rows_left[:, cut], rows_right[...], TN), (cut, slice(None))
        staged[where] = part.astype(jnp.bfloat16)
        copies.append(pltpu.make_async_copy(staged.at[where], out.at[where], sems.at[i]))
        copies[-1].start()
    for copy in copies:
        copy.wait()


def weight_grad(left, right, across, name, after):
    left, left_cuts = [x for x, _ in left], [cut for _, cut in left]
    right, right_cuts = [x for x, _ in right], [cut for _, cut in right]
    n = sum(stop - start for start, stop in left_cuts)
    k, m = left[0].shape[1], right[0].shape[1]
    long = m if across else k
    tile = tile_of(long, 512)
    return call(
        functools.partial(weight_kernel, left_cuts, right_cuts, tile, across),
        [VMEM] * (len(left) + len(right)),
        HBM,
        shape((k, m)),
        name,
        scratch=[
            pltpu.VMEM((n, k), jnp.bfloat16),
            pltpu.VMEM((n, m), jnp.bfloat16),
            pltpu.VMEM((k, m), jnp.bfloat16),
            pltpu.SemaphoreType.DMA((long // tile,)),
        ],
        after=after,
        cost=0,
    )(*left, *right)


def body(dp, row, col, tokens, w_in, w_out, grad_out):
    blocks, m = dp // CORES, grad_out.shape[0]
    width, size = w_in.shape[0], w_in.shape[2] // dp
    mine = lax.axis_index("dp")
    place = mine.astype(jnp.int32)[None]
    row_place = lax.axis_index("row").astype(jnp.int32)[None]
    col_place = lax.axis_index("col").astype(jnp.int32)[None]
    C = CFG

    def shifted(x, axis, step):
        count = {"dp": dp, "row": row, "col": col}[axis]
        return lax.ppermute(x, axis, [(i, (i + step) % count) for i in range(count)])

    def across_cores(x):
        return lax.ppermute(x, "dp", [(i, i ^ 1) for i in range(dp)])

    def across_rows(x):
        return [shifted(x, "row", step) for step in range(1, row)]

    def all_replicas(own, other, there):
        groups = [own, *other]
        for part in there:
            groups += [part, across_cores(part)]
        return groups

    def hop(parts, on):
        return [across_cores(mark(parts))] if on else []

    cot_mine, own, *other_widths = split(row_place, in_hbm(tokens), in_hbm(grad_out), row)
    stacked, cot_mine2 = stack(
        [own] + [shifted(part, "row", step + 1) for step, part in enumerate(other_widths)],
        cot_mine,
    )
    src = cot_mine if C["cot_early"] else cot_mine2
    stacks = [stacked] + [shifted(stacked, "col", step) for step in range(1, col)]
    cots = [src] + [shifted(src, "col", step) for step in range(1, col)]
    w_first = load(place, w_in[:, 0, :], dp, size, True, "load_first", [stacked])
    tok = tokens_in_order(row_place, col_place, stacks, row, [w_first], C["tok_pieces"])
    tok_other = [across_cores(x) for x in tok]
    pre_total, pre_sent, tok_later = first(tok, tok_other, w_first, NN, "preact_partial")
    pre_parts = across_rows(pre_sent)
    w_second = load(place, w_out[0], dp, size, False, "load_second", {"first": [w_first], "tok": [tok[0]], "pre": [pre_sent]}[C["load2"]])
    cot = in_order(col_place, cots, {"first": [w_first], "tok": [tok[0]], "pre": [pre_sent], "load2": [w_second]}[C["order2"]], C["cot_pieces"])
    cot_other = [across_cores(x) for x in cot]
    hops = hop(cot_other, C["hop_cot"])
    back_total, back_sent, cot_later, *passed = first(cot, cot_other, w_second, NT, "back_partial", [pre_sent] * C["back_pre"] + hops, tok_later if C["tok_y"] == "back" else None)
    if passed:
        tok_later = passed[0]
    back_parts = across_rows(back_sent)
    if C["tok_y"] != "K3":
        tok_there = [shifted(tok_later, "dp", CORES * b) for b in range(1, blocks)]
    if C["cot_y"] != "K3":
        cot_there = [shifted(cot_later, "dp", CORES * b) for b in range(1, blocks)]
    after = [back_sent] * C["k3_back"] + (tok_there if C["k3_toky"] else [])
    after += hop(pre_parts, C["hop_c"])
    passing = [tok_later] * (C["tok_y"] == "K3") + [cot_later] * (C["cot_y"] == "K3")
    out_keep, *rest = second(
        pre_total, pre_parts, None, w_second, size, "block_out_partial", passing, after, C["out_pieces"]
    )
    out_sends, rest = rest[: C["out_pieces"]], rest[C["out_pieces"] :]
    slopes, rest = rest[0], rest[1:]
    hidden, passed = rest[:blocks], rest[blocks:]
    if C["tok_y"] == "K3":
        tok_there = [shifted(passed[0], "dp", CORES * b) for b in range(1, blocks)]
    if C["cot_y"] == "K3":
        cot_there = [shifted(passed[-1], "dp", CORES * b) for b in range(1, blocks)]
    out_own, *out_sent = cores_sum(
        col_place, out_keep, [across_cores(x) for x in out_sends], col, "block_out_cores",
        back_parts if C["se_d"] else []
    )

    def col_total(own, sent):
        for step, part in enumerate(sent):
            own = own + shifted(part, "col", step + 1).astype(jnp.float32)
        return own.astype(jnp.bfloat16)

    block_out = col_total(out_own, out_sent)
    tok_all = all_replicas(tok_later, tok_other, tok_there)
    cot_all = all_replicas(cot_later, cot_other, cot_there)
    full_ties = {"E": out_own, "bo": block_out, "ty": tok_there[-1], "cy": cot_there[-1], "tx": tok_all[-1], "cx": cot_all[-1]}
    after = [full_ties[t] for t in C["k4"]] + hop(back_parts, C["hop_d"])
    merged = C["hid"] == "merged"
    in_keep, *rest = second(
        back_total, back_parts, slopes, w_first, size, "grad_in_partial", hidden[1:] if merged else (), after, C["in_pieces"]
    )
    in_sends, both = rest[: C["in_pieces"]], rest[C["in_pieces"] :]
    in_own, *in_sent = cores_sum(
        col_place, in_keep, [across_cores(x) for x in in_sends], col, "grad_in_cores",
        [full_ties[t] for t in C["sf"]]
    )
    grad_in = col_total(in_own, in_sent)

    def full(groups):
        return [(x, (0, x.shape[0])) for x in groups]

    owned = [shifted(both[b], "dp", CORES * b) for b in range(1, blocks)]
    n = hidden[0].shape[0]
    pre_mine = full(both[:1]) + [(x, (0, n)) for x in owned]
    if merged:
        hid_mine = full(hidden[:1]) + [(x, (n, 2 * n)) for x in owned]
    else:
        hid_mine = full(hidden[:1] + [shifted(hidden[b], "dp", CORES * b) for b in range(1, blocks)])
    after = [in_own] + [block_out] * C["wg_bo"]
    grad_out_w = weight_grad(hid_mine, full(cot_all), True, "grad_w_out", after)
    grad_in_w = weight_grad(full(tok_all), pre_mine, False, "grad_w_in", after)
    return block_out, grad_in, grad_in_w[:, None, :], grad_out_w[None]


def solution(mesh):
    in_specs = (
        P(("dp", "row", "col"), None),
        P("row", "col", None),
        P("col", None, "row"),
        P(("dp", "col"), "row"),
    )
    out_specs = (
        P(("dp", "col"), "row"),
        P(("dp", "col"), "row"),
        P("row", "col", "dp"),
        P("col", "dp", "row"),
    )
    sizes = (mesh.shape["dp"], mesh.shape["row"], mesh.shape["col"])
    return jax.shard_map(
        functools.partial(body, *sizes),
        mesh=mesh,
        in_specs=in_specs,
        out_specs=out_specs,
        check_vma=False,
    )
```

time: 72.5 us -> 66.9 us (0.923)
  starting transfers between devices: 31.7 us -> 29.5 us
  waiting for transfers between devices: 14 us -> 11.8 us
  local copies, waits for them, and re-layouts: 1.78 us -> 0.01 us
    ppermute x11 -> x8, waiting for transfers between devices: 4.21 us -> 1.23 us  [across_cores(): return lax.ppermute(x, 'dp', [(i, i ^ 1) for i in range(dp)])]
    unnamed x6 -> x2, local copies, waits for them, and re-layouts: 1.78 us -> 0.01 us
    ppermute x19 -> x18, starting transfers between devices: 29.8 us -> 28.3 us  [shifted(): lax.ppermute(x, axis, [(i, (i + step) % count) for i in range(count)])]
    ppermute x19 -> x18, waiting for transfers between devices: 9.8 us -> 10.5 us  [shifted(): lax.ppermute(x, axis, [(i, (i + step) % count) for i in range(count)])]
    pallas_call x15 -> x14, Pallas kernels: 23.1 us -> 23.8 us  [call(): return lambda *args: kernel_call(*args, *after)]
    ppermute x11 -> x8, starting transfers between devices: 1.87 us -> 1.21 us  [across_cores(): return lax.ppermute(x, 'dp', [(i, i ^ 1) for i in range(dp)])]
  transfers between devices with their start and end apart: 30 -> 26, of which waited for: 12 -> 9; matrix products, arithmetic and copies ran while one was open for 0% -> 0% of each run, Pallas kernels for 32% -> 34%
where the time goes in v4:
time: 66.9 us; the launch traced here: 66.7 us
  starting transfers between devices  29.5 us (44%)
  Pallas kernels  23.8 us (36%)
  waiting for transfers between devices  11.8 us (18%)
  between operations  0.86 us (1%)
  other arithmetic  0.75 us (1%)
    ppermute x18, starting transfers between devices, shifted(): lax.ppermute(x, axis, [(i, (i + step) % count) for i in range(count)])  28.3 us
    pallas_call x14, Pallas kernels, call(): return lambda *args: kernel_call(*args, *after)  23.8 us
    ppermute x18, waiting for transfers between devices, shifted(): lax.ppermute(x, axis, [(i, (i + step) % count) for i in range(count)])  10.5 us
  transfers between devices with their start and end apart: 26, of which 9 were waited for; matrix products, arithmetic and copies ran while one was open for 0% of the time, Pallas kernels for 34%

profile of v4, /device:TPU:0, one launch (start us, length us, event | category | flops | bytes accessed | tf_op | source)
XLA Modules:
  0.0 66.7 jit_solution(15126940164021722800)
XLA Ops:
  0.6 1.0 %split_width.1 = (bf16[16,3072]{1,0:T(8,128)(2,1)S(1)}, bf16[8,3072]{1,0:T(8,128)(2,1)S(1)}, bf16[8,3072]{1,0:T(8,128)(2,1)S(1)}) custom-call(s32[1]{0:T(128)} %bitcast.1.refs_0_, bf16[8,6144]{1,0:T(8,128)(2,1)} %refs_1_.1, bf16[16,3072]{1,0:T(8,128)(2,1)} %refs_2_.1), custom_call_target="tpu_custom_call" | custom-call | tf_op jit(solution)/shard_map/split_width/pallas_call | solution.py:55
  1.6 3.0 %collective-permute-start = (bf16[8,3072]{1,0:T(8,128)(2,1)S(1)}, bf16[8,3072]{1,0:T(8,128)(2,1)S(1)}, u32[]{:S(2)}, u32[]{:S(2)}) collective-permute-start(bf16[8,3072]{1,0:T(8,128)(2,1)S(1)} %get-tuple-element.36), channel_id=1, source_target_pairs={{0,4},{4,0},{1,5},{5,1},{2,6},{6,2},{3,7},{7,3},{8,12},{12,8},{9,1... | collective-permute-start | bytes 147464 | tf_op jit(solution)/shard_map/ppermute | solution.py:416
  4.6 2.1 %collective-permute-done.refs_1_ = bf16[8,3072]{1,0:T(8,128)(2,1)S(1)} collective-permute-done((bf16[8,3072]{1,0:T(8,128)(2,1)S(1)}, bf16[8,3072]{1,0:T(8,128)(2,1)S(1)}, u32[]{:S(2)}, u32[]{:S(2)}) %collective-permute-start) | collective-permute-done | bytes 49184 | tf_op jit(solution)/shard_map/ppermute | solution.py:416
  6.7 2.2 %collective-permute-start.1 = (bf16[16,3072]{1,0:T(8,128)(2,1)S(1)}, bf16[16,3072]{1,0:T(8,128)(2,1)S(1)}, u32[]{:S(2)}, u32[]{:S(2)}) collective-permute-start(bf16[16,3072]{1,0:T(8,128)(2,1)S(1)} %get-tuple-element.38.refs_2_), channel_id=1, source_target_pairs={{0,1},{1,2},{2,3},{3,0},{4,5},{5,6},{6,7},{7,4},{8,9},{9,10},{10,1... | collective-permute-start | bytes 294920 | tf_op jit(solution)/shard_map/ppermute | solution.py:416
  8.9 2.6 %collective-permute-start.2 = (bf16[16,3072]{1,0:T(8,128)(2,1)S(1)}, bf16[16,3072]{1,0:T(8,128)(2,1)S(1)}, u32[]{:S(2)}, u32[]{:S(2)}) collective-permute-start(bf16[16,3072]{1,0:T(8,128)(2,1)S(1)} %get-tuple-element.38.refs_2_), channel_id=1, source_target_pairs={{0,2},{1,3},{2,0},{3,1},{4,6},{5,7},{6,4},{7,5},{8,10},{9,11},{10,... | collective-permute-start | bytes 294920 | tf_op jit(solution)/shard_map/ppermute | solution.py:416
  11.5 1.3 %collective-permute-start.3 = (bf16[16,3072]{1,0:T(8,128)(2,1)S(1)}, bf16[16,3072]{1,0:T(8,128)(2,1)S(1)}, u32[]{:S(2)}, u32[]{:S(2)}) collective-permute-start(bf16[16,3072]{1,0:T(8,128)(2,1)S(1)} %get-tuple-element.38.refs_2_), channel_id=1, source_target_pairs={{0,3},{1,0},{2,1},{3,2},{4,7},{5,4},{6,5},{7,6},{8,11},{9,8},{10,9... | collective-permute-start | bytes 294920 | tf_op jit(solution)/shard_map/ppermute | solution.py:416
  12.8 3.9 %load_first.1.refs_6_.refs_2_.refs_3_ = bf16[3072,1536]{1,0:T(8,128)(2,1)S(1)} custom-call(s32[1]{0:T(128)} %bitcast.2.refs_0_, bf16[3072,3072]{1,0:T(8,128)(2,1)} %bitcast.7, bf16[16,3072]{1,0:T(8,128)(2,1)S(1)} %get-tuple-element.38.refs_2_), custom_call_target="tpu_custom_call" | custom-call | tf_op jit(solution)/shard_map/load_first/pallas_call | solution.py:55
  17.3 2.3 %collective-permute-start.11 = (bf16[16,3072]{1,0:T(8,128)(2,1)S(1)}, bf16[16,3072]{1,0:T(8,128)(2,1)S(1)}, u32[]{:S(2)}, u32[]{:S(2)}) collective-permute-start(bf16[16,3072]{1,0:T(8,128)(2,1)S(1)} %get-tuple-element.48.refs_1_), channel_id=1, source_target_pairs={{0,1},{1,2},{2,3},{3,0},{4,5},{5,6},{6,7},{7,4},{8,9},{9,10},{10,1... | collective-permute-start | bytes 294920 | tf_op jit(solution)/shard_map/ppermute | solution.py:416
  19.7 1.8 %collective-permute-start.12 = (bf16[16,3072]{1,0:T(8,128)(2,1)S(1)}, bf16[16,3072]{1,0:T(8,128)(2,1)S(1)}, u32[]{:S(2)}, u32[]{:S(2)}) collective-permute-start(bf16[16,3072]{1,0:T(8,128)(2,1)S(1)} %get-tuple-element.48.refs_1_), channel_id=1, source_target_pairs={{0,2},{1,3},{2,0},{3,1},{4,6},{5,7},{6,4},{7,5},{8,10},{9,11},{10,... | collective-permute-start | bytes 294920 | tf_op jit(solution)/shard_map/ppermute | solution.py:416
  21.4 0.7 %collective-permute-start.13 = (bf16[16,3072]{1,0:T(8,128)(2,1)S(1)}, bf16[16,3072]{1,0:T(8,128)(2,1)S(1)}, u32[]{:S(2)}, u32[]{:S(2)}) collective-permute-start(bf16[16,3072]{1,0:T(8,128)(2,1)S(1)} %get-tuple-element.48.refs_1_), channel_id=1, source_target_pairs={{0,3},{1,0},{2,1},{3,2},{4,7},{5,4},{6,5},{7,6},{8,11},{9,8},{10,9... | collective-permute-start | bytes 294920 | tf_op jit(solution)/shard_map/ppermute | solution.py:416
  22.1 1.4 %preact_partial.1 = (f32[128,1536]{1,0:T(8,128)S(1)}, bf16[128,1536]{1,0:T(8,128)(2,1)S(1)}, bf16[64,3072]{1,0:T(8,128)(2,1)S(1)}) custom-call(bf16[64,3072]{1,0:T(8,128)(2,1)S(1)} %order_tokens.1.refs_0_, bf16[64,3072]{1,0:T(8,128)(2,1)S(1)} %collective-permute-done.4.refs_1_, bf16[3072,1536]{1,0:T(8,128)(2,1)S(1)} %load_first.1.refs_6_.refs_2_.refs_3_), custom_call_target="tpu_custom_call" | custom-call | tf_op jit(solution)/shard_map/preact_partial/pallas_call | solution.py:55
  23.5 1.6 %collective-permute-start.5 = (bf16[128,1536]{1,0:T(8,128)(2,1)S(1)}, bf16[128,1536]{1,0:T(8,128)(2,1)S(1)}, u32[]{:S(2)}, u32[]{:S(2)}) collective-permute-start(bf16[128,1536]{1,0:T(8,128)(2,1)S(1)} %get-tuple-element.40.refs_2_), channel_id=1, source_target_pairs={{0,4},{4,0},{1,5},{5,1},{2,6},{6,2},{3,7},{7,3},{8,12},{12,8},{9,1... | collective-permute-start | bytes 1179656 | tf_op jit(solution)/shard_map/ppermute | solution.py:416
  25.1 3.8 %load_second.1.refs_2_.refs_5_.refs_4_ = bf16[1536,3072]{1,0:T(8,128)(2,1)S(1)} custom-call(s32[1]{0:T(128)} %bitcast.2.refs_0_, bf16[3072,3072]{1,0:T(8,128)(2,1)} %bitcast.8, bf16[128,1536]{1,0:T(8,128)(2,1)S(1)} %get-tuple-element.40.refs_2_), custom_call_target="tpu_custom_call" | custom-call | tf_op jit(solution)/shard_map/load_second/pallas_call | solution.py:55
  29.6 1.5 %collective-permute-start.21 = (bf16[64,3072]{1,0:T(8,128)(2,1)S(1)}, bf16[64,3072]{1,0:T(8,128)(2,1)S(1)}, u32[]{:S(2)}, u32[]{:S(2)}) collective-permute-start(bf16[64,3072]{1,0:T(8,128)(2,1)S(1)} %get-tuple-element.61.refs_0_), channel_id=1, source_target_pairs={{0,16},{8,24},{16,0},{24,8},{1,17},{9,25},{17,1},{25,9},{2,18},{10... | collective-permute-start | bytes 1179656 | tf_op jit(solution)/shard_map/ppermute | solution.py:416
  31.1 3.2 %back_partial.1 = (f32[128,1536]{1,0:T(8,128)S(1)}, bf16[128,1536]{1,0:T(8,128)(2,1)S(1)}, bf16[64,3072]{1,0:T(8,128)(2,1)S(1)}) custom-call(bf16[32,3072]{1,0:T(8,128)(2,1)S(1)} %get-tuple-element.49.refs_0_, bf16[32,3072]{1,0:T(8,128)(2,1)S(1)} %get-tuple-element.50.refs_1_, bf16[32,3072]{1,0:T(8,128)(2,1)S(1)} %collective-permute-done.14.refs_2_.refs_3_, ...), custom_call_target="tpu_custom_call" | custom-call | tf_op jit(solution)/shard_map/back_partial/pallas_call | solution.py:55
  34.3 1.3 %collective-permute-start.16 = (bf16[128,1536]{1,0:T(8,128)(2,1)S(1)}, bf16[128,1536]{1,0:T(8,128)(2,1)S(1)}, u32[]{:S(2)}, u32[]{:S(2)}) collective-permute-start(bf16[128,1536]{1,0:T(8,128)(2,1)S(1)} %get-tuple-element.52), channel_id=1, source_target_pairs={{0,4},{4,0},{1,5},{5,1},{2,6},{6,2},{3,7},{7,3},{8,12},{12,8},{9,1... | collective-permute-start | bytes 1179656 | tf_op jit(solution)/shard_map/ppermute | solution.py:416
  35.7 1.2 %collective-permute-start.24 = (bf16[64,3072]{1,0:T(8,128)(2,1)S(1)}, bf16[64,3072]{1,0:T(8,128)(2,1)S(1)}, u32[]{:S(2)}, u32[]{:S(2)}) collective-permute-start(bf16[64,3072]{1,0:T(8,128)(2,1)S(1)} %get-tuple-element.65.refs_2_), channel_id=1, source_target_pairs={{0,16},{8,24},{16,0},{24,8},{1,17},{9,25},{17,1},{25,9},{2,18},{10... | collective-permute-start | bytes 1179656 | tf_op jit(solution)/shard_map/ppermute | solution.py:416
  36.9 1.6 %block_out_partial.1 = (f32[64,3072]{1,0:T(8,128)S(1)}, bf16[32,3072]{1,0:T(8,128)(2,1)S(1)}, bf16[32,3072]{1,0:T(8,128)(2,1)S(1)}, f32[128,1536]{1,0:T(8,128)S(...) custom-call(f32[128,1536]{1,0:T(8,128)S(1)} %get-tuple-element.39.refs_0_, ...), custom_call_target="tpu_custom_call" | custom-call | tf_op jit(solution)/shard_map/block_out_partial/pallas_call | solution.py:55
  39.1 0.9 %collective-permute-done.6.refs_2_ = bf16[32,3072]{1,0:T(8,128)(2,1)S(1)} collective-permute-done((bf16[32,3072]{1,0:T(8,128)(2,1)S(1)}, bf16[32,3072]{1,0:T(8,128)(2,1)S(1)}, u32[]{:S(2)}, u32[]{:S(2)}) %collective-permute-start.6) | collective-permute-done | bytes 196640 | tf_op jit(solution)/shard_map/ppermute | solution.py:419
  40.5 3.1 %collective-permute-start.10 = (bf16[16,3072]{1,0:T(8,128)(2,1)S(1)}, bf16[16,3072]{1,0:T(8,128)(2,1)S(1)}, u32[]{:S(2)}, u32[]{:S(2)}) collective-permute-start(bf16[16,3072]{1,0:T(8,128)(2,1)S(1)} %get-tuple-element.47), channel_id=1, source_target_pairs={{0,3},{1,0},{2,1},{3,2},{4,7},{5,4},{6,5},{7,6},{8,11},{9,8},{10,9... | collective-permute-start | bytes 294920 | tf_op jit(solution)/shard_map/ppermute | solution.py:416
  43.5 1.0 %collective-permute-start.9 = (bf16[16,3072]{1,0:T(8,128)(2,1)S(1)}, bf16[16,3072]{1,0:T(8,128)(2,1)S(1)}, u32[]{:S(2)}, u32[]{:S(2)}) collective-permute-start(bf16[16,3072]{1,0:T(8,128)(2,1)S(1)} %get-tuple-element.46), channel_id=1, source_target_pairs={{0,2},{1,3},{2,0},{3,1},{4,6},{5,7},{6,4},{7,5},{8,10},{9,11},{10,... | collective-permute-start | bytes 294920 | tf_op jit(solution)/shard_map/ppermute | solution.py:416
  44.6 0.8 %collective-permute-done.16.refs_1_ = bf16[128,1536]{1,0:T(8,128)(2,1)S(1)} collective-permute-done((bf16[128,1536]{1,0:T(8,128)(2,1)S(1)}, bf16[128,1536]{1,0:T(8,128)(2,1)S(1)}, u32[]{:S(2)}, u32[]{:S(2)}) %collective-permute-start.16) | collective-permute-done | bytes 393248 | tf_op jit(solution)/shard_map/ppermute | solution.py:416
  45.3 3.1 %grad_in_partial.1 = (f32[64,3072]{1,0:T(8,128)S(1)}, bf16[64,3072]{1,0:T(8,128)(2,1)S(1)}, bf16[128,768]{1,0:T(8,128)(2,1)S(1)}, bf16[256,768]{1,0:T(8,128)(2,1)S(1)}) custom-call(f32[128,1536]{1,0:T(8,128)S(1)} %get-tuple-element.51.refs_0_, bf16[128,1536]{1,0:T(8,128)(2,1)S(1)} %collective-permute-done.16.refs_1_, ...), custom_call_target="tpu_custom_call" | custom-call | tf_op jit(solution)/shard_map/grad_in_partial/pallas_call | solution.py:55
  48.5 0.6 collective-permute-done.24.refs_5_
  49.1 1.5 %collective-permute-start.23 = (bf16[256,768]{1,0:T(8,128)(2,1)S(1)}, bf16[256,768]{1,0:T(8,128)(2,1)S(1)}, u32[]{:S(2)}, u32[]{:S(2)}) collective-permute-start(bf16[256,768]{1,0:T(8,128)(2,1)S(1)} %get-tuple-element.63), channel_id=1, source_target_pairs={{0,16},{8,24},{16,0},{24,8},{1,17},{9,25},{17,1},{25,9},{2,18},{10... | collective-permute-start | bytes 1179656 | tf_op jit(solution)/shard_map/ppermute | solution.py:416
  50.6 3.1 %collective-permute-done.9 = bf16[16,3072]{1,0:T(8,128)(2,1)S(1)} collective-permute-done((bf16[16,3072]{1,0:T(8,128)(2,1)S(1)}, bf16[16,3072]{1,0:T(8,128)(2,1)S(1)}, u32[]{:S(2)}, u32[]{:S(2)}) %collective-permute-start.9) | collective-permute-done | bytes 98336 | tf_op jit(solution)/shard_map/ppermute | solution.py:416
  54.6 0.9 %collective-permute-start.19 = (bf16[16,3072]{1,0:T(8,128)(2,1)S(1)}, bf16[16,3072]{1,0:T(8,128)(2,1)S(1)}, u32[]{:S(2)}, u32[]{:S(2)}) collective-permute-start(bf16[16,3072]{1,0:T(8,128)(2,1)S(1)} %get-tuple-element.59), channel_id=1, source_target_pairs={{0,2},{1,3},{2,0},{3,1},{4,6},{5,7},{6,4},{7,5},{8,10},{9,11},{10,... | collective-permute-start | bytes 294920 | tf_op jit(solution)/shard_map/ppermute | solution.py:416
  55.5 1.6 %collective-permute-start.18 = (bf16[16,3072]{1,0:T(8,128)(2,1)S(1)}, bf16[16,3072]{1,0:T(8,128)(2,1)S(1)}, u32[]{:S(2)}, u32[]{:S(2)}) collective-permute-start(bf16[16,3072]{1,0:T(8,128)(2,1)S(1)} %get-tuple-element.58), channel_id=1, source_target_pairs={{0,1},{1,2},{2,3},{3,0},{4,5},{5,6},{6,7},{7,4},{8,9},{9,10},{10,1... | collective-permute-start | bytes 294920 | tf_op jit(solution)/shard_map/ppermute | solution.py:416
  57.2 3.5 %collective-permute-done.23.refs_5_.refs_1_ = bf16[256,768]{1,0:T(8,128)(2,1)S(1)} collective-permute-done((bf16[256,768]{1,0:T(8,128)(2,1)S(1)}, bf16[256,768]{1,0:T(8,128)(2,1)S(1)}, u32[]{:S(2)}, u32[]{:S(2)}) %collective-permute-start.23) | collective-permute-done | bytes 393248 | tf_op jit(solution)/shard_map/ppermute | solution.py:416
  60.6 2.7 %grad_w_in.1 = bf16[3072,768]{1,0:T(8,128)(2,1)} custom-call(bf16[64,3072]{1,0:T(8,128)(2,1)S(1)} %get-tuple-element.61.refs_0_, bf16[64,3072]{1,0:T(8,128)(2,1)S(1)} %collective-permute-done.4.refs_1_, bf16[64,3072]{1,0:T(8,128)(2,1)S(1)} %collective-permute-done.21.refs_2_, bf16[64,3072]{1,0:T(8,128)(2,1)S(1)} %collective-permute-done.22.refs_3_, ...), custom_call_target="tpu_custom_call" | custom-call | tf_op jit(solution)/shard_map/grad_w_in/pallas_call | solution.py:55
  63.4 2.6 %grad_w_out.1 = bf16[768,3072]{1,0:T(8,128)(2,1)} custom-call(bf16[128,768]{1,0:T(8,128)(2,1)S(1)} %get-tuple-element.64.refs_0_, bf16[256,768]{1,0:T(8,128)(2,1)S(1)} %collective-permute-done.23.refs_5_.refs_1_, bf16[64,3072]{1,0:T(8,128)(2,1)S(1)} %get-tuple-element.65.refs_2_, bf16[32,3072]{1,0:T(8,128)(2,1)S(1)} %collective-permute-done.14.refs_2_.refs_3_, ...), custom_call_target="tpu_custom_call" | custom-call | tf_op jit(solution)/shard_map/grad_w_out/pallas_call | solution.py:55
  66.0 0.7 %add_convert_fusion = bf16[16,3072]{1,0:T(8,128)(2,1)} fusion(bf16[16,3072]{1,0:T(8,128)(2,1)S(1)} %collective-permute-done.20, bf16[16,3072]{1,0:T(8,128)(2,1)S(1)} %collective-permute-done.19, f32[16,3072]{1,0:T(8,128)S(1)} %get-tuple-element.57.refs_6_.refs_7_, bf16[16,3072]{1,0:T(8,128)(2,1)S(1)} %collective-permute-done.18), kind=kLoop, calls=%fused_computation | loop fusion | flops 344064 | bytes 589824 | tf_op jit(solution)/shard_map/convert_element_type | solution.py:479
  (38 shorter events, 3.1 us)
Async XLA Ops:
  1.6 5.1 %collective-permute-start = (bf16[8,3072]{1,0:T(8,128)(2,1)S(1)}, bf16[8,3072]{1,0:T(8,128)(2,1)S(1)}, u32[]{:S(2)}, u32[]{:S(2)}) collective-permute-start(bf16[8,3072]{1,0:T(8,128)(2,1)S(1)} %get-tuple-element.36), channel_id=1, source_target_pairs={{0,4},{4,0},{1,5},{5,1},{2,6},{6,2},{3,7},{7,3},{8,12},{12,8},{9,1... | collective-permute-start | bytes 147464 | tf_op jit(solution)/shard_map/ppermute | solution.py:416
  6.7 10.0 %collective-permute-start.1 = (bf16[16,3072]{1,0:T(8,128)(2,1)S(1)}, bf16[16,3072]{1,0:T(8,128)(2,1)S(1)}, u32[]{:S(2)}, u32[]{:S(2)}) collective-permute-start(bf16[16,3072]{1,0:T(8,128)(2,1)S(1)} %get-tuple-element.38.refs_2_), channel_id=1, source_target_pairs={{0,1},{1,2},{2,3},{3,0},{4,5},{5,6},{6,7},{7,4},{8,9},{9,10},{10,1... | collective-permute-start | bytes 294920 | tf_op jit(solution)/shard_map/ppermute | solution.py:416
  8.9 8.2 %collective-permute-start.2 = (bf16[16,3072]{1,0:T(8,128)(2,1)S(1)}, bf16[16,3072]{1,0:T(8,128)(2,1)S(1)}, u32[]{:S(2)}, u32[]{:S(2)}) collective-permute-start(bf16[16,3072]{1,0:T(8,128)(2,1)S(1)} %get-tuple-element.38.refs_2_), channel_id=1, source_target_pairs={{0,2},{1,3},{2,0},{3,1},{4,6},{5,7},{6,4},{7,5},{8,10},{9,11},{10,... | collective-permute-start | bytes 294920 | tf_op jit(solution)/shard_map/ppermute | solution.py:416
  11.5 5.7 %collective-permute-start.3 = (bf16[16,3072]{1,0:T(8,128)(2,1)S(1)}, bf16[16,3072]{1,0:T(8,128)(2,1)S(1)}, u32[]{:S(2)}, u32[]{:S(2)}) collective-permute-start(bf16[16,3072]{1,0:T(8,128)(2,1)S(1)} %get-tuple-element.38.refs_2_), channel_id=1, source_target_pairs={{0,3},{1,0},{2,1},{3,2},{4,7},{5,4},{6,5},{7,6},{8,11},{9,8},{10,9... | collective-permute-start | bytes 294920 | tf_op jit(solution)/shard_map/ppermute | solution.py:416
  17.3 4.9 %collective-permute-start.4 = (bf16[64,3072]{1,0:T(8,128)(2,1)S(1)}, bf16[64,3072]{1,0:T(8,128)(2,1)S(1)}, u32[]{:S(2)}, u32[]{:S(2)}) collective-permute-start(bf16[64,3072]{1,0:T(8,128)(2,1)S(1)} %order_tokens.1.refs_0_), channel_id=1, source_target_pairs={{0,8},{8,0},{16,24},{24,16},{1,9},{9,1},{17,25},{25,17},{2,10},{10... | collective-permute-start | bytes 1179656 | tf_op jit(solution)/shard_map/ppermute | solution.py:419
  17.3 11.6 %collective-permute-start.11 = (bf16[16,3072]{1,0:T(8,128)(2,1)S(1)}, bf16[16,3072]{1,0:T(8,128)(2,1)S(1)}, u32[]{:S(2)}, u32[]{:S(2)}) collective-permute-start(bf16[16,3072]{1,0:T(8,128)(2,1)S(1)} %get-tuple-element.48.refs_1_), channel_id=1, source_target_pairs={{0,1},{1,2},{2,3},{3,0},{4,5},{5,6},{6,7},{7,4},{8,9},{9,10},{10,1... | collective-permute-start | bytes 294920 | tf_op jit(solution)/shard_map/ppermute | solution.py:416
  19.7 9.3 %collective-permute-start.12 = (bf16[16,3072]{1,0:T(8,128)(2,1)S(1)}, bf16[16,3072]{1,0:T(8,128)(2,1)S(1)}, u32[]{:S(2)}, u32[]{:S(2)}) collective-permute-start(bf16[16,3072]{1,0:T(8,128)(2,1)S(1)} %get-tuple-element.48.refs_1_), channel_id=1, source_target_pairs={{0,2},{1,3},{2,0},{3,1},{4,6},{5,7},{6,4},{7,5},{8,10},{9,11},{10,... | collective-permute-start | bytes 294920 | tf_op jit(solution)/shard_map/ppermute | solution.py:416
  21.4 7.5 %collective-permute-start.13 = (bf16[16,3072]{1,0:T(8,128)(2,1)S(1)}, bf16[16,3072]{1,0:T(8,128)(2,1)S(1)}, u32[]{:S(2)}, u32[]{:S(2)}) collective-permute-start(bf16[16,3072]{1,0:T(8,128)(2,1)S(1)} %get-tuple-element.48.refs_1_), channel_id=1, source_target_pairs={{0,3},{1,0},{2,1},{3,2},{4,7},{5,4},{6,5},{7,6},{8,11},{9,8},{10,9... | collective-permute-start | bytes 294920 | tf_op jit(solution)/shard_map/ppermute | solution.py:416
  23.5 13.4 %collective-permute-start.5 = (bf16[128,1536]{1,0:T(8,128)(2,1)S(1)}, bf16[128,1536]{1,0:T(8,128)(2,1)S(1)}, u32[]{:S(2)}, u32[]{:S(2)}) collective-permute-start(bf16[128,1536]{1,0:T(8,128)(2,1)S(1)} %get-tuple-element.40.refs_2_), channel_id=1, source_target_pairs={{0,4},{4,0},{1,5},{5,1},{2,6},{6,2},{3,7},{7,3},{8,12},{12,8},{9,1... | collective-permute-start | bytes 1179656 | tf_op jit(solution)/shard_map/ppermute | solution.py:416
  29.0 2.1 %collective-permute-start.14 = (bf16[32,3072]{1,0:T(8,128)(2,1)S(1)}, bf16[32,3072]{1,0:T(8,128)(2,1)S(1)}, u32[]{:S(2)}, u32[]{:S(2)}) collective-permute-start(bf16[32,3072]{1,0:T(8,128)(2,1)S(1)} %get-tuple-element.49.refs_0_), channel_id=1, source_target_pairs={{0,8},{8,0},{16,24},{24,16},{1,9},{9,1},{17,25},{25,17},{2,10},{10... | collective-permute-start | bytes 589832 | tf_op jit(solution)/shard_map/ppermute | solution.py:419
  29.1 2.0 %collective-permute-start.15 = (bf16[32,3072]{1,0:T(8,128)(2,1)S(1)}, bf16[32,3072]{1,0:T(8,128)(2,1)S(1)}, u32[]{:S(2)}, u32[]{:S(2)}) collective-permute-start(bf16[32,3072]{1,0:T(8,128)(2,1)S(1)} %get-tuple-element.50.refs_1_), channel_id=1, source_target_pairs={{0,8},{8,0},{16,24},{24,16},{1,9},{9,1},{17,25},{25,17},{2,10},{10... | collective-permute-start | bytes 589832 | tf_op jit(solution)/shard_map/ppermute | solution.py:419
  29.6 15.0 %collective-permute-start.21 = (bf16[64,3072]{1,0:T(8,128)(2,1)S(1)}, bf16[64,3072]{1,0:T(8,128)(2,1)S(1)}, u32[]{:S(2)}, u32[]{:S(2)}) collective-permute-start(bf16[64,3072]{1,0:T(8,128)(2,1)S(1)} %get-tuple-element.61.refs_0_), channel_id=1, source_target_pairs={{0,16},{8,24},{16,0},{24,8},{1,17},{9,25},{17,1},{25,9},{2,18},{10... | collective-permute-start | bytes 1179656 | tf_op jit(solution)/shard_map/ppermute | solution.py:416
  34.3 11.0 %collective-permute-start.16 = (bf16[128,1536]{1,0:T(8,128)(2,1)S(1)}, bf16[128,1536]{1,0:T(8,128)(2,1)S(1)}, u32[]{:S(2)}, u32[]{:S(2)}) collective-permute-start(bf16[128,1536]{1,0:T(8,128)(2,1)S(1)} %get-tuple-element.52), channel_id=1, source_target_pairs={{0,4},{4,0},{1,5},{5,1},{2,6},{6,2},{3,7},{7,3},{8,12},{12,8},{9,1... | collective-permute-start | bytes 1179656 | tf_op jit(solution)/shard_map/ppermute | solution.py:416
  35.7 13.4 %collective-permute-start.24 = (bf16[64,3072]{1,0:T(8,128)(2,1)S(1)}, bf16[64,3072]{1,0:T(8,128)(2,1)S(1)}, u32[]{:S(2)}, u32[]{:S(2)}) collective-permute-start(bf16[64,3072]{1,0:T(8,128)(2,1)S(1)} %get-tuple-element.65.refs_2_), channel_id=1, source_target_pairs={{0,16},{8,24},{16,0},{24,8},{1,17},{9,25},{17,1},{25,9},{2,18},{10... | collective-permute-start | bytes 1179656 | tf_op jit(solution)/shard_map/ppermute | solution.py:416
  38.5 1.5 %collective-permute-start.6 = (bf16[32,3072]{1,0:T(8,128)(2,1)S(1)}, bf16[32,3072]{1,0:T(8,128)(2,1)S(1)}, u32[]{:S(2)}, u32[]{:S(2)}) collective-permute-start(bf16[32,3072]{1,0:T(8,128)(2,1)S(1)} %get-tuple-element.42), channel_id=1, source_target_pairs={{0,8},{8,0},{16,24},{24,16},{1,9},{9,1},{17,25},{25,17},{2,10},{10... | collective-permute-start | bytes 589832 | tf_op jit(solution)/shard_map/ppermute | solution.py:419
  38.6 1.7 %collective-permute-start.7 = (bf16[32,3072]{1,0:T(8,128)(2,1)S(1)}, bf16[32,3072]{1,0:T(8,128)(2,1)S(1)}, u32[]{:S(2)}, u32[]{:S(2)}) collective-permute-start(bf16[32,3072]{1,0:T(8,128)(2,1)S(1)} %get-tuple-element.43), channel_id=1, source_target_pairs={{0,8},{8,0},{16,24},{24,16},{1,9},{9,1},{17,25},{25,17},{2,10},{10... | collective-permute-start | bytes 589832 | tf_op jit(solution)/shard_map/ppermute | solution.py:419
  40.5 8.7 %collective-permute-start.10 = (bf16[16,3072]{1,0:T(8,128)(2,1)S(1)}, bf16[16,3072]{1,0:T(8,128)(2,1)S(1)}, u32[]{:S(2)}, u32[]{:S(2)}) collective-permute-start(bf16[16,3072]{1,0:T(8,128)(2,1)S(1)} %get-tuple-element.47), channel_id=1, source_target_pairs={{0,3},{1,0},{2,1},{3,2},{4,7},{5,4},{6,5},{7,6},{8,11},{9,8},{10,9... | collective-permute-start | bytes 294920 | tf_op jit(solution)/shard_map/ppermute | solution.py:416
  43.5 10.3 %collective-permute-start.9 = (bf16[16,3072]{1,0:T(8,128)(2,1)S(1)}, bf16[16,3072]{1,0:T(8,128)(2,1)S(1)}, u32[]{:S(2)}, u32[]{:S(2)}) collective-permute-start(bf16[16,3072]{1,0:T(8,128)(2,1)S(1)} %get-tuple-element.46), channel_id=1, source_target_pairs={{0,2},{1,3},{2,0},{3,1},{4,6},{5,7},{6,4},{7,5},{8,10},{9,11},{10,... | collective-permute-start | bytes 294920 | tf_op jit(solution)/shard_map/ppermute | solution.py:416
  44.6 9.2 %collective-permute-start.8 = (bf16[16,3072]{1,0:T(8,128)(2,1)S(1)}, bf16[16,3072]{1,0:T(8,128)(2,1)S(1)}, u32[]{:S(2)}, u32[]{:S(2)}) collective-permute-start(bf16[16,3072]{1,0:T(8,128)(2,1)S(1)} %get-tuple-element.45), channel_id=1, source_target_pairs={{0,1},{1,2},{2,3},{3,0},{4,5},{5,6},{6,7},{7,4},{8,9},{9,10},{10,1... | collective-permute-start | bytes 294920 | tf_op jit(solution)/shard_map/ppermute | solution.py:416
  45.3 10.2 %collective-permute-start.22 = (bf16[64,3072]{1,0:T(8,128)(2,1)S(1)}, bf16[64,3072]{1,0:T(8,128)(2,1)S(1)}, u32[]{:S(2)}, u32[]{:S(2)}) collective-permute-start(bf16[64,3072]{1,0:T(8,128)(2,1)S(1)} %collective-permute-done.21.refs_2_), channel_id=1, source_target_pairs={{0,8},{8,0},{16,24},{24,16},{1,9},{9,1},{17,25},{25,17},{2,10},{10... | collective-permute-start | bytes 1179656 | tf_op jit(solution)/shard_map/ppermute | solution.py:419
  49.1 4.8 %collective-permute-start.17 = (bf16[64,3072]{1,0:T(8,128)(2,1)S(1)}, bf16[64,3072]{1,0:T(8,128)(2,1)S(1)}, u32[]{:S(2)}, u32[]{:S(2)}) collective-permute-start(bf16[64,3072]{1,0:T(8,128)(2,1)S(1)} %get-tuple-element.56), channel_id=1, source_target_pairs={{0,8},{8,0},{16,24},{24,16},{1,9},{9,1},{17,25},{25,17},{2,10},{10... | collective-permute-start | bytes 1179656 | tf_op jit(solution)/shard_map/ppermute | solution.py:419
  49.1 11.5 %collective-permute-start.23 = (bf16[256,768]{1,0:T(8,128)(2,1)S(1)}, bf16[256,768]{1,0:T(8,128)(2,1)S(1)}, u32[]{:S(2)}, u32[]{:S(2)}) collective-permute-start(bf16[256,768]{1,0:T(8,128)(2,1)S(1)} %get-tuple-element.63), channel_id=1, source_target_pairs={{0,16},{8,24},{16,0},{24,8},{1,17},{9,25},{17,1},{25,9},{2,18},{10... | collective-permute-start | bytes 1179656 | tf_op jit(solution)/shard_map/ppermute | solution.py:416
  53.8 9.6 %collective-permute-start.25 = (bf16[64,3072]{1,0:T(8,128)(2,1)S(1)}, bf16[64,3072]{1,0:T(8,128)(2,1)S(1)}, u32[]{:S(2)}, u32[]{:S(2)}) collective-permute-start(bf16[64,3072]{1,0:T(8,128)(2,1)S(1)} %collective-permute-done.24.refs_5_), channel_id=1, source_target_pairs={{0,8},{8,0},{16,24},{24,16},{1,9},{9,1},{17,25},{25,17},{2,10},{10... | collective-permute-start | bytes 1179656 | tf_op jit(solution)/shard_map/ppermute | solution.py:419
  53.8 12.9 %copy-start = (bf16[16,3072]{1,0:T(8,128)(2,1)}, bf16[16,3072]{1,0:T(8,128)(2,1)S(1)}, u32[]{:S(2)}) copy-start(bf16[16,3072]{1,0:T(8,128)(2,1)S(1)} %add_convert_fusion.1.refs_3_) | copy-start | bytes 294916
  54.0 12.0 %collective-permute-start.20 = (bf16[16,3072]{1,0:T(8,128)(2,1)S(1)}, bf16[16,3072]{1,0:T(8,128)(2,1)S(1)}, u32[]{:S(2)}, u32[]{:S(2)}) collective-permute-start(bf16[16,3072]{1,0:T(8,128)(2,1)S(1)} %get-tuple-element.60), channel_id=1, source_target_pairs={{0,3},{1,0},{2,1},{3,2},{4,7},{5,4},{6,5},{7,6},{8,11},{9,8},{10,9... | collective-permute-start | bytes 294920 | tf_op jit(solution)/shard_map/ppermute | solution.py:416
  54.6 11.4 %collective-permute-start.19 = (bf16[16,3072]{1,0:T(8,128)(2,1)S(1)}, bf16[16,3072]{1,0:T(8,128)(2,1)S(1)}, u32[]{:S(2)}, u32[]{:S(2)}) collective-permute-start(bf16[16,3072]{1,0:T(8,128)(2,1)S(1)} %get-tuple-element.59), channel_id=1, source_target_pairs={{0,2},{1,3},{2,0},{3,1},{4,6},{5,7},{6,4},{7,5},{8,10},{9,11},{10,... | collective-permute-start | bytes 294920 | tf_op jit(solution)/shard_map/ppermute | solution.py:416
  55.5 10.5 %collective-permute-start.18 = (bf16[16,3072]{1,0:T(8,128)(2,1)S(1)}, bf16[16,3072]{1,0:T(8,128)(2,1)S(1)}, u32[]{:S(2)}, u32[]{:S(2)}) collective-permute-start(bf16[16,3072]{1,0:T(8,128)(2,1)S(1)} %get-tuple-element.58), channel_id=1, source_target_pairs={{0,1},{1,2},{2,3},{3,0},{4,5},{5,6},{6,7},{7,4},{8,9},{9,10},{10,1... | collective-permute-start | bytes 294920 | tf_op jit(solution)/shard_map/ppermute | solution.py:416

commit v5 on v4

--- a/solution.py
+++ b/solution.py
@@ -8,7 +8,7 @@
 from jax.sharding import PartitionSpec as P
 
 CORES = 2
-CFG = {'cot_early': 0, 'tok_pieces': 1, 'cot_pieces': 2, 'out_pieces': 2, 'in_pieces': 1, 'load2': 'pre', 'order2': 'load2', 'hop_cot': 0, 'hop_c': 0, 'hop_d': 0, 'back_pre': 0, 'tok_y': 'preact', 'cot_y': 'back', 'k3_back': 0, 'k3_toky': 0, 'se_d': 0, 'k4': ['E'], 'sf': ['bo'], 'wg_bo': 0, 'hid': 'merged'}
+CFG = {'cot_early': 0, 'tok_pieces': 1, 'cot_pieces': 2, 'out_pieces': 2, 'in_pieces': 1, 'load2': 'pre', 'order2': 'load2', 'hop_cot': 0, 'hop_c': 0, 'hop_d': 0, 'back_pre': 0, 'tok_y': 'preact', 'cot_y': 'back', 'k3_back': 1, 'k3_toky': 0, 'se_d': 0, 'k4': ['E', 'ty'], 'sf': ['bo', 'cy'], 'wg_bo': 0, 'hid': 'sep', 'wgo': 'SF', 'half': 0, 'sfs': []}
 MIB = 1024 * 1024
 NT = (((1,), (1,)), ((), ()))
 NN = (((1,), (0,)), ((), ()))
@@ -21,6 +21,10 @@
 
 def mm(a, b, dims):
     return lax.dot_general(a, b, dims, preferred_element_type=jnp.float32)
+
+
+def mm_streamed(rows, weights):
+    return mm(weights, rows, NT).T
 
 
 def tile_of(size, most):
@@ -59,32 +63,31 @@
     return jax.ShapeDtypeStruct(tuple(dims), dtype)
 
 
-def load_kernel(dp, size, pieces, columns, place, w, out, sems):
-    blocks = dp // CORES
+def load_kernel(dp, size, pieces, columns, which, place, w, out, sems):
     rows = (w.shape[0] if columns else size) // pieces
     copies = []
-    for b in range(blocks):
+    for i, b in enumerate(which):
         for p in range(pieces):
             if columns:
                 cut = pl.ds(p * rows, rows)
                 source = w.at[cut, pl.ds(pl.multiple_of(lax.rem(place[0] + CORES * b, dp) * size, 128), size)]
-                to = out.at[cut, pl.ds(b * size, size)]
+                to = out.at[cut, pl.ds(i * size, size)]
             else:
                 at = pl.multiple_of(lax.rem(place[0] + CORES * b, dp) * size + p * rows, 16)
                 source = w.at[pl.ds(at, rows)]
-                to = out.at[pl.ds(b * size + p * rows, rows)]
-            copies.append(pltpu.make_async_copy(source, to, sems.at[b * pieces + p]))
+                to = out.at[pl.ds(i * size + p * rows, rows)]
+            copies.append(pltpu.make_async_copy(source, to, sems.at[i * pieces + p]))
     for copy in copies:
         copy.start()
     for copy in copies:
         copy.wait()
 
 
-def load(place, w, dp, size, columns, name, after):
-    blocks, pieces = dp // CORES, 8
+def load(place, w, dp, size, columns, which, name, after):
+    blocks, pieces = len(which), 4
     units = blocks * size
     return call(
-        functools.partial(load_kernel, dp, size, pieces, columns),
+        functools.partial(load_kernel, dp, size, pieces, columns, which),
         [SMEM, HBM],
         VMEM,
         pltpu.VMEM((w.shape[0], units) if columns else (units, w.shape[1]), jnp.bfloat16),
@@ -126,7 +129,7 @@
     cot_out[...] = cot[...]
 
 
-def stack(parts, cot):
+def stack(parts, cot, after):
     rows, width = parts[0].shape
     return call(
         stack_kernel,
@@ -134,6 +137,7 @@
         [VMEM] * 2,
         [shape((rows * len(parts), width)), shape(cot.shape)],
         "stack_rows",
+        after=after,
     )(*parts, cot)
 
 
@@ -192,8 +196,8 @@
     )(col_place, *parts)
 
 
-def first_kernel(dims, tile, mine, count, *refs):
-    groups, w, refs = refs[:count], refs[count], refs[count + 1 :]
+def first_kernel(dims, tile, mine, count, weights, *refs):
+    groups, ws, refs = refs[:count], refs[count : count + weights], refs[count + weights :]
     if len(refs) == 6:
         refs[4][...] = refs[0][...]
         refs = refs[1:4] + refs[5:]
@@ -205,28 +209,42 @@
         if i < mine:
             own_out[cut] = group[...]
         at += group.shape[0]
+    size = total.shape[1] // weights
     for at in range(0, total.shape[1], tile):
         cut = slice(at, at + tile)
-        part = mm(rows[...], w[:, cut] if dims is NN else w[cut, :], dims)
+        b, start = divmod(at, size)
+        units = slice(start, start + tile)
+        if dims is NN:
+            part = mm(rows[...], ws[b][:, units], NN)
+        else:
+            part = mm_streamed(rows[...], ws[b][units, :])
         total[:, cut] = part
         sent[:, cut] = part.astype(jnp.bfloat16)
 
 
-def first(own, other, w, dims, name, after=(), passing=None):
+def first(own, other, ws, dims, name, after=(), passing=None):
     half, width = len(own) * own[0].shape[0], own[0].shape[1]
     n = 2 * half
-    units = w.shape[1 if dims is NN else 0]
+    each = ws[0].shape[1 if dims is NN else 0]
+    units = len(ws) * each
     extra = [] if passing is None else [passing]
     return call(
-        functools.partial(first_kernel, dims, tile_of(units, 256), len(own), len(own) + len(other)),
-        [VMEM] * (len(own) + len(other) + 1 + len(extra)),
+        functools.partial(
+            first_kernel,
+            dims,
+            tile_of(each, 256 if dims is NN else 512),
+            len(own),
+            len(own) + len(other),
+            len(ws),
+        ),
+        [VMEM] * (len(own) + len(other) + len(ws) + len(extra)),
         [VMEM] * (3 + len(extra)),
         [shape((n, units), jnp.float32), shape((n, units)), shape((half, width))]
         + [shape(x.shape) for x in extra],
         name,
         scratch=[pltpu.VMEM((n, width), jnp.bfloat16)],
         after=after,
-    )(*own, *other, w, *extra)
+    )(*own, *other, *ws, *extra)
 
 
 def gelu_parts(preact):
@@ -235,12 +253,18 @@
     return (preact * cdf, slopes)
 
 
-def second_product(dims, vals, w, keep, sends):
+def second_product(dims, vals, ws, keep, sends):
     half, width = keep.shape
     tile = tile_of(width, 512)
     for at in range(0, width, tile):
         cut = slice(at, at + tile)
-        part = mm(vals[...], w[:, cut] if dims is NN else w[cut, :], dims)
+        if dims is NN:
+            size = vals.shape[1] // len(ws)
+            part = mm(vals[:, :size], ws[0][:, cut], NN)
+            for b in range(1, len(ws)):
+                part += mm(vals[:, b * size : (b + 1) * size], ws[b][:, cut], NN)
+        else:
+            part = mm_streamed(vals[...], ws[0][cut, :])
         keep[:, cut] = part[:half]
         for i, send in enumerate(sends):
             rows = send.shape[0]
@@ -254,9 +278,10 @@
     return whole
 
 
-def forward_kernel(blocks, shares, pieces, passing, *refs):
-    total, parts, w = refs[0], refs[1 : 1 + shares], refs[1 + shares]
-    passed, refs = refs[2 + shares : 2 + shares + passing], refs[2 + shares + passing :]
+def forward_kernel(blocks, shares, pieces, passing, weights, *refs):
+    total, parts, refs = refs[0], refs[1 : 1 + shares], refs[1 + shares :]
+    ws, refs = refs[:weights], refs[weights:]
+    passed, refs = refs[:passing], refs[passing:]
     keep, *sends = refs[: 1 + pieces]
     slopes, *hidden, vals = refs[1 + pieces :]
     hidden, outs = hidden[:blocks], hidden[blocks:]
@@ -270,10 +295,10 @@
         vals[:, cut] = value
         hidden[b][...] = value
         slopes[:, cut] = slope
-    second_product(NN, vals, w, keep, sends)
-
-
-def backward_kernel(blocks, shares, pieces, passing, *refs):
+    second_product(NN, vals, ws, keep, sends)
+
+
+def backward_kernel(blocks, shares, pieces, passing, weights, *refs):
     total, parts, slopes, w = refs[0], refs[1 : 1 + shares], refs[1 + shares], refs[2 + shares]
     hidden, refs = refs[3 + shares : 3 + shares + passing], refs[3 + shares + passing :]
     keep, *sends = refs[: 1 + pieces]
@@ -286,15 +311,15 @@
         pre[b][:n] = value
         if b > 0 and passing:
             pre[b][n:] = hidden[b - 1][...]
-    second_product(NT, vals, w, keep, sends)
-
-
-def second(total, parts, slopes, w, size, name, passing, after, pieces):
+    second_product(NT, vals, [w], keep, sends)
+
+
+def second(total, parts, slopes, ws, size, name, passing, after, pieces):
     n, units = total.shape
     half = n // 2
     blocks = units // size
     forward = slopes is None
-    width = w.shape[1] if forward else w.shape[0]
+    width = ws[0].shape[1] if forward else ws[0].shape[0]
     out_shape = [shape((half, width), jnp.float32)] + [shape((half // pieces, width))] * pieces
     if forward:
         out_shape.append(shape((n, units), jnp.float32))
@@ -305,42 +330,36 @@
     extra = [] if forward else [slopes]
     kernel = forward_kernel if forward else backward_kernel
     return call(
-        functools.partial(kernel, blocks, len(parts), pieces, len(passing)),
-        [VMEM] * (2 + len(parts) + len(extra) + len(passing)),
+        functools.partial(kernel, blocks, len(parts), pieces, len(passing), len(ws)),
+        [VMEM] * (1 + len(parts) + len(extra) + len(ws) + len(passing)),
         [VMEM] * len(out_shape),
         out_shape,
         name,
         scratch=[pltpu.VMEM((n, units), jnp.bfloat16)],
         after=after,
-    )(total, *parts, *extra, w, *passing)
-
-
-def cores_kernel(pieces, place, keep, *refs):
-    parts, own = refs[:pieces], refs[pieces]
-    *sent, held = refs[pieces + 1 :]
-    rows = own.shape[0]
+    )(total, *parts, *extra, *ws, *passing)
+
+
+def cores_kernel(pieces, count, steps, place, keep, *refs):
+    parts, outs, held = refs[:pieces], refs[pieces:-1], refs[-1]
+    rows = keep.shape[0] // count
     at = 0
     for part in parts:
         cut = slice(at, at + part.shape[0])
         held[cut] = keep[cut] + part[...].astype(jnp.float32)
         at += part.shape[0]
-    count = 1 + len(sent)
-    me = place[0]
-    for k in range(count):
-        at = pl.ds(pl.multiple_of(lax.rem(me + k, count) * rows, 16), rows)
-        if k == 0:
-            own[...] = held[at]
-        else:
-            sent[k - 1][...] = held[at].astype(jnp.bfloat16)
-
-
-def cores_sum(col_place, keep, parts, count, name, after=()):
+    for k, out in zip(steps, outs):
+        at = pl.ds(pl.multiple_of(lax.rem(place[0] + k, count) * rows, 16), rows)
+        out[...] = held[at].astype(out.dtype)
+
+
+def cores_sum(col_place, keep, parts, count, steps, name, after=()):
     rows, width = keep.shape[0] // count, keep.shape[1]
     return call(
-        functools.partial(cores_kernel, len(parts)),
+        functools.partial(cores_kernel, len(parts), count, steps),
         [SMEM, VMEM] + [VMEM] * len(parts),
-        [VMEM] * count,
-        [shape((rows, width), jnp.float32)] + [shape((rows, width))] * (count - 1),
+        [VMEM] * len(steps),
+        [shape((rows, width), jnp.bfloat16 if k else jnp.float32) for k in steps],
         name,
         scratch=[pltpu.VMEM(keep.shape, jnp.float32)],
         after=after,
@@ -431,20 +450,25 @@
         return [across_cores(mark(parts))] if on else []
 
     cot_mine, own, *other_widths = split(row_place, in_hbm(tokens), in_hbm(grad_out), row)
+    w_begin = None
+    if C["half"]:
+        w_begin = load(place, w_out[0], dp, size, False, range(1), "load_half", [own])
     stacked, cot_mine2 = stack(
         [own] + [shifted(part, "row", step + 1) for step, part in enumerate(other_widths)],
         cot_mine,
+        [w_begin] if C["half"] else [],
     )
     src = cot_mine if C["cot_early"] else cot_mine2
     stacks = [stacked] + [shifted(stacked, "col", step) for step in range(1, col)]
     cots = [src] + [shifted(src, "col", step) for step in range(1, col)]
-    w_first = load(place, w_in[:, 0, :], dp, size, True, "load_first", [stacked])
+    w_first = load(place, w_in[:, 0, :], dp, size, True, range(blocks), "load_first", [stacked])
     tok = tokens_in_order(row_place, col_place, stacks, row, [w_first], C["tok_pieces"])
     tok_other = [across_cores(x) for x in tok]
-    pre_total, pre_sent, tok_later = first(tok, tok_other, w_first, NN, "preact_partial")
+    pre_total, pre_sent, tok_later = first(tok, tok_other, [w_first], NN, "preact_partial")
     pre_parts = across_rows(pre_sent)
-    w_second = load(place, w_out[0], dp, size, False, "load_second", {"first": [w_first], "tok": [tok[0]], "pre": [pre_sent]}[C["load2"]])
-    cot = in_order(col_place, cots, {"first": [w_first], "tok": [tok[0]], "pre": [pre_sent], "load2": [w_second]}[C["order2"]], C["cot_pieces"])
+    w_rest = load(place, w_out[0], dp, size, False, range(C["half"], blocks), "load_half" if C["half"] else "load_second", {"first": [w_first], "tok": [tok[0]], "pre": [pre_sent]}[C["load2"]])
+    w_second = ([w_begin] if C["half"] else []) + [w_rest]
+    cot = in_order(col_place, cots, {"first": [w_first], "tok": [tok[0]], "pre": [pre_sent], "load2": [w_rest]}[C["order2"]], C["cot_pieces"])
     cot_other = [across_cores(x) for x in cot]
     hops = hop(cot_other, C["hop_cot"])
     back_total, back_sent, cot_later, *passed = first(cot, cot_other, w_second, NT, "back_partial", [pre_sent] * C["back_pre"] + hops, tok_later if C["tok_y"] == "back" else None)
@@ -469,7 +493,7 @@
     if C["cot_y"] == "K3":
         cot_there = [shifted(passed[-1], "dp", CORES * b) for b in range(1, blocks)]
     out_own, *out_sent = cores_sum(
-        col_place, out_keep, [across_cores(x) for x in out_sends], col, "block_out_cores",
+        col_place, out_keep, [across_cores(x) for x in out_sends], col, range(col), "block_out_cores",
         back_parts if C["se_d"] else []
     )
 
@@ -485,14 +509,19 @@
     after = [full_ties[t] for t in C["k4"]] + hop(back_parts, C["hop_d"])
     merged = C["hid"] == "merged"
     in_keep, *rest = second(
-        back_total, back_parts, slopes, w_first, size, "grad_in_partial", hidden[1:] if merged else (), after, C["in_pieces"]
+        back_total, back_parts, slopes, [w_first], size, "grad_in_partial", hidden[1:] if merged else (), after, C["in_pieces"]
     )
     in_sends, both = rest[: C["in_pieces"]], rest[C["in_pieces"] :]
-    in_own, *in_sent = cores_sum(
-        col_place, in_keep, [across_cores(x) for x in in_sends], col, "grad_in_cores",
-        [full_ties[t] for t in C["sf"]]
-    )
-    grad_in = col_total(in_own, in_sent)
+    in_parts = [across_cores(x) for x in in_sends]
+    ahead = [k for k in C["sfs"] if k < col]
+    late = [k for k in range(col) if k not in ahead]
+    sums = {}
+    if ahead:
+        sums.update(zip(ahead, cores_sum(col_place, in_keep, in_parts, col, ahead, "grad_in_ahead")))
+    ties = [full_ties[t] for t in C["sf"]]
+    sums.update(zip(late, cores_sum(col_place, in_keep, in_parts, col, late, "grad_in_cores", ties)))
+    in_own = sums[0]
+    grad_in = col_total(in_own, [sums[k] for k in range(1, col)])
 
     def full(groups):
         return [(x, (0, x.shape[0])) for x in groups]
@@ -505,7 +534,8 @@
     else:
         hid_mine = full(hidden[:1] + [shifted(hidden[b], "dp", CORES * b) for b in range(1, blocks)])
     after = [in_own] + [block_out] * C["wg_bo"]
-    grad_out_w = weight_grad(hid_mine, full(cot_all), True, "grad_w_out", after)
+    out_after = {"none": [], "E": [out_own], "K4": [in_keep], "SF": after}[C["wgo"]]
+    grad_out_w = weight_grad(hid_mine, full(cot_all), True, "grad_w_out", out_after)
     grad_in_w = weight_grad(full(tok_all), pre_mine, False, "grad_w_in", after)
     return block_out, grad_in, grad_in_w[:, None, :], grad_out_w[None]
 

time: 66.9 us -> 64.4 us (0.963)
  waiting for transfers between devices: 11.8 us -> 5.62 us
  starting transfers between devices: 29.5 us -> 34.2 us
  Pallas kernels: 23.8 us -> 22.9 us
    ppermute x18 -> x19, waiting for transfers between devices: 10.5 us -> 4.22 us  [shifted(): lax.ppermute(x, axis, [(i, (i + step) % count) for i in range(count)])]
    ppermute x18 -> x19, starting transfers between devices: 28.3 us -> 32.5 us  [shifted(): lax.ppermute(x, axis, [(i, (i + step) % count) for i in range(count)])]
    pallas_call x14, Pallas kernels: 23.8 us -> 22.9 us  [call(): return lambda *args: kernel_call(*args, *after)]
  transfers between devices with their start and end apart: 26 -> 27, of which waited for: 9 -> 9; matrix products, arithmetic and copies ran while one was open for 0% -> 0% of each run, Pallas kernels for 34% -> 34%
where the time goes in v5:
time: 64.4 us; the launch traced here: 64.3 us
  starting transfers between devices  34.2 us (53%)
  Pallas kernels  22.9 us (36%)
  waiting for transfers between devices  5.62 us (9%)
  between operations  0.84 us (1%)
  other arithmetic  0.73 us (1%)
    ppermute x19, starting transfers between devices, shifted(): lax.ppermute(x, axis, [(i, (i + step) % count) for i in range(count)])  32.5 us
    pallas_call x14, Pallas kernels, call(): return lambda *args: kernel_call(*args, *after)  22.9 us
    ppermute x19, waiting for transfers between devices, shifted(): lax.ppermute(x, axis, [(i, (i + step) % count) for i in range(count)])  4.22 us
    ppermute x8, starting transfers between devices, across_cores(): return lax.ppermute(x, 'dp', [(i, i ^ 1) for i in range(dp)])  1.72 us
    ppermute x8, waiting for transfers between devices, across_cores(): return lax.ppermute(x, 'dp', [(i, i ^ 1) for i in range(dp)])  1.4 us
  transfers between devices with their start and end apart: 27, of which 9 were waited for; matrix products, arithmetic and copies ran while one was open for 0% of the time, Pallas kernels for 34%

profile of v5, /device:TPU:0, one launch (start us, length us, event | category | flops | bytes accessed | tf_op | source)
XLA Modules:
  0.0 64.3 jit_solution(7603192881152759610)
XLA Ops:
  0.6 1.0 %split_width.1 = (bf16[16,3072]{1,0:T(8,128)(2,1)S(1)}, bf16[8,3072]{1,0:T(8,128)(2,1)S(1)}, bf16[8,3072]{1,0:T(8,128)(2,1)S(1)}) custom-call(s32[1]{0:T(128)} %bitcast.1.refs_0_, bf16[8,6144]{1,0:T(8,128)(2,1)} %refs_1_.1, bf16[16,3072]{1,0:T(8,128)(2,1)} %refs_2_.1), custom_call_target="tpu_custom_call" | custom-call | tf_op jit(solution)/shard_map/split_width/pallas_call | solution.py:59
  1.6 3.0 %collective-permute-start = (bf16[8,3072]{1,0:T(8,128)(2,1)S(1)}, bf16[8,3072]{1,0:T(8,128)(2,1)S(1)}, u32[]{:S(2)}, u32[]{:S(2)}) collective-permute-start(bf16[8,3072]{1,0:T(8,128)(2,1)S(1)} %get-tuple-element.36), channel_id=1, source_target_pairs={{0,4},{4,0},{1,5},{5,1},{2,6},{6,2},{3,7},{7,3},{8,12},{12,8},{9,1... | collective-permute-start | bytes 147464 | tf_op jit(solution)/shard_map/ppermute | solution.py:435
  4.6 2.1 %collective-permute-done.refs_1_ = bf16[8,3072]{1,0:T(8,128)(2,1)S(1)} collective-permute-done((bf16[8,3072]{1,0:T(8,128)(2,1)S(1)}, bf16[8,3072]{1,0:T(8,128)(2,1)S(1)}, u32[]{:S(2)}, u32[]{:S(2)}) %collective-permute-start) | collective-permute-done | bytes 49184 | tf_op jit(solution)/shard_map/ppermute | solution.py:435
  6.7 2.2 %collective-permute-start.1 = (bf16[16,3072]{1,0:T(8,128)(2,1)S(1)}, bf16[16,3072]{1,0:T(8,128)(2,1)S(1)}, u32[]{:S(2)}, u32[]{:S(2)}) collective-permute-start(bf16[16,3072]{1,0:T(8,128)(2,1)S(1)} %get-tuple-element.38.refs_2_), channel_id=1, source_target_pairs={{0,1},{1,2},{2,3},{3,0},{4,5},{5,6},{6,7},{7,4},{8,9},{9,10},{10,1... | collective-permute-start | bytes 294920 | tf_op jit(solution)/shard_map/ppermute | solution.py:435
  8.9 2.6 %collective-permute-start.2 = (bf16[16,3072]{1,0:T(8,128)(2,1)S(1)}, bf16[16,3072]{1,0:T(8,128)(2,1)S(1)}, u32[]{:S(2)}, u32[]{:S(2)}) collective-permute-start(bf16[16,3072]{1,0:T(8,128)(2,1)S(1)} %get-tuple-element.38.refs_2_), channel_id=1, source_target_pairs={{0,2},{1,3},{2,0},{3,1},{4,6},{5,7},{6,4},{7,5},{8,10},{9,11},{10,... | collective-permute-start | bytes 294920 | tf_op jit(solution)/shard_map/ppermute | solution.py:435
  11.5 1.3 %collective-permute-start.3 = (bf16[16,3072]{1,0:T(8,128)(2,1)S(1)}, bf16[16,3072]{1,0:T(8,128)(2,1)S(1)}, u32[]{:S(2)}, u32[]{:S(2)}) collective-permute-start(bf16[16,3072]{1,0:T(8,128)(2,1)S(1)} %get-tuple-element.38.refs_2_), channel_id=1, source_target_pairs={{0,3},{1,0},{2,1},{3,2},{4,7},{5,4},{6,5},{7,6},{8,11},{9,8},{10,9... | collective-permute-start | bytes 294920 | tf_op jit(solution)/shard_map/ppermute | solution.py:435
  12.8 3.8 %load_first.1.refs_6_.refs_2_.refs_3_ = bf16[3072,1536]{1,0:T(8,128)(2,1)S(1)} custom-call(s32[1]{0:T(128)} %bitcast.2.refs_0_, bf16[3072,3072]{1,0:T(8,128)(2,1)} %bitcast.7, bf16[16,3072]{1,0:T(8,128)(2,1)S(1)} %get-tuple-element.38.refs_2_), custom_call_target="tpu_custom_call" | custom-call | tf_op jit(solution)/shard_map/load_first/pallas_call | solution.py:59
  17.3 2.3 %collective-permute-start.6 = (bf16[16,3072]{1,0:T(8,128)(2,1)S(1)}, bf16[16,3072]{1,0:T(8,128)(2,1)S(1)}, u32[]{:S(2)}, u32[]{:S(2)}) collective-permute-start(bf16[16,3072]{1,0:T(8,128)(2,1)S(1)} %get-tuple-element.41.refs_1_), channel_id=1, source_target_pairs={{0,1},{1,2},{2,3},{3,0},{4,5},{5,6},{6,7},{7,4},{8,9},{9,10},{10,1... | collective-permute-start | bytes 294920 | tf_op jit(solution)/shard_map/ppermute | solution.py:435
  19.7 1.8 %collective-permute-start.7 = (bf16[16,3072]{1,0:T(8,128)(2,1)S(1)}, bf16[16,3072]{1,0:T(8,128)(2,1)S(1)}, u32[]{:S(2)}, u32[]{:S(2)}) collective-permute-start(bf16[16,3072]{1,0:T(8,128)(2,1)S(1)} %get-tuple-element.41.refs_1_), channel_id=1, source_target_pairs={{0,2},{1,3},{2,0},{3,1},{4,6},{5,7},{6,4},{7,5},{8,10},{9,11},{10,... | collective-permute-start | bytes 294920 | tf_op jit(solution)/shard_map/ppermute | solution.py:435
  21.4 0.7 %collective-permute-start.8 = (bf16[16,3072]{1,0:T(8,128)(2,1)S(1)}, bf16[16,3072]{1,0:T(8,128)(2,1)S(1)}, u32[]{:S(2)}, u32[]{:S(2)}) collective-permute-start(bf16[16,3072]{1,0:T(8,128)(2,1)S(1)} %get-tuple-element.41.refs_1_), channel_id=1, source_target_pairs={{0,3},{1,0},{2,1},{3,2},{4,7},{5,4},{6,5},{7,6},{8,11},{9,8},{10,9... | collective-permute-start | bytes 294920 | tf_op jit(solution)/shard_map/ppermute | solution.py:435
  22.1 1.4 %preact_partial.1 = (f32[128,1536]{1,0:T(8,128)S(1)}, bf16[128,1536]{1,0:T(8,128)(2,1)S(1)}, bf16[64,3072]{1,0:T(8,128)(2,1)S(1)}) custom-call(bf16[64,3072]{1,0:T(8,128)(2,1)S(1)} %order_tokens.1.refs_0_, bf16[64,3072]{1,0:T(8,128)(2,1)S(1)} %collective-permute-done.4.refs_1_, bf16[3072,1536]{1,0:T(8,128)(2,1)S(1)} %load_first.1.refs_6_.refs_2_.refs_3_), custom_call_target="tpu_custom_call" | custom-call | tf_op jit(solution)/shard_map/preact_partial/pallas_call | solution.py:59
  23.5 1.6 %collective-permute-start.5 = (bf16[128,1536]{1,0:T(8,128)(2,1)S(1)}, bf16[128,1536]{1,0:T(8,128)(2,1)S(1)}, u32[]{:S(2)}, u32[]{:S(2)}) collective-permute-start(bf16[128,1536]{1,0:T(8,128)(2,1)S(1)} %get-tuple-element.40.refs_2_), channel_id=1, source_target_pairs={{0,4},{4,0},{1,5},{5,1},{2,6},{6,2},{3,7},{7,3},{8,12},{12,8},{9,1... | collective-permute-start | bytes 1179656 | tf_op jit(solution)/shard_map/ppermute | solution.py:435
  25.1 3.8 %load_second.1.refs_5_.refs_4_.refs_2_ = bf16[1536,3072]{1,0:T(8,128)(2,1)S(1)} custom-call(s32[1]{0:T(128)} %bitcast.2.refs_0_, bf16[3072,3072]{1,0:T(8,128)(2,1)} %bitcast.8, bf16[128,1536]{1,0:T(8,128)(2,1)S(1)} %get-tuple-element.40.refs_2_), custom_call_target="tpu_custom_call" | custom-call | tf_op jit(solution)/shard_map/load_second/pallas_call | solution.py:59
  29.6 1.5 %collective-permute-start.17 = (bf16[64,3072]{1,0:T(8,128)(2,1)S(1)}, bf16[64,3072]{1,0:T(8,128)(2,1)S(1)}, u32[]{:S(2)}, u32[]{:S(2)}) collective-permute-start(bf16[64,3072]{1,0:T(8,128)(2,1)S(1)} %get-tuple-element.54.refs_0_), channel_id=1, source_target_pairs={{0,16},{8,24},{16,0},{24,8},{1,17},{9,25},{17,1},{25,9},{2,18},{10... | collective-permute-start | bytes 1179656 | tf_op jit(solution)/shard_map/ppermute | solution.py:435
  31.1 2.7 %back_partial.1 = (f32[128,1536]{1,0:T(8,128)S(1)}, bf16[128,1536]{1,0:T(8,128)(2,1)S(1)}, bf16[64,3072]{1,0:T(8,128)(2,1)S(1)}) custom-call(bf16[32,3072]{1,0:T(8,128)(2,1)S(1)} %get-tuple-element.42.refs_0_, bf16[32,3072]{1,0:T(8,128)(2,1)S(1)} %get-tuple-element.43.refs_1_, bf16[32,3072]{1,0:T(8,128)(2,1)S(1)} %collective-permute-done.9.refs_2_.refs_3_, ...), custom_call_target="tpu_custom_call" | custom-call | tf_op jit(solution)/shard_map/back_partial/pallas_call | solution.py:59
  33.8 1.4 %collective-permute-start.16 = (bf16[128,1536]{1,0:T(8,128)(2,1)S(1)}, bf16[128,1536]{1,0:T(8,128)(2,1)S(1)}, u32[]{:S(2)}, u32[]{:S(2)}) collective-permute-start(bf16[128,1536]{1,0:T(8,128)(2,1)S(1)} %get-tuple-element.44.refs_3_), channel_id=1, source_target_pairs={{0,4},{4,0},{1,5},{5,1},{2,6},{6,2},{3,7},{7,3},{8,12},{12,8},{9,1... | collective-permute-start | bytes 1179656 | tf_op jit(solution)/shard_map/ppermute | solution.py:435
  35.2 1.2 %collective-permute-start.19 = (bf16[64,3072]{1,0:T(8,128)(2,1)S(1)}, bf16[64,3072]{1,0:T(8,128)(2,1)S(1)}, u32[]{:S(2)}, u32[]{:S(2)}) collective-permute-start(bf16[64,3072]{1,0:T(8,128)(2,1)S(1)} %get-tuple-element.57.refs_2_), channel_id=1, source_target_pairs={{0,16},{8,24},{16,0},{24,8},{1,17},{9,25},{17,1},{25,9},{2,18},{10... | collective-permute-start | bytes 1179656 | tf_op jit(solution)/shard_map/ppermute | solution.py:435
  36.4 1.6 %block_out_partial.1 = (f32[64,3072]{1,0:T(8,128)S(1)}, bf16[32,3072]{1,0:T(8,128)(2,1)S(1)}, bf16[32,3072]{1,0:T(8,128)(2,1)S(1)}, f32[128,1536]{1,0:T(8,128)S(...) custom-call(f32[128,1536]{1,0:T(8,128)S(1)} %get-tuple-element.39.refs_0_, ...), custom_call_target="tpu_custom_call" | custom-call | tf_op jit(solution)/shard_map/block_out_partial/pallas_call | solution.py:59
  38.6 0.9 %collective-permute-done.11.refs_2_ = bf16[32,3072]{1,0:T(8,128)(2,1)S(1)} collective-permute-done((bf16[32,3072]{1,0:T(8,128)(2,1)S(1)}, bf16[32,3072]{1,0:T(8,128)(2,1)S(1)}, u32[]{:S(2)}, u32[]{:S(2)}) %collective-permute-start.11) | collective-permute-done | bytes 196640 | tf_op jit(solution)/shard_map/ppermute | solution.py:438
  40.0 2.6 %collective-permute-start.13 = (bf16[16,3072]{1,0:T(8,128)(2,1)S(1)}, bf16[16,3072]{1,0:T(8,128)(2,1)S(1)}, u32[]{:S(2)}, u32[]{:S(2)}) collective-permute-start(bf16[16,3072]{1,0:T(8,128)(2,1)S(1)} %get-tuple-element.49), channel_id=1, source_target_pairs={{0,1},{1,2},{2,3},{3,0},{4,5},{5,6},{6,7},{7,4},{8,9},{9,10},{10,1... | collective-permute-start | bytes 294920 | tf_op jit(solution)/shard_map/ppermute | solution.py:435
  42.6 1.0 %collective-permute-start.14 = (bf16[16,3072]{1,0:T(8,128)(2,1)S(1)}, bf16[16,3072]{1,0:T(8,128)(2,1)S(1)}, u32[]{:S(2)}, u32[]{:S(2)}) collective-permute-start(bf16[16,3072]{1,0:T(8,128)(2,1)S(1)} %get-tuple-element.50), channel_id=1, source_target_pairs={{0,2},{1,3},{2,0},{3,1},{4,6},{5,7},{6,4},{7,5},{8,10},{9,11},{10,... | collective-permute-start | bytes 294920 | tf_op jit(solution)/shard_map/ppermute | solution.py:435
  43.6 1.5 %collective-permute-start.15 = (bf16[16,3072]{1,0:T(8,128)(2,1)S(1)}, bf16[16,3072]{1,0:T(8,128)(2,1)S(1)}, u32[]{:S(2)}, u32[]{:S(2)}) collective-permute-start(bf16[16,3072]{1,0:T(8,128)(2,1)S(1)} %get-tuple-element.51), channel_id=1, source_target_pairs={{0,3},{1,0},{2,1},{3,2},{4,7},{5,4},{6,5},{7,6},{8,11},{9,8},{10,9... | collective-permute-start | bytes 294920 | tf_op jit(solution)/shard_map/ppermute | solution.py:435
  45.1 1.3 %collective-permute-start.25 = (bf16[128,768]{1,0:T(8,128)(2,1)S(1)}, bf16[128,768]{1,0:T(8,128)(2,1)S(1)}, u32[]{:S(2)}, u32[]{:S(2)}) collective-permute-start(bf16[128,768]{1,0:T(8,128)(2,1)S(1)} %get-tuple-element.65), channel_id=1, source_target_pairs={{0,16},{8,24},{16,0},{24,8},{1,17},{9,25},{17,1},{25,9},{2,18},{10... | collective-permute-start | bytes 589832 | tf_op jit(solution)/shard_map/ppermute | solution.py:435
  46.3 2.7 %grad_in_partial.1 = (f32[64,3072]{1,0:T(8,128)S(1)}, bf16[64,3072]{1,0:T(8,128)(2,1)S(1)}, bf16[128,768]{1,0:T(8,128)(2,1)S(1)}, bf16[128,768]{1,0:T(8,128)(2,1)S(1)}) custom-call(f32[128,1536]{1,0:T(8,128)S(1)} %get-tuple-element.52.refs_0_, bf16[128,1536]{1,0:T(8,128)(2,1)S(1)} %collective-permute-done.16.refs_1_, ...), custom_call_target="tpu_custom_call" | custom-call | tf_op jit(solution)/shard_map/grad_in_partial/pallas_call | solution.py:59
  49.1 0.9 %collective-permute-done.19.refs_4_.refs_5_ = bf16[64,3072]{1,0:T(8,128)(2,1)S(1)} collective-permute-done((bf16[64,3072]{1,0:T(8,128)(2,1)S(1)}, bf16[64,3072]{1,0:T(8,128)(2,1)S(1)}, u32[]{:S(2)}, u32[]{:S(2)}) %collective-permute-start.19) | collective-permute-done | bytes 393248 | tf_op jit(solution)/shard_map/ppermute | solution.py:435
  51.0 1.0 %collective-permute-start.24 = (bf16[128,768]{1,0:T(8,128)(2,1)S(1)}, bf16[128,768]{1,0:T(8,128)(2,1)S(1)}, u32[]{:S(2)}, u32[]{:S(2)}) collective-permute-start(bf16[128,768]{1,0:T(8,128)(2,1)S(1)} %get-tuple-element.63), channel_id=1, source_target_pairs={{0,16},{8,24},{16,0},{24,8},{1,17},{9,25},{17,1},{25,9},{2,18},{10... | collective-permute-start | bytes 589832 | tf_op jit(solution)/shard_map/ppermute | solution.py:435
  52.4 2.3 %collective-permute-start.20 = (bf16[16,3072]{1,0:T(8,128)(2,1)S(1)}, bf16[16,3072]{1,0:T(8,128)(2,1)S(1)}, u32[]{:S(2)}, u32[]{:S(2)}) collective-permute-start(bf16[16,3072]{1,0:T(8,128)(2,1)S(1)} %get-tuple-element.59), channel_id=1, source_target_pairs={{0,1},{1,2},{2,3},{3,0},{4,5},{5,6},{6,7},{7,4},{8,9},{9,10},{10,1... | collective-permute-start | bytes 294920 | tf_op jit(solution)/shard_map/ppermute | solution.py:435
  54.7 1.4 %collective-permute-start.21 = (bf16[16,3072]{1,0:T(8,128)(2,1)S(1)}, bf16[16,3072]{1,0:T(8,128)(2,1)S(1)}, u32[]{:S(2)}, u32[]{:S(2)}) collective-permute-start(bf16[16,3072]{1,0:T(8,128)(2,1)S(1)} %get-tuple-element.60), channel_id=1, source_target_pairs={{0,2},{1,3},{2,0},{3,1},{4,6},{5,7},{6,4},{7,5},{8,10},{9,11},{10,... | collective-permute-start | bytes 294920 | tf_op jit(solution)/shard_map/ppermute | solution.py:435
  56.2 1.9 %collective-permute-start.22 = (bf16[16,3072]{1,0:T(8,128)(2,1)S(1)}, bf16[16,3072]{1,0:T(8,128)(2,1)S(1)}, u32[]{:S(2)}, u32[]{:S(2)}) collective-permute-start(bf16[16,3072]{1,0:T(8,128)(2,1)S(1)} %get-tuple-element.61), channel_id=1, source_target_pairs={{0,3},{1,0},{2,1},{3,2},{4,7},{5,4},{6,5},{7,6},{8,11},{9,8},{10,9... | collective-permute-start | bytes 294920 | tf_op jit(solution)/shard_map/ppermute | solution.py:435
  58.0 2.6 %grad_w_out.1 = bf16[768,3072]{1,0:T(8,128)(2,1)} custom-call(bf16[128,768]{1,0:T(8,128)(2,1)S(1)} %get-tuple-element.64.refs_0_, bf16[128,768]{1,0:T(8,128)(2,1)S(1)} %collective-permute-done.25.refs_1_, bf16[64,3072]{1,0:T(8,128)(2,1)S(1)} %get-tuple-element.57.refs_2_, bf16[32,3072]{1,0:T(8,128)(2,1)S(1)} %collective-permute-done.9.refs_2_.refs_3_, ...), custom_call_target="tpu_custom_call" | custom-call | tf_op jit(solution)/shard_map/grad_w_out/pallas_call | solution.py:59
  60.7 2.7 %grad_w_in.1 = bf16[3072,768]{1,0:T(8,128)(2,1)} custom-call(bf16[64,3072]{1,0:T(8,128)(2,1)S(1)} %get-tuple-element.54.refs_0_, bf16[64,3072]{1,0:T(8,128)(2,1)S(1)} %collective-permute-done.4.refs_1_, bf16[64,3072]{1,0:T(8,128)(2,1)S(1)} %collective-permute-done.17.refs_5_.refs_2_, bf16[64,3072]{1,0:T(8,128)(2,1)S(1)} %collective-permute-done.23.refs_3_, ...), custom_call_target="tpu_custom_call" | custom-call | tf_op jit(solution)/shard_map/grad_w_in/pallas_call | solution.py:59
  63.6 0.7 %add_convert_fusion = bf16[16,3072]{1,0:T(8,128)(2,1)} fusion(bf16[16,3072]{1,0:T(8,128)(2,1)S(1)} %collective-permute-done.22, bf16[16,3072]{1,0:T(8,128)(2,1)S(1)} %collective-permute-done.21, f32[16,3072]{1,0:T(8,128)S(1)} %get-tuple-element.58.refs_6_.refs_7_, bf16[16,3072]{1,0:T(8,128)(2,1)S(1)} %collective-permute-done.20), kind=kLoop, calls=%fused_computation | loop fusion | flops 344064 | bytes 589824 | tf_op jit(solution)/shard_map/convert_element_type | solution.py:503
  (40 shorter events, 3.9 us)
Async XLA Ops:
  1.6 5.1 %collective-permute-start = (bf16[8,3072]{1,0:T(8,128)(2,1)S(1)}, bf16[8,3072]{1,0:T(8,128)(2,1)S(1)}, u32[]{:S(2)}, u32[]{:S(2)}) collective-permute-start(bf16[8,3072]{1,0:T(8,128)(2,1)S(1)} %get-tuple-element.36), channel_id=1, source_target_pairs={{0,4},{4,0},{1,5},{5,1},{2,6},{6,2},{3,7},{7,3},{8,12},{12,8},{9,1... | collective-permute-start | bytes 147464 | tf_op jit(solution)/shard_map/ppermute | solution.py:435
  6.7 9.9 %collective-permute-start.1 = (bf16[16,3072]{1,0:T(8,128)(2,1)S(1)}, bf16[16,3072]{1,0:T(8,128)(2,1)S(1)}, u32[]{:S(2)}, u32[]{:S(2)}) collective-permute-start(bf16[16,3072]{1,0:T(8,128)(2,1)S(1)} %get-tuple-element.38.refs_2_), channel_id=1, source_target_pairs={{0,1},{1,2},{2,3},{3,0},{4,5},{5,6},{6,7},{7,4},{8,9},{9,10},{10,1... | collective-permute-start | bytes 294920 | tf_op jit(solution)/shard_map/ppermute | solution.py:435
  8.9 8.2 %collective-permute-start.2 = (bf16[16,3072]{1,0:T(8,128)(2,1)S(1)}, bf16[16,3072]{1,0:T(8,128)(2,1)S(1)}, u32[]{:S(2)}, u32[]{:S(2)}) collective-permute-start(bf16[16,3072]{1,0:T(8,128)(2,1)S(1)} %get-tuple-element.38.refs_2_), channel_id=1, source_target_pairs={{0,2},{1,3},{2,0},{3,1},{4,6},{5,7},{6,4},{7,5},{8,10},{9,11},{10,... | collective-permute-start | bytes 294920 | tf_op jit(solution)/shard_map/ppermute | solution.py:435
  11.5 5.7 %collective-permute-start.3 = (bf16[16,3072]{1,0:T(8,128)(2,1)S(1)}, bf16[16,3072]{1,0:T(8,128)(2,1)S(1)}, u32[]{:S(2)}, u32[]{:S(2)}) collective-permute-start(bf16[16,3072]{1,0:T(8,128)(2,1)S(1)} %get-tuple-element.38.refs_2_), channel_id=1, source_target_pairs={{0,3},{1,0},{2,1},{3,2},{4,7},{5,4},{6,5},{7,6},{8,11},{9,8},{10,9... | collective-permute-start | bytes 294920 | tf_op jit(solution)/shard_map/ppermute | solution.py:435
  17.3 4.9 %collective-permute-start.4 = (bf16[64,3072]{1,0:T(8,128)(2,1)S(1)}, bf16[64,3072]{1,0:T(8,128)(2,1)S(1)}, u32[]{:S(2)}, u32[]{:S(2)}) collective-permute-start(bf16[64,3072]{1,0:T(8,128)(2,1)S(1)} %order_tokens.1.refs_0_), channel_id=1, source_target_pairs={{0,8},{8,0},{16,24},{24,16},{1,9},{9,1},{17,25},{25,17},{2,10},{10... | collective-permute-start | bytes 1179656 | tf_op jit(solution)/shard_map/ppermute | solution.py:438
  17.3 11.6 %collective-permute-start.6 = (bf16[16,3072]{1,0:T(8,128)(2,1)S(1)}, bf16[16,3072]{1,0:T(8,128)(2,1)S(1)}, u32[]{:S(2)}, u32[]{:S(2)}) collective-permute-start(bf16[16,3072]{1,0:T(8,128)(2,1)S(1)} %get-tuple-element.41.refs_1_), channel_id=1, source_target_pairs={{0,1},{1,2},{2,3},{3,0},{4,5},{5,6},{6,7},{7,4},{8,9},{9,10},{10,1... | collective-permute-start | bytes 294920 | tf_op jit(solution)/shard_map/ppermute | solution.py:435
  19.7 9.2 %collective-permute-start.7 = (bf16[16,3072]{1,0:T(8,128)(2,1)S(1)}, bf16[16,3072]{1,0:T(8,128)(2,1)S(1)}, u32[]{:S(2)}, u32[]{:S(2)}) collective-permute-start(bf16[16,3072]{1,0:T(8,128)(2,1)S(1)} %get-tuple-element.41.refs_1_), channel_id=1, source_target_pairs={{0,2},{1,3},{2,0},{3,1},{4,6},{5,7},{6,4},{7,5},{8,10},{9,11},{10,... | collective-permute-start | bytes 294920 | tf_op jit(solution)/shard_map/ppermute | solution.py:435
  21.4 7.5 %collective-permute-start.8 = (bf16[16,3072]{1,0:T(8,128)(2,1)S(1)}, bf16[16,3072]{1,0:T(8,128)(2,1)S(1)}, u32[]{:S(2)}, u32[]{:S(2)}) collective-permute-start(bf16[16,3072]{1,0:T(8,128)(2,1)S(1)} %get-tuple-element.41.refs_1_), channel_id=1, source_target_pairs={{0,3},{1,0},{2,1},{3,2},{4,7},{5,4},{6,5},{7,6},{8,11},{9,8},{10,9... | collective-permute-start | bytes 294920 | tf_op jit(solution)/shard_map/ppermute | solution.py:435
  23.5 12.8 %collective-permute-start.5 = (bf16[128,1536]{1,0:T(8,128)(2,1)S(1)}, bf16[128,1536]{1,0:T(8,128)(2,1)S(1)}, u32[]{:S(2)}, u32[]{:S(2)}) collective-permute-start(bf16[128,1536]{1,0:T(8,128)(2,1)S(1)} %get-tuple-element.40.refs_2_), channel_id=1, source_target_pairs={{0,4},{4,0},{1,5},{5,1},{2,6},{6,2},{3,7},{7,3},{8,12},{12,8},{9,1... | collective-permute-start | bytes 1179656 | tf_op jit(solution)/shard_map/ppermute | solution.py:435
  29.0 2.1 %collective-permute-start.10 = (bf16[32,3072]{1,0:T(8,128)(2,1)S(1)}, bf16[32,3072]{1,0:T(8,128)(2,1)S(1)}, u32[]{:S(2)}, u32[]{:S(2)}) collective-permute-start(bf16[32,3072]{1,0:T(8,128)(2,1)S(1)} %get-tuple-element.43.refs_1_), channel_id=1, source_target_pairs={{0,8},{8,0},{16,24},{24,16},{1,9},{9,1},{17,25},{25,17},{2,10},{10... | collective-permute-start | bytes 589832 | tf_op jit(solution)/shard_map/ppermute | solution.py:438
  29.1 2.0 %collective-permute-start.9 = (bf16[32,3072]{1,0:T(8,128)(2,1)S(1)}, bf16[32,3072]{1,0:T(8,128)(2,1)S(1)}, u32[]{:S(2)}, u32[]{:S(2)}) collective-permute-start(bf16[32,3072]{1,0:T(8,128)(2,1)S(1)} %get-tuple-element.42.refs_0_), channel_id=1, source_target_pairs={{0,8},{8,0},{16,24},{24,16},{1,9},{9,1},{17,25},{25,17},{2,10},{10... | collective-permute-start | bytes 589832 | tf_op jit(solution)/shard_map/ppermute | solution.py:438
  29.6 14.0 %collective-permute-start.17 = (bf16[64,3072]{1,0:T(8,128)(2,1)S(1)}, bf16[64,3072]{1,0:T(8,128)(2,1)S(1)}, u32[]{:S(2)}, u32[]{:S(2)}) collective-permute-start(bf16[64,3072]{1,0:T(8,128)(2,1)S(1)} %get-tuple-element.54.refs_0_), channel_id=1, source_target_pairs={{0,16},{8,24},{16,0},{24,8},{1,17},{9,25},{17,1},{25,9},{2,18},{10... | collective-permute-start | bytes 1179656 | tf_op jit(solution)/shard_map/ppermute | solution.py:435
  33.8 11.2 %collective-permute-start.16 = (bf16[128,1536]{1,0:T(8,128)(2,1)S(1)}, bf16[128,1536]{1,0:T(8,128)(2,1)S(1)}, u32[]{:S(2)}, u32[]{:S(2)}) collective-permute-start(bf16[128,1536]{1,0:T(8,128)(2,1)S(1)} %get-tuple-element.44.refs_3_), channel_id=1, source_target_pairs={{0,4},{4,0},{1,5},{5,1},{2,6},{6,2},{3,7},{7,3},{8,12},{12,8},{9,1... | collective-permute-start | bytes 1179656 | tf_op jit(solution)/shard_map/ppermute | solution.py:435
  35.2 14.8 %collective-permute-start.19 = (bf16[64,3072]{1,0:T(8,128)(2,1)S(1)}, bf16[64,3072]{1,0:T(8,128)(2,1)S(1)}, u32[]{:S(2)}, u32[]{:S(2)}) collective-permute-start(bf16[64,3072]{1,0:T(8,128)(2,1)S(1)} %get-tuple-element.57.refs_2_), channel_id=1, source_target_pairs={{0,16},{8,24},{16,0},{24,8},{1,17},{9,25},{17,1},{25,9},{2,18},{10... | collective-permute-start | bytes 1179656 | tf_op jit(solution)/shard_map/ppermute | solution.py:435
  38.0 1.5 %collective-permute-start.11 = (bf16[32,3072]{1,0:T(8,128)(2,1)S(1)}, bf16[32,3072]{1,0:T(8,128)(2,1)S(1)}, u32[]{:S(2)}, u32[]{:S(2)}) collective-permute-start(bf16[32,3072]{1,0:T(8,128)(2,1)S(1)} %get-tuple-element.46), channel_id=1, source_target_pairs={{0,8},{8,0},{16,24},{24,16},{1,9},{9,1},{17,25},{25,17},{2,10},{10... | collective-permute-start | bytes 589832 | tf_op jit(solution)/shard_map/ppermute | solution.py:438
  38.1 1.7 %collective-permute-start.12 = (bf16[32,3072]{1,0:T(8,128)(2,1)S(1)}, bf16[32,3072]{1,0:T(8,128)(2,1)S(1)}, u32[]{:S(2)}, u32[]{:S(2)}) collective-permute-start(bf16[32,3072]{1,0:T(8,128)(2,1)S(1)} %get-tuple-element.47), channel_id=1, source_target_pairs={{0,8},{8,0},{16,24},{24,16},{1,9},{9,1},{17,25},{25,17},{2,10},{10... | collective-permute-start | bytes 589832 | tf_op jit(solution)/shard_map/ppermute | solution.py:438
  40.0 10.0 %collective-permute-start.13 = (bf16[16,3072]{1,0:T(8,128)(2,1)S(1)}, bf16[16,3072]{1,0:T(8,128)(2,1)S(1)}, u32[]{:S(2)}, u32[]{:S(2)}) collective-permute-start(bf16[16,3072]{1,0:T(8,128)(2,1)S(1)} %get-tuple-element.49), channel_id=1, source_target_pairs={{0,1},{1,2},{2,3},{3,0},{4,5},{5,6},{6,7},{7,4},{8,9},{9,10},{10,1... | collective-permute-start | bytes 294920 | tf_op jit(solution)/shard_map/ppermute | solution.py:435
  42.6 8.4 %collective-permute-start.14 = (bf16[16,3072]{1,0:T(8,128)(2,1)S(1)}, bf16[16,3072]{1,0:T(8,128)(2,1)S(1)}, u32[]{:S(2)}, u32[]{:S(2)}) collective-permute-start(bf16[16,3072]{1,0:T(8,128)(2,1)S(1)} %get-tuple-element.50), channel_id=1, source_target_pairs={{0,2},{1,3},{2,0},{3,1},{4,6},{5,7},{6,4},{7,5},{8,10},{9,11},{10,... | collective-permute-start | bytes 294920 | tf_op jit(solution)/shard_map/ppermute | solution.py:435
  43.6 8.4 %collective-permute-start.15 = (bf16[16,3072]{1,0:T(8,128)(2,1)S(1)}, bf16[16,3072]{1,0:T(8,128)(2,1)S(1)}, u32[]{:S(2)}, u32[]{:S(2)}) collective-permute-start(bf16[16,3072]{1,0:T(8,128)(2,1)S(1)} %get-tuple-element.51), channel_id=1, source_target_pairs={{0,3},{1,0},{2,1},{3,2},{4,7},{5,4},{6,5},{7,6},{8,11},{9,8},{10,9... | collective-permute-start | bytes 294920 | tf_op jit(solution)/shard_map/ppermute | solution.py:435
  45.1 9.7 %collective-permute-start.25 = (bf16[128,768]{1,0:T(8,128)(2,1)S(1)}, bf16[128,768]{1,0:T(8,128)(2,1)S(1)}, u32[]{:S(2)}, u32[]{:S(2)}) collective-permute-start(bf16[128,768]{1,0:T(8,128)(2,1)S(1)} %get-tuple-element.65), channel_id=1, source_target_pairs={{0,16},{8,24},{16,0},{24,8},{1,17},{9,25},{17,1},{25,9},{2,18},{10... | collective-permute-start | bytes 589832 | tf_op jit(solution)/shard_map/ppermute | solution.py:435
  50.0 10.7 %collective-permute-start.23 = (bf16[64,3072]{1,0:T(8,128)(2,1)S(1)}, bf16[64,3072]{1,0:T(8,128)(2,1)S(1)}, u32[]{:S(2)}, u32[]{:S(2)}) collective-permute-start(bf16[64,3072]{1,0:T(8,128)(2,1)S(1)} %collective-permute-done.17.refs_5_.refs_2_), channel_id=1, source_target_pairs={{0,8},{8,0},{16,24},{24,16},{1,9},{9,1},{17,25},{25,17},{2,10},{10... | collective-permute-start | bytes 1179656 | tf_op jit(solution)/shard_map/ppermute | solution.py:438
  50.0 2.3 %collective-permute-start.18 = (bf16[64,3072]{1,0:T(8,128)(2,1)S(1)}, bf16[64,3072]{1,0:T(8,128)(2,1)S(1)}, u32[]{:S(2)}, u32[]{:S(2)}) collective-permute-start(bf16[64,3072]{1,0:T(8,128)(2,1)S(1)} %get-tuple-element.56), channel_id=1, source_target_pairs={{0,8},{8,0},{16,24},{24,16},{1,9},{9,1},{17,25},{25,17},{2,10},{10... | collective-permute-start | bytes 1179656 | tf_op jit(solution)/shard_map/ppermute | solution.py:438
  51.0 9.7 %collective-permute-start.24 = (bf16[128,768]{1,0:T(8,128)(2,1)S(1)}, bf16[128,768]{1,0:T(8,128)(2,1)S(1)}, u32[]{:S(2)}, u32[]{:S(2)}) collective-permute-start(bf16[128,768]{1,0:T(8,128)(2,1)S(1)} %get-tuple-element.63), channel_id=1, source_target_pairs={{0,16},{8,24},{16,0},{24,8},{1,17},{9,25},{17,1},{25,9},{2,18},{10... | collective-permute-start | bytes 589832 | tf_op jit(solution)/shard_map/ppermute | solution.py:435
  52.0 4.1 %collective-permute-start.26 = (bf16[64,3072]{1,0:T(8,128)(2,1)S(1)}, bf16[64,3072]{1,0:T(8,128)(2,1)S(1)}, u32[]{:S(2)}, u32[]{:S(2)}) collective-permute-start(bf16[64,3072]{1,0:T(8,128)(2,1)S(1)} %collective-permute-done.19.refs_4_.refs_5_), channel_id=1, source_target_pairs={{0,8},{8,0},{16,24},{24,16},{1,9},{9,1},{17,25},{25,17},{2,10},{10... | collective-permute-start | bytes 1179656 | tf_op jit(solution)/shard_map/ppermute | solution.py:438
  52.1 12.2 %copy-start = (bf16[16,3072]{1,0:T(8,128)(2,1)}, bf16[16,3072]{1,0:T(8,128)(2,1)S(1)}, u32[]{:S(2)}) copy-start(bf16[16,3072]{1,0:T(8,128)(2,1)S(1)} %add_convert_fusion.1.refs_3_) | copy-start | bytes 294916
  52.4 11.0 %collective-permute-start.20 = (bf16[16,3072]{1,0:T(8,128)(2,1)S(1)}, bf16[16,3072]{1,0:T(8,128)(2,1)S(1)}, u32[]{:S(2)}, u32[]{:S(2)}) collective-permute-start(bf16[16,3072]{1,0:T(8,128)(2,1)S(1)} %get-tuple-element.59), channel_id=1, source_target_pairs={{0,1},{1,2},{2,3},{3,0},{4,5},{5,6},{6,7},{7,4},{8,9},{9,10},{10,1... | collective-permute-start | bytes 294920 | tf_op jit(solution)/shard_map/ppermute | solution.py:435
  54.7 8.8 %collective-permute-start.21 = (bf16[16,3072]{1,0:T(8,128)(2,1)S(1)}, bf16[16,3072]{1,0:T(8,128)(2,1)S(1)}, u32[]{:S(2)}, u32[]{:S(2)}) collective-permute-start(bf16[16,3072]{1,0:T(8,128)(2,1)S(1)} %get-tuple-element.60), channel_id=1, source_target_pairs={{0,2},{1,3},{2,0},{3,1},{4,6},{5,7},{6,4},{7,5},{8,10},{9,11},{10,... | collective-permute-start | bytes 294920 | tf_op jit(solution)/shard_map/ppermute | solution.py:435
  56.2 7.4 %collective-permute-start.22 = (bf16[16,3072]{1,0:T(8,128)(2,1)S(1)}, bf16[16,3072]{1,0:T(8,128)(2,1)S(1)}, u32[]{:S(2)}, u32[]{:S(2)}) collective-permute-start(bf16[16,3072]{1,0:T(8,128)(2,1)S(1)} %get-tuple-element.61), channel_id=1, source_target_pairs={{0,3},{1,0},{2,1},{3,2},{4,7},{5,4},{6,5},{7,6},{8,11},{9,8},{10,9... | collective-permute-start | bytes 294920 | tf_op jit(solution)/shard_map/ppermute | solution.py:435

commit v6 on v4

v6 whole, which is shorter than its diff:
```python
import functools

import jax
import jax.numpy as jnp
from jax import lax
from jax.experimental import pallas as pl
from jax.experimental.pallas import tpu as pltpu
from jax.sharding import PartitionSpec as P

CORES = 2
OUT_PIECES = 2
COT_PIECES = 2
VMEM_LIMIT = 24 * 1024 * 1024
NT = (((1,), (1,)), ((), ()))
NN = (((1,), (0,)), ((), ()))
TN = (((0,), (0,)), ((), ()))
VMEM = pl.BlockSpec(memory_space=pltpu.VMEM)
SMEM = pl.BlockSpec(memory_space=pltpu.SMEM)
HBM = pl.BlockSpec(memory_space=pltpu.HBM)
ANY = pl.BlockSpec(memory_space=pl.ANY)


def mm(a, b, dims):
    return lax.dot_general(a, b, dims, preferred_element_type=jnp.float32)


def mm_streamed(rows, weights):
    return mm(weights, rows, NT).T


def tile_of(size, most):
    for tile in range(most, 0, -128):
        if size % tile == 0:
            return tile
    return size


def in_hbm(x):
    return pltpu.with_memory_space_constraint(x, pltpu.HBM)


def call(kernel, in_specs, out_specs, out_shape, name, scratch=(), after=()):
    reads = len(in_specs)

    def run(*refs):
        kernel(*refs[:reads], *refs[reads + len(after) :])

    kernel_call = pl.pallas_call(
        run,
        in_specs=list(in_specs) + [ANY] * len(after),
        out_specs=out_specs,
        out_shape=out_shape,
        scratch_shapes=scratch,
        compiler_params=pltpu.CompilerParams(vmem_limit_bytes=VMEM_LIMIT),
        cost_estimate=pl.CostEstimate(flops=0, bytes_accessed=0, transcendentals=0),
        name=name,
    )
    return lambda *args: kernel_call(*args, *after)


def shape(dims, dtype=jnp.bfloat16):
    return jax.ShapeDtypeStruct(tuple(dims), dtype)


def load_kernel(dp, size, pieces, columns, place, w, out, sems):
    rows = (w.shape[0] if columns else size) // pieces
    copies = []
    for b in range(dp // CORES):
        start = lax.rem(place[0] + CORES * b, dp) * size
        for p in range(pieces):
            if columns:
                cut = pl.ds(p * rows, rows)
                source = w.at[cut, pl.ds(pl.multiple_of(start, 128), size)]
                to = out.at[cut, pl.ds(b * size, size)]
            else:
                source = w.at[pl.ds(pl.multiple_of(start + p * rows, 16), rows)]
                to = out.at[pl.ds(b * size + p * rows, rows)]
            copies.append(pltpu.make_async_copy(source, to, sems.at[b * pieces + p]))
    for copy in copies:
        copy.start()
    for copy in copies:
        copy.wait()


def load(place, w, dp, size, columns, name, after):
    blocks, pieces = dp // CORES, 4
    units = blocks * size
    return call(
        functools.partial(load_kernel, dp, size, pieces, columns),
        [SMEM, HBM],
        VMEM,
        pltpu.VMEM((w.shape[0], units) if columns else (units, w.shape[1]), jnp.bfloat16),
        name,
        scratch=[pltpu.SemaphoreType.DMA((blocks * pieces,))],
        after=after,
    )(place, in_hbm(w))


def split_kernel(place, tokens, cots, cot, *rest):
    *outs, sems = rest
    count, width = len(outs), outs[0].shape[1]
    copies = [pltpu.make_async_copy(cots, cot, sems.at[count])]
    for k in reversed(range(count)):
        at = lax.rem(place[0] + k, count) * width
        source = tokens.at[:, pl.ds(pl.multiple_of(at, 128), width)]
        copies.append(pltpu.make_async_copy(source, outs[k], sems.at[k]))
    for copy in reversed(copies):
        copy.start()
    for copy in copies:
        copy.wait()


def split(row_place, tokens, cots, count):
    rows, width = tokens.shape[0], tokens.shape[1] // count
    return call(
        split_kernel,
        [SMEM, HBM, HBM],
        [VMEM] * (1 + count),
        [shape(cots.shape)] + [shape((rows, width))] * count,
        "split_width",
        scratch=[pltpu.SemaphoreType.DMA((1 + count,))],
    )(row_place, tokens, cots)


def stack_kernel(*refs):
    *parts, cot, out, cot_out = refs
    out[...] = jnp.concatenate([r[...].astype(jnp.float32) for r in parts]).astype(out.dtype)
    cot_out[...] = cot[...]


def stack(parts, cot):
    rows, width = parts[0].shape
    return call(
        stack_kernel,
        [VMEM] * (1 + len(parts)),
        [VMEM] * 2,
        [shape((rows * len(parts), width)), shape(cot.shape)],
        "stack_rows",
    )(*parts, cot)


def tokens_kernel(row, row_place, col_place, *refs):
    *stacks, out, held = refs
    col, n = len(stacks), held.shape[1]
    my_row, my_col = row_place[0], col_place[0]
    for k, part in enumerate(stacks):
        rows = part[...].astype(jnp.float32)
        for r in range(row):
            at = lax.rem(my_row + row - r, row) * col + lax.rem(my_col + col - k, col)
            held[at] = rows[r * n : (r + 1) * n]
    for at in range(0, row * col, 2):
        pair = jnp.concatenate([held[at], held[at + 1]])
        out[at * n : (at + 2) * n] = pair.astype(out.dtype)


def tokens_in_order(row_place, col_place, stacks, row, after):
    rows, width = stacks[0].shape
    col = len(stacks)
    return call(
        functools.partial(tokens_kernel, row),
        [SMEM, SMEM] + [VMEM] * col,
        VMEM,
        shape((rows * col, width)),
        "order_tokens",
        scratch=[pltpu.VMEM((row * col, rows // row, width), jnp.float32)],
        after=after,
    )(row_place, col_place, *stacks)


def order_kernel(count, place, *refs):
    parts, outs, held = refs[:count], refs[count:-1], refs[-1]
    me, rows = place[0], parts[0].shape[0]
    for k, part in enumerate(parts):
        held[lax.rem(me + count - k, count)] = part[...]
    each = count // len(outs)
    for k in range(count):
        start = k % each * rows
        outs[k // each][start : start + rows] = held[k]


def in_order(col_place, parts, after):
    rows, width = parts[0].shape
    count = len(parts)
    return call(
        functools.partial(order_kernel, count),
        [SMEM] + [VMEM] * count,
        [VMEM] * COT_PIECES,
        [shape((rows * count // COT_PIECES, width))] * COT_PIECES,
        "order_rows",
        scratch=[pltpu.VMEM((count, rows, width), jnp.bfloat16)],
        after=after,
    )(col_place, *parts)


def first_kernel(dims, tile, mine, *refs):
    *groups, w, total, sent, own_out, rows = refs
    at = 0
    for i, group in enumerate(groups):
        cut = slice(at, at + group.shape[0])
        rows[cut] = group[...]
        if i < mine:
            own_out[cut] = group[...]
        at += group.shape[0]
    for at in range(0, total.shape[1], tile):
        cut = slice(at, at + tile)
        if dims is NN:
            part = mm(rows[...], w[:, cut], NN)
        else:
            part = mm_streamed(rows[...], w[cut, :])
        total[:, cut] = part
        sent[:, cut] = part.astype(jnp.bfloat16)


def first(own, other, w, dims, name):
    half, width = len(own) * own[0].shape[0], own[0].shape[1]
    n = 2 * half
    units = w.shape[1 if dims is NN else 0]
    tile = tile_of(units, 256 if dims is NN else 512)
    return call(
        functools.partial(first_kernel, dims, tile, len(own)),
        [VMEM] * (len(own) + len(other) + 1),
        [VMEM] * 3,
        [shape((n, units), jnp.float32), shape((n, units)), shape((half, width))],
        name,
        scratch=[pltpu.VMEM((n, width), jnp.bfloat16)],
    )(*own, *other, w)


def gelu_parts(preact):
    cdf = 0.5 * (1.0 + lax.erf(preact * 0.7071067811865476))
    slopes = cdf + preact * jnp.exp(-0.5 * preact * preact) * 0.3989422804014327
    return (preact * cdf, slopes)


def second_product(dims, vals, w, keep, sends):
    half, width = keep.shape
    tile = tile_of(width, 512)
    for at in range(0, width, tile):
        cut = slice(at, at + tile)
        if dims is NN:
            part = mm(vals[...], w[:, cut], NN)
        else:
            part = mm_streamed(vals[...], w[cut, :])
        keep[:, cut] = part[:half]
        for i, send in enumerate(sends):
            rows = send.shape[0]
            send[:, cut] = part[half + i * rows : half + (i + 1) * rows].astype(jnp.bfloat16)


def row_sum(total, parts, cut):
    whole = total[:, cut]
    for part in parts:
        whole = whole + part[:, cut].astype(jnp.float32)
    return whole


def forward_kernel(blocks, shares, *refs):
    total, parts, w = refs[0], refs[1 : 1 + shares], refs[1 + shares]
    keep, *sends = refs[2 + shares : 3 + shares + OUT_PIECES]
    slopes, *hidden, vals = refs[3 + shares + OUT_PIECES :]
    size = total.shape[1] // blocks
    for b in range(blocks):
        cut = slice(b * size, (b + 1) * size)
        value, slope = gelu_parts(row_sum(total, parts, cut))
        value = value.astype(jnp.bfloat16)
        vals[:, cut] = value
        hidden[b][...] = value
        slopes[:, cut] = slope
    second_product(NN, vals, w, keep, sends)


def block_out_partial(total, parts, w, size, after):
    n, units = total.shape
    half, blocks, width = n // 2, units // size, w.shape[1]
    out_shape = (
        [shape((half, width), jnp.float32)]
        + [shape((half // OUT_PIECES, width))] * OUT_PIECES
        + [shape((n, units), jnp.float32)]
        + [shape((n, size))] * blocks
    )
    keep, *rest = call(
        functools.partial(forward_kernel, blocks, len(parts)),
        [VMEM] * (2 + len(parts)),
        [VMEM] * len(out_shape),
        out_shape,
        "block_out_partial",
        scratch=[pltpu.VMEM((n, units), jnp.bfloat16)],
        after=after,
    )(total, *parts, w)
    return keep, rest[:OUT_PIECES], rest[OUT_PIECES], rest[OUT_PIECES + 1 :]


def backward_kernel(blocks, shares, *refs):
    total, parts, slopes, w = refs[0], refs[1 : 1 + shares], refs[1 + shares], refs[2 + shares]
    hidden, refs = refs[3 + shares : 2 + shares + blocks], refs[2 + shares + blocks :]
    keep, send, *pre = refs[: 2 + blocks]
    *handed_on, vals = refs[2 + blocks :]
    for a, b in zip(hidden, handed_on):
        b[...] = a[...]
    size = total.shape[1] // blocks
    for b in range(blocks):
        cut = slice(b * size, (b + 1) * size)
        value = (row_sum(total, parts, cut) * slopes[:, cut]).astype(jnp.bfloat16)
        vals[:, cut] = value
        pre[b][...] = value
    second_product(NT, vals, w, keep, [send])


def grad_in_partial(total, parts, slopes, w, hidden, size, after):
    n, units = total.shape
    half, blocks, width = n // 2, units // size, w.shape[0]
    out_shape = [shape((half, width), jnp.float32), shape((half, width))]
    out_shape += [shape((n, size))] * (blocks + len(hidden))
    keep, send, *rest = call(
        functools.partial(backward_kernel, blocks, len(parts)),
        [VMEM] * (3 + len(parts) + len(hidden)),
        [VMEM] * len(out_shape),
        out_shape,
        "grad_in_partial",
        scratch=[pltpu.VMEM((n, units), jnp.bfloat16)],
        after=after,
    )(total, *parts, slopes, w, *hidden)
    return keep, send, rest[:blocks], rest[blocks:]


def cores_kernel(pieces, count, steps, place, keep, *refs):
    parts, outs, held = refs[:pieces], refs[pieces:-1], refs[-1]
    rows = keep.shape[0] // count
    at = 0
    for part in parts:
        cut = slice(at, at + part.shape[0])
        held[cut] = keep[cut] + part[...].astype(jnp.float32)
        at += part.shape[0]
    for k, out in zip(steps, outs):
        at = pl.ds(pl.multiple_of(lax.rem(place[0] + k, count) * rows, 16), rows)
        out[...] = held[at].astype(out.dtype)


def cores_sum(col_place, keep, parts, count, steps, name, after=()):
    rows, width = keep.shape[0] // count, keep.shape[1]
    return call(
        functools.partial(cores_kernel, len(parts), count, steps),
        [SMEM, VMEM] + [VMEM] * len(parts),
        [VMEM] * len(steps),
        [shape((rows, width), jnp.bfloat16 if k else jnp.float32) for k in steps],
        name,
        scratch=[pltpu.VMEM(keep.shape, jnp.float32)],
        after=after,
    )(col_place, keep, *parts)


def weight_kernel(lefts, tile, across, *refs):
    left, right, out = refs[:lefts], refs[lefts:-5], refs[-5]
    rows_left, rows_right, staged, sems = refs[-4:]
    for groups, rows in ((left, rows_left), (right, rows_right)):
        at = 0
        for group in groups:
            rows[at : at + group.shape[0]] = group[...]
            at += group.shape[0]
    copies = []
    for i, at in enumerate(range(0, out.shape[1 if across else 0], tile)):
        cut = slice(at, at + tile)
        if across:
            part, where = mm(rows_left[...], rows_right[:, cut], TN), (slice(None), cut)
        else:
            part, where = mm(rows_left[:, cut], rows_right[...], TN), (cut, slice(None))
        staged[where] = part.astype(jnp.bfloat16)
        copies.append(pltpu.make_async_copy(staged.at[where], out.at[where], sems.at[i]))
        copies[-1].start()
    for copy in copies:
        copy.wait()


def weight_grad(left, right, across, name, after=()):
    n = sum(group.shape[0] for group in left)
    k, m = left[0].shape[1], right[0].shape[1]
    long = m if across else k
    tile = tile_of(long, 512)
    return call(
        functools.partial(weight_kernel, len(left), tile, across),
        [VMEM] * (len(left) + len(right)),
        HBM,
        shape((k, m)),
        name,
        scratch=[
            pltpu.VMEM((n, k), jnp.bfloat16),
            pltpu.VMEM((n, m), jnp.bfloat16),
            pltpu.VMEM((k, m), jnp.bfloat16),
            pltpu.SemaphoreType.DMA((long // tile,)),
        ],
        after=after,
    )(*left, *right)


def body(dp, row, col, tokens, w_in, w_out, grad_out):
    blocks = dp // CORES
    width, size = w_in.shape[0], w_in.shape[2] // dp
    dp_place = lax.axis_index("dp").astype(jnp.int32)[None]
    row_place = lax.axis_index("row").astype(jnp.int32)[None]
    col_place = lax.axis_index("col").astype(jnp.int32)[None]

    def shifted(x, axis, step):
        count = {"dp": dp, "row": row, "col": col}[axis]
        return lax.ppermute(x, axis, [(i, (i + step) % count) for i in range(count)])

    def across_cores(x):
        return lax.ppermute(x, "dp", [(i, i ^ 1) for i in range(dp)])

    def across_rows(x):
        return [shifted(x, "row", step) for step in range(1, row)]

    def across_chips(x):
        return [shifted(x, "dp", CORES * b) for b in range(1, blocks)]

    cot_mine, own, *other_widths = split(row_place, in_hbm(tokens), in_hbm(grad_out), row)
    arrived = [shifted(part, "row", step + 1) for step, part in enumerate(other_widths)]
    stacked, cot_mine = stack([own, *arrived], cot_mine)
    stacks = [stacked] + [shifted(stacked, "col", step) for step in range(1, col)]
    cots = [cot_mine] + [shifted(cot_mine, "col", step) for step in range(1, col)]
    w_first = load(dp_place, w_in[:, 0, :], dp, size, True, "load_first", [stacked])
    tok = tokens_in_order(row_place, col_place, stacks, row, [w_first])
    tok_other = across_cores(tok)

    pre_total, pre_sent, tok_later = first([tok], [tok_other], w_first, NN, "preact_partial")
    pre_parts = across_rows(pre_sent)
    w_second = load(dp_place, w_out[0], dp, size, False, "load_second", [pre_sent])
    cot = in_order(col_place, cots, [w_second])
    cot_other = [across_cores(x) for x in cot]
    back_total, back_sent, cot_later = first(cot, cot_other, w_second, NT, "back_partial")
    back_parts = across_rows(back_sent)
    tok_there = across_chips(tok_later)
    cot_there = across_chips(cot_later)

    far_first = sorted(range(1, col), key=lambda k: -min(k, col - k))

    def col_total(sums):
        total = sums[0]
        for part in [shifted(sums[k], "col", k) for k in far_first]:
            total = total + part.astype(jnp.float32)
        return total.astype(jnp.bfloat16)

    out_keep, out_sends, slopes, hidden = block_out_partial(
        pre_total, pre_parts, w_second, size, [back_sent]
    )
    out_parts = [across_cores(x) for x in out_sends]
    out_sums = cores_sum(col_place, out_keep, out_parts, col, range(col), "block_out_cores")
    block_out = col_total(out_sums)

    def all_replicas(own, other, there):
        groups = [own, *other]
        for part in there:
            groups += [part, across_cores(part)]
        return groups

    tok_all = all_replicas(tok_later, [tok_other], tok_there)
    cot_all = all_replicas(cot_later, cot_other, cot_there)
    in_keep, in_send, grad_pre, handed_on = grad_in_partial(
        back_total, back_parts, slopes, w_first, hidden[1:], size, [out_sums[0], tok_there[-1]]
    )

    def to_owner(others):
        return [shifted(x, "dp", CORES * (b + 1)) for b, x in enumerate(others)]

    hid_arrived = to_owner(handed_on)
    in_parts = [across_cores(in_send)]
    ahead = [1]
    late = [k for k in range(col) if k not in ahead]
    after = [block_out, cot_all[-1], tok_all[-1]]
    in_sums = dict(
        zip(ahead, cores_sum(col_place, in_keep, in_parts, col, ahead, "grad_in_ahead"))
    )
    in_sums.update(
        zip(late, cores_sum(col_place, in_keep, in_parts, col, late, "grad_in_cores", after))
    )
    grad_in = col_total(in_sums)

    pre_arrived = to_owner(grad_pre[1:])
    grad_out_w = weight_grad([hidden[0], *hid_arrived], cot_all, True, "grad_w_out")
    grad_in_w = weight_grad(tok_all, [grad_pre[0], *pre_arrived], False, "grad_w_in", [in_sums[0]])
    return block_out, grad_in, grad_in_w[:, None, :], grad_out_w[None]


def solution(mesh):
    in_specs = (
        P(("dp", "row", "col"), None),
        P("row", "col", None),
        P("col", None, "row"),
        P(("dp", "col"), "row"),
    )
    out_specs = (
        P(("dp", "col"), "row"),
        P(("dp", "col"), "row"),
        P("row", "col", "dp"),
        P("col", "dp", "row"),
    )
    sizes = (mesh.shape["dp"], mesh.shape["row"], mesh.shape["col"])
    return jax.shard_map(
        functools.partial(body, *sizes),
        mesh=mesh,
        in_specs=in_specs,
        out_specs=out_specs,
        check_vma=False,
    )
```

time: 66.9 us -> 64.3 us (0.961)
  waiting for transfers between devices: 11.8 us -> 5.62 us
  starting transfers between devices: 29.5 us -> 34 us
  Pallas kernels: 23.8 us -> 23 us
    ppermute x18 -> x19, waiting for transfers between devices: 10.5 us -> 3.68 us  [shifted(): lax.ppermute(x, axis, [(i, (i + step) % count) for i in range(count)])]
    ppermute x18 -> x19, starting transfers between devices: 28.3 us -> 32.8 us  [shifted(): lax.ppermute(x, axis, [(i, (i + step) % count) for i in range(count)])]
    pallas_call x14 -> x15, Pallas kernels: 23.8 us -> 23 us  [call(): return lambda *args: kernel_call(*args, *after)]
    ppermute x8, waiting for transfers between devices: 1.23 us -> 1.94 us  [across_cores(): return lax.ppermute(x, 'dp', [(i, i ^ 1) for i in range(dp)])]
  transfers between devices with their start and end apart: 26 -> 27, of which waited for: 9 -> 9; matrix products, arithmetic and copies ran while one was open for 0% -> 0% of each run, Pallas kernels for 34% -> 34%
where the time goes in v6:
time: 64.3 us; the launch traced here: 64.2 us
  starting transfers between devices  34 us (53%)
  Pallas kernels  23 us (36%)
  waiting for transfers between devices  5.62 us (9%)
  between operations  0.84 us (1%)
  other arithmetic  0.74 us (1%)
    ppermute x19, starting transfers between devices, shifted(): lax.ppermute(x, axis, [(i, (i + step) % count) for i in range(count)])  32.8 us
    pallas_call x15, Pallas kernels, call(): return lambda *args: kernel_call(*args, *after)  23 us
    ppermute x19, waiting for transfers between devices, shifted(): lax.ppermute(x, axis, [(i, (i + step) % count) for i in range(count)])  3.68 us
    ppermute x8, waiting for transfers between devices, across_cores(): return lax.ppermute(x, 'dp', [(i, i ^ 1) for i in range(dp)])  1.94 us
  transfers between devices with their start and end apart: 27, of which 9 were waited for; matrix products, arithmetic and copies ran while one was open for 0% of the time, Pallas kernels for 34%

profile of v6, /device:TPU:0, one launch (start us, length us, event | category | flops | bytes accessed | tf_op | source)
XLA Modules:
  0.0 64.2 jit_solution(17334149457211920716)
XLA Ops:
  0.6 1.0 %split_width.1 = (bf16[16,3072]{1,0:T(8,128)(2,1)S(1)}, bf16[8,3072]{1,0:T(8,128)(2,1)S(1)}, bf16[8,3072]{1,0:T(8,128)(2,1)S(1)}) custom-call(s32[1]{0:T(128)} %bitcast.1.refs_0_, bf16[8,6144]{1,0:T(8,128)(2,1)} %refs_1_.1, bf16[16,3072]{1,0:T(8,128)(2,1)} %refs_2_.1), custom_call_target="tpu_custom_call" | custom-call | tf_op jit(solution)/shard_map/split_width/pallas_call | solution.py:58
  1.6 3.0 %collective-permute-start = (bf16[8,3072]{1,0:T(8,128)(2,1)S(1)}, bf16[8,3072]{1,0:T(8,128)(2,1)S(1)}, u32[]{:S(2)}, u32[]{:S(2)}) collective-permute-start(bf16[8,3072]{1,0:T(8,128)(2,1)S(1)} %get-tuple-element.36), channel_id=1, source_target_pairs={{0,4},{4,0},{1,5},{5,1},{2,6},{6,2},{3,7},{7,3},{8,12},{12,8},{9,1... | collective-permute-start | bytes 147464 | tf_op jit(solution)/shard_map/ppermute | solution.py:404
  4.6 2.1 %collective-permute-done.refs_1_ = bf16[8,3072]{1,0:T(8,128)(2,1)S(1)} collective-permute-done((bf16[8,3072]{1,0:T(8,128)(2,1)S(1)}, bf16[8,3072]{1,0:T(8,128)(2,1)S(1)}, u32[]{:S(2)}, u32[]{:S(2)}) %collective-permute-start) | collective-permute-done | bytes 49184 | tf_op jit(solution)/shard_map/ppermute | solution.py:404
  6.7 2.2 %collective-permute-start.1 = (bf16[16,3072]{1,0:T(8,128)(2,1)S(1)}, bf16[16,3072]{1,0:T(8,128)(2,1)S(1)}, u32[]{:S(2)}, u32[]{:S(2)}) collective-permute-start(bf16[16,3072]{1,0:T(8,128)(2,1)S(1)} %get-tuple-element.38.refs_2_), channel_id=1, source_target_pairs={{0,1},{1,2},{2,3},{3,0},{4,5},{5,6},{6,7},{7,4},{8,9},{9,10},{10,1... | collective-permute-start | bytes 294920 | tf_op jit(solution)/shard_map/ppermute | solution.py:404
  8.9 2.6 %collective-permute-start.2 = (bf16[16,3072]{1,0:T(8,128)(2,1)S(1)}, bf16[16,3072]{1,0:T(8,128)(2,1)S(1)}, u32[]{:S(2)}, u32[]{:S(2)}) collective-permute-start(bf16[16,3072]{1,0:T(8,128)(2,1)S(1)} %get-tuple-element.38.refs_2_), channel_id=1, source_target_pairs={{0,2},{1,3},{2,0},{3,1},{4,6},{5,7},{6,4},{7,5},{8,10},{9,11},{10,... | collective-permute-start | bytes 294920 | tf_op jit(solution)/shard_map/ppermute | solution.py:404
  11.5 1.3 %collective-permute-start.3 = (bf16[16,3072]{1,0:T(8,128)(2,1)S(1)}, bf16[16,3072]{1,0:T(8,128)(2,1)S(1)}, u32[]{:S(2)}, u32[]{:S(2)}) collective-permute-start(bf16[16,3072]{1,0:T(8,128)(2,1)S(1)} %get-tuple-element.38.refs_2_), channel_id=1, source_target_pairs={{0,3},{1,0},{2,1},{3,2},{4,7},{5,4},{6,5},{7,6},{8,11},{9,8},{10,9... | collective-permute-start | bytes 294920 | tf_op jit(solution)/shard_map/ppermute | solution.py:404
  12.8 3.8 %load_first.1.refs_6_.refs_2_.refs_3_ = bf16[3072,1536]{1,0:T(8,128)(2,1)S(1)} custom-call(s32[1]{0:T(128)} %bitcast.2.refs_0_, bf16[3072,3072]{1,0:T(8,128)(2,1)} %bitcast.7, bf16[16,3072]{1,0:T(8,128)(2,1)S(1)} %get-tuple-element.38.refs_2_), custom_call_target="tpu_custom_call" | custom-call | tf_op jit(solution)/shard_map/load_first/pallas_call | solution.py:58
  17.3 2.3 %collective-permute-start.6 = (bf16[16,3072]{1,0:T(8,128)(2,1)S(1)}, bf16[16,3072]{1,0:T(8,128)(2,1)S(1)}, u32[]{:S(2)}, u32[]{:S(2)}) collective-permute-start(bf16[16,3072]{1,0:T(8,128)(2,1)S(1)} %get-tuple-element.41.refs_1_), channel_id=1, source_target_pairs={{0,1},{1,2},{2,3},{3,0},{4,5},{5,6},{6,7},{7,4},{8,9},{9,10},{10,1... | collective-permute-start | bytes 294920 | tf_op jit(solution)/shard_map/ppermute | solution.py:404
  19.7 1.8 %collective-permute-start.7 = (bf16[16,3072]{1,0:T(8,128)(2,1)S(1)}, bf16[16,3072]{1,0:T(8,128)(2,1)S(1)}, u32[]{:S(2)}, u32[]{:S(2)}) collective-permute-start(bf16[16,3072]{1,0:T(8,128)(2,1)S(1)} %get-tuple-element.41.refs_1_), channel_id=1, source_target_pairs={{0,2},{1,3},{2,0},{3,1},{4,6},{5,7},{6,4},{7,5},{8,10},{9,11},{10,... | collective-permute-start | bytes 294920 | tf_op jit(solution)/shard_map/ppermute | solution.py:404
  21.4 0.7 %collective-permute-start.8 = (bf16[16,3072]{1,0:T(8,128)(2,1)S(1)}, bf16[16,3072]{1,0:T(8,128)(2,1)S(1)}, u32[]{:S(2)}, u32[]{:S(2)}) collective-permute-start(bf16[16,3072]{1,0:T(8,128)(2,1)S(1)} %get-tuple-element.41.refs_1_), channel_id=1, source_target_pairs={{0,3},{1,0},{2,1},{3,2},{4,7},{5,4},{6,5},{7,6},{8,11},{9,8},{10,9... | collective-permute-start | bytes 294920 | tf_op jit(solution)/shard_map/ppermute | solution.py:404
  22.1 1.4 %preact_partial.1 = (f32[128,1536]{1,0:T(8,128)S(1)}, bf16[128,1536]{1,0:T(8,128)(2,1)S(1)}, bf16[64,3072]{1,0:T(8,128)(2,1)S(1)}) custom-call(bf16[64,3072]{1,0:T(8,128)(2,1)S(1)} %order_tokens.1.refs_0_, bf16[64,3072]{1,0:T(8,128)(2,1)S(1)} %collective-permute-done.4.refs_1_, bf16[3072,1536]{1,0:T(8,128)(2,1)S(1)} %load_first.1.refs_6_.refs_2_.refs_3_), custom_call_target="tpu_custom_call" | custom-call | tf_op jit(solution)/shard_map/preact_partial/pallas_call | solution.py:58
  23.5 1.6 %collective-permute-start.5 = (bf16[128,1536]{1,0:T(8,128)(2,1)S(1)}, bf16[128,1536]{1,0:T(8,128)(2,1)S(1)}, u32[]{:S(2)}, u32[]{:S(2)}) collective-permute-start(bf16[128,1536]{1,0:T(8,128)(2,1)S(1)} %get-tuple-element.40.refs_2_), channel_id=1, source_target_pairs={{0,4},{4,0},{1,5},{5,1},{2,6},{6,2},{3,7},{7,3},{8,12},{12,8},{9,1... | collective-permute-start | bytes 1179656 | tf_op jit(solution)/shard_map/ppermute | solution.py:404
  25.1 3.8 %load_second.1.refs_5_.refs_4_.refs_2_ = bf16[1536,3072]{1,0:T(8,128)(2,1)S(1)} custom-call(s32[1]{0:T(128)} %bitcast.2.refs_0_, bf16[3072,3072]{1,0:T(8,128)(2,1)} %bitcast.8, bf16[128,1536]{1,0:T(8,128)(2,1)S(1)} %get-tuple-element.40.refs_2_), custom_call_target="tpu_custom_call" | custom-call | tf_op jit(solution)/shard_map/load_second/pallas_call | solution.py:58
  29.6 1.5 %collective-permute-start.17 = (bf16[64,3072]{1,0:T(8,128)(2,1)S(1)}, bf16[64,3072]{1,0:T(8,128)(2,1)S(1)}, u32[]{:S(2)}, u32[]{:S(2)}) collective-permute-start(bf16[64,3072]{1,0:T(8,128)(2,1)S(1)} %get-tuple-element.55.refs_0_), channel_id=1, source_target_pairs={{0,16},{8,24},{16,0},{24,8},{1,17},{9,25},{17,1},{25,9},{2,18},{10... | collective-permute-start | bytes 1179656 | tf_op jit(solution)/shard_map/ppermute | solution.py:404
  31.1 2.7 %back_partial.1 = (f32[128,1536]{1,0:T(8,128)S(1)}, bf16[128,1536]{1,0:T(8,128)(2,1)S(1)}, bf16[64,3072]{1,0:T(8,128)(2,1)S(1)}) custom-call(bf16[32,3072]{1,0:T(8,128)(2,1)S(1)} %get-tuple-element.42.refs_0_, bf16[32,3072]{1,0:T(8,128)(2,1)S(1)} %get-tuple-element.43.refs_1_, bf16[32,3072]{1,0:T(8,128)(2,1)S(1)} %collective-permute-done.9.refs_2_.refs_3_, ...), custom_call_target="tpu_custom_call" | custom-call | tf_op jit(solution)/shard_map/back_partial/pallas_call | solution.py:58
  33.8 1.4 %collective-permute-start.16 = (bf16[128,1536]{1,0:T(8,128)(2,1)S(1)}, bf16[128,1536]{1,0:T(8,128)(2,1)S(1)}, u32[]{:S(2)}, u32[]{:S(2)}) collective-permute-start(bf16[128,1536]{1,0:T(8,128)(2,1)S(1)} %get-tuple-element.44.refs_3_), channel_id=1, source_target_pairs={{0,4},{4,0},{1,5},{5,1},{2,6},{6,2},{3,7},{7,3},{8,12},{12,8},{9,1... | collective-permute-start | bytes 1179656 | tf_op jit(solution)/shard_map/ppermute | solution.py:404
  35.2 1.2 %collective-permute-start.19 = (bf16[64,3072]{1,0:T(8,128)(2,1)S(1)}, bf16[64,3072]{1,0:T(8,128)(2,1)S(1)}, u32[]{:S(2)}, u32[]{:S(2)}) collective-permute-start(bf16[64,3072]{1,0:T(8,128)(2,1)S(1)} %get-tuple-element.58.refs_2_), channel_id=1, source_target_pairs={{0,16},{8,24},{16,0},{24,8},{1,17},{9,25},{17,1},{25,9},{2,18},{10... | collective-permute-start | bytes 1179656 | tf_op jit(solution)/shard_map/ppermute | solution.py:404
  36.4 1.6 %block_out_partial.1 = (f32[64,3072]{1,0:T(8,128)S(1)}, bf16[32,3072]{1,0:T(8,128)(2,1)S(1)}, bf16[32,3072]{1,0:T(8,128)(2,1)S(1)}, f32[128,1536]{1,0:T(8,128)S(...) custom-call(f32[128,1536]{1,0:T(8,128)S(1)} %get-tuple-element.39.refs_0_, ...), custom_call_target="tpu_custom_call" | custom-call | tf_op jit(solution)/shard_map/block_out_partial/pallas_call | solution.py:58
  38.6 0.9 %collective-permute-done.11.refs_2_ = bf16[32,3072]{1,0:T(8,128)(2,1)S(1)} collective-permute-done((bf16[32,3072]{1,0:T(8,128)(2,1)S(1)}, bf16[32,3072]{1,0:T(8,128)(2,1)S(1)}, u32[]{:S(2)}, u32[]{:S(2)}) %collective-permute-start.11) | collective-permute-done | bytes 196640 | tf_op jit(solution)/shard_map/ppermute | solution.py:407
  40.0 1.7 %collective-permute-start.13 = (bf16[16,3072]{1,0:T(8,128)(2,1)S(1)}, bf16[16,3072]{1,0:T(8,128)(2,1)S(1)}, u32[]{:S(2)}, u32[]{:S(2)}) collective-permute-start(bf16[16,3072]{1,0:T(8,128)(2,1)S(1)} %get-tuple-element.49), channel_id=1, source_target_pairs={{0,2},{1,3},{2,0},{3,1},{4,6},{5,7},{6,4},{7,5},{8,10},{9,11},{10,... | collective-permute-start | bytes 294920 | tf_op jit(solution)/shard_map/ppermute | solution.py:404
  41.6 2.0 %collective-permute-start.14 = (bf16[16,3072]{1,0:T(8,128)(2,1)S(1)}, bf16[16,3072]{1,0:T(8,128)(2,1)S(1)}, u32[]{:S(2)}, u32[]{:S(2)}) collective-permute-start(bf16[16,3072]{1,0:T(8,128)(2,1)S(1)} %get-tuple-element.50), channel_id=1, source_target_pairs={{0,1},{1,2},{2,3},{3,0},{4,5},{5,6},{6,7},{7,4},{8,9},{9,10},{10,1... | collective-permute-start | bytes 294920 | tf_op jit(solution)/shard_map/ppermute | solution.py:404
  43.6 1.8 %collective-permute-start.15 = (bf16[16,3072]{1,0:T(8,128)(2,1)S(1)}, bf16[16,3072]{1,0:T(8,128)(2,1)S(1)}, u32[]{:S(2)}, u32[]{:S(2)}) collective-permute-start(bf16[16,3072]{1,0:T(8,128)(2,1)S(1)} %get-tuple-element.51), channel_id=1, source_target_pairs={{0,3},{1,0},{2,1},{3,2},{4,7},{5,4},{6,5},{7,6},{8,11},{9,8},{10,9... | collective-permute-start | bytes 294920 | tf_op jit(solution)/shard_map/ppermute | solution.py:404
  45.4 2.8 %grad_in_partial.1 = (f32[64,3072]{1,0:T(8,128)S(1)}, bf16[64,3072]{1,0:T(8,128)(2,1)S(1)}, bf16[128,768]{1,0:T(8,128)(2,1)S(1)}, bf16[128,768]{1,0:T(8,128)(2,1)S(1)}, bf16[128,768]{1,0:T(8,128)(2,1)S(1)}) custom-call(f32[128,1536]{1,0:T(8,128)S(1)} %get-tuple-element.52.refs_0_, bf16[128,1536]{1,0:T(8,128)(2,1)S(1)} %collective-permute-done.16.refs_1_, ...), custom_call_target="tpu_custom_call" | custom-call | tf_op jit(solution)/shard_map/grad_in_partial/pallas_call | solution.py:58
  48.2 0.9 %collective-permute-done.19.refs_5_ = bf16[64,3072]{1,0:T(8,128)(2,1)S(1)} collective-permute-done((bf16[64,3072]{1,0:T(8,128)(2,1)S(1)}, bf16[64,3072]{1,0:T(8,128)(2,1)S(1)}, u32[]{:S(2)}, u32[]{:S(2)}) %collective-permute-start.19) | collective-permute-done | bytes 393248 | tf_op jit(solution)/shard_map/ppermute | solution.py:404
  49.1 1.5 %collective-permute-start.26 = (bf16[128,768]{1,0:T(8,128)(2,1)S(1)}, bf16[128,768]{1,0:T(8,128)(2,1)S(1)}, u32[]{:S(2)}, u32[]{:S(2)}) collective-permute-start(bf16[128,768]{1,0:T(8,128)(2,1)S(1)} %get-tuple-element.65), channel_id=1, source_target_pairs={{0,16},{8,24},{16,0},{24,8},{1,17},{9,25},{17,1},{25,9},{2,18},{10... | collective-permute-start | bytes 589832 | tf_op jit(solution)/shard_map/ppermute | solution.py:404
  50.7 0.8 %collective-permute-start.25 = (bf16[128,768]{1,0:T(8,128)(2,1)S(1)}, bf16[128,768]{1,0:T(8,128)(2,1)S(1)}, u32[]{:S(2)}, u32[]{:S(2)}) collective-permute-start(bf16[128,768]{1,0:T(8,128)(2,1)S(1)} %get-tuple-element.63), channel_id=1, source_target_pairs={{0,16},{8,24},{16,0},{24,8},{1,17},{9,25},{17,1},{25,9},{2,18},{10... | collective-permute-start | bytes 589832 | tf_op jit(solution)/shard_map/ppermute | solution.py:404
  51.6 0.7 %collective-permute-done.18.refs_2_ = bf16[64,3072]{1,0:T(8,128)(2,1)S(1)} collective-permute-done((bf16[64,3072]{1,0:T(8,128)(2,1)S(1)}, bf16[64,3072]{1,0:T(8,128)(2,1)S(1)}, u32[]{:S(2)}, u32[]{:S(2)}) %collective-permute-start.18) | collective-permute-done | bytes 393248 | tf_op jit(solution)/shard_map/ppermute | solution.py:407
  52.4 2.5 %collective-permute-start.23 = (bf16[16,3072]{1,0:T(8,128)(2,1)S(1)}, bf16[16,3072]{1,0:T(8,128)(2,1)S(1)}, u32[]{:S(2)}, u32[]{:S(2)}) collective-permute-start(bf16[16,3072]{1,0:T(8,128)(2,1)S(1)} %grad_in_ahead.1), channel_id=1, source_target_pairs={{0,1},{1,2},{2,3},{3,0},{4,5},{5,6},{6,7},{7,4},{8,9},{9,10},{10,1... | collective-permute-start | bytes 294920 | tf_op jit(solution)/shard_map/ppermute | solution.py:404
  55.0 1.5 %collective-permute-start.22 = (bf16[16,3072]{1,0:T(8,128)(2,1)S(1)}, bf16[16,3072]{1,0:T(8,128)(2,1)S(1)}, u32[]{:S(2)}, u32[]{:S(2)}) collective-permute-start(bf16[16,3072]{1,0:T(8,128)(2,1)S(1)} %get-tuple-element.60), channel_id=1, source_target_pairs={{0,2},{1,3},{2,0},{3,1},{4,6},{5,7},{6,4},{7,5},{8,10},{9,11},{10,... | collective-permute-start | bytes 294920 | tf_op jit(solution)/shard_map/ppermute | solution.py:404
  56.6 1.5 %collective-permute-start.24 = (bf16[16,3072]{1,0:T(8,128)(2,1)S(1)}, bf16[16,3072]{1,0:T(8,128)(2,1)S(1)}, u32[]{:S(2)}, u32[]{:S(2)}) collective-permute-start(bf16[16,3072]{1,0:T(8,128)(2,1)S(1)} %get-tuple-element.61), channel_id=1, source_target_pairs={{0,3},{1,0},{2,1},{3,2},{4,7},{5,4},{6,5},{7,6},{8,11},{9,8},{10,9... | collective-permute-start | bytes 294920 | tf_op jit(solution)/shard_map/ppermute | solution.py:404
  58.0 2.6 %grad_w_out.1 = bf16[768,3072]{1,0:T(8,128)(2,1)} custom-call(bf16[128,768]{1,0:T(8,128)(2,1)S(1)} %get-tuple-element.64.refs_0_, bf16[128,768]{1,0:T(8,128)(2,1)S(1)} %collective-permute-done.26.refs_1_, bf16[64,3072]{1,0:T(8,128)(2,1)S(1)} %get-tuple-element.58.refs_2_, bf16[32,3072]{1,0:T(8,128)(2,1)S(1)} %collective-permute-done.9.refs_2_.refs_3_, ...), custom_call_target="tpu_custom_call" | custom-call | tf_op jit(solution)/shard_map/grad_w_out/pallas_call | solution.py:58
  60.7 2.7 %grad_w_in.1 = bf16[3072,768]{1,0:T(8,128)(2,1)} custom-call(bf16[64,3072]{1,0:T(8,128)(2,1)S(1)} %get-tuple-element.55.refs_0_, bf16[64,3072]{1,0:T(8,128)(2,1)S(1)} %collective-permute-done.4.refs_1_, bf16[64,3072]{1,0:T(8,128)(2,1)S(1)} %collective-permute-done.17.refs_6_.refs_2_, bf16[64,3072]{1,0:T(8,128)(2,1)S(1)} %collective-permute-done.21.refs_5_.refs_3_, ...), custom_call_target="tpu_custom_call" | custom-call | tf_op jit(solution)/shard_map/grad_w_in/pallas_call | solution.py:58
  (41 shorter events, 3.5 us)
Async XLA Ops:
  1.6 5.1 %collective-permute-start = (bf16[8,3072]{1,0:T(8,128)(2,1)S(1)}, bf16[8,3072]{1,0:T(8,128)(2,1)S(1)}, u32[]{:S(2)}, u32[]{:S(2)}) collective-permute-start(bf16[8,3072]{1,0:T(8,128)(2,1)S(1)} %get-tuple-element.36), channel_id=1, source_target_pairs={{0,4},{4,0},{1,5},{5,1},{2,6},{6,2},{3,7},{7,3},{8,12},{12,8},{9,1... | collective-permute-start | bytes 147464 | tf_op jit(solution)/shard_map/ppermute | solution.py:404
  6.7 9.9 %collective-permute-start.1 = (bf16[16,3072]{1,0:T(8,128)(2,1)S(1)}, bf16[16,3072]{1,0:T(8,128)(2,1)S(1)}, u32[]{:S(2)}, u32[]{:S(2)}) collective-permute-start(bf16[16,3072]{1,0:T(8,128)(2,1)S(1)} %get-tuple-element.38.refs_2_), channel_id=1, source_target_pairs={{0,1},{1,2},{2,3},{3,0},{4,5},{5,6},{6,7},{7,4},{8,9},{9,10},{10,1... | collective-permute-start | bytes 294920 | tf_op jit(solution)/shard_map/ppermute | solution.py:404
  8.9 8.2 %collective-permute-start.2 = (bf16[16,3072]{1,0:T(8,128)(2,1)S(1)}, bf16[16,3072]{1,0:T(8,128)(2,1)S(1)}, u32[]{:S(2)}, u32[]{:S(2)}) collective-permute-start(bf16[16,3072]{1,0:T(8,128)(2,1)S(1)} %get-tuple-element.38.refs_2_), channel_id=1, source_target_pairs={{0,2},{1,3},{2,0},{3,1},{4,6},{5,7},{6,4},{7,5},{8,10},{9,11},{10,... | collective-permute-start | bytes 294920 | tf_op jit(solution)/shard_map/ppermute | solution.py:404
  11.5 5.7 %collective-permute-start.3 = (bf16[16,3072]{1,0:T(8,128)(2,1)S(1)}, bf16[16,3072]{1,0:T(8,128)(2,1)S(1)}, u32[]{:S(2)}, u32[]{:S(2)}) collective-permute-start(bf16[16,3072]{1,0:T(8,128)(2,1)S(1)} %get-tuple-element.38.refs_2_), channel_id=1, source_target_pairs={{0,3},{1,0},{2,1},{3,2},{4,7},{5,4},{6,5},{7,6},{8,11},{9,8},{10,9... | collective-permute-start | bytes 294920 | tf_op jit(solution)/shard_map/ppermute | solution.py:404
  17.3 4.9 %collective-permute-start.4 = (bf16[64,3072]{1,0:T(8,128)(2,1)S(1)}, bf16[64,3072]{1,0:T(8,128)(2,1)S(1)}, u32[]{:S(2)}, u32[]{:S(2)}) collective-permute-start(bf16[64,3072]{1,0:T(8,128)(2,1)S(1)} %order_tokens.1.refs_0_), channel_id=1, source_target_pairs={{0,8},{8,0},{16,24},{24,16},{1,9},{9,1},{17,25},{25,17},{2,10},{10... | collective-permute-start | bytes 1179656 | tf_op jit(solution)/shard_map/ppermute | solution.py:407
  17.3 11.6 %collective-permute-start.6 = (bf16[16,3072]{1,0:T(8,128)(2,1)S(1)}, bf16[16,3072]{1,0:T(8,128)(2,1)S(1)}, u32[]{:S(2)}, u32[]{:S(2)}) collective-permute-start(bf16[16,3072]{1,0:T(8,128)(2,1)S(1)} %get-tuple-element.41.refs_1_), channel_id=1, source_target_pairs={{0,1},{1,2},{2,3},{3,0},{4,5},{5,6},{6,7},{7,4},{8,9},{9,10},{10,1... | collective-permute-start | bytes 294920 | tf_op jit(solution)/shard_map/ppermute | solution.py:404
  19.7 9.2 %collective-permute-start.7 = (bf16[16,3072]{1,0:T(8,128)(2,1)S(1)}, bf16[16,3072]{1,0:T(8,128)(2,1)S(1)}, u32[]{:S(2)}, u32[]{:S(2)}) collective-permute-start(bf16[16,3072]{1,0:T(8,128)(2,1)S(1)} %get-tuple-element.41.refs_1_), channel_id=1, source_target_pairs={{0,2},{1,3},{2,0},{3,1},{4,6},{5,7},{6,4},{7,5},{8,10},{9,11},{10,... | collective-permute-start | bytes 294920 | tf_op jit(solution)/shard_map/ppermute | solution.py:404
  21.4 7.5 %collective-permute-start.8 = (bf16[16,3072]{1,0:T(8,128)(2,1)S(1)}, bf16[16,3072]{1,0:T(8,128)(2,1)S(1)}, u32[]{:S(2)}, u32[]{:S(2)}) collective-permute-start(bf16[16,3072]{1,0:T(8,128)(2,1)S(1)} %get-tuple-element.41.refs_1_), channel_id=1, source_target_pairs={{0,3},{1,0},{2,1},{3,2},{4,7},{5,4},{6,5},{7,6},{8,11},{9,8},{10,9... | collective-permute-start | bytes 294920 | tf_op jit(solution)/shard_map/ppermute | solution.py:404
  23.5 12.8 %collective-permute-start.5 = (bf16[128,1536]{1,0:T(8,128)(2,1)S(1)}, bf16[128,1536]{1,0:T(8,128)(2,1)S(1)}, u32[]{:S(2)}, u32[]{:S(2)}) collective-permute-start(bf16[128,1536]{1,0:T(8,128)(2,1)S(1)} %get-tuple-element.40.refs_2_), channel_id=1, source_target_pairs={{0,4},{4,0},{1,5},{5,1},{2,6},{6,2},{3,7},{7,3},{8,12},{12,8},{9,1... | collective-permute-start | bytes 1179656 | tf_op jit(solution)/shard_map/ppermute | solution.py:404
  29.0 2.1 %collective-permute-start.10 = (bf16[32,3072]{1,0:T(8,128)(2,1)S(1)}, bf16[32,3072]{1,0:T(8,128)(2,1)S(1)}, u32[]{:S(2)}, u32[]{:S(2)}) collective-permute-start(bf16[32,3072]{1,0:T(8,128)(2,1)S(1)} %get-tuple-element.43.refs_1_), channel_id=1, source_target_pairs={{0,8},{8,0},{16,24},{24,16},{1,9},{9,1},{17,25},{25,17},{2,10},{10... | collective-permute-start | bytes 589832 | tf_op jit(solution)/shard_map/ppermute | solution.py:407
  29.1 2.0 %collective-permute-start.9 = (bf16[32,3072]{1,0:T(8,128)(2,1)S(1)}, bf16[32,3072]{1,0:T(8,128)(2,1)S(1)}, u32[]{:S(2)}, u32[]{:S(2)}) collective-permute-start(bf16[32,3072]{1,0:T(8,128)(2,1)S(1)} %get-tuple-element.42.refs_0_), channel_id=1, source_target_pairs={{0,8},{8,0},{16,24},{24,16},{1,9},{9,1},{17,25},{25,17},{2,10},{10... | collective-permute-start | bytes 589832 | tf_op jit(solution)/shard_map/ppermute | solution.py:407
  29.6 14.0 %collective-permute-start.17 = (bf16[64,3072]{1,0:T(8,128)(2,1)S(1)}, bf16[64,3072]{1,0:T(8,128)(2,1)S(1)}, u32[]{:S(2)}, u32[]{:S(2)}) collective-permute-start(bf16[64,3072]{1,0:T(8,128)(2,1)S(1)} %get-tuple-element.55.refs_0_), channel_id=1, source_target_pairs={{0,16},{8,24},{16,0},{24,8},{1,17},{9,25},{17,1},{25,9},{2,18},{10... | collective-permute-start | bytes 1179656 | tf_op jit(solution)/shard_map/ppermute | solution.py:404
  33.8 11.6 %collective-permute-start.16 = (bf16[128,1536]{1,0:T(8,128)(2,1)S(1)}, bf16[128,1536]{1,0:T(8,128)(2,1)S(1)}, u32[]{:S(2)}, u32[]{:S(2)}) collective-permute-start(bf16[128,1536]{1,0:T(8,128)(2,1)S(1)} %get-tuple-element.44.refs_3_), channel_id=1, source_target_pairs={{0,4},{4,0},{1,5},{5,1},{2,6},{6,2},{3,7},{7,3},{8,12},{12,8},{9,1... | collective-permute-start | bytes 1179656 | tf_op jit(solution)/shard_map/ppermute | solution.py:404
  35.2 13.9 %collective-permute-start.19 = (bf16[64,3072]{1,0:T(8,128)(2,1)S(1)}, bf16[64,3072]{1,0:T(8,128)(2,1)S(1)}, u32[]{:S(2)}, u32[]{:S(2)}) collective-permute-start(bf16[64,3072]{1,0:T(8,128)(2,1)S(1)} %get-tuple-element.58.refs_2_), channel_id=1, source_target_pairs={{0,16},{8,24},{16,0},{24,8},{1,17},{9,25},{17,1},{25,9},{2,18},{10... | collective-permute-start | bytes 1179656 | tf_op jit(solution)/shard_map/ppermute | solution.py:404
  38.0 1.5 %collective-permute-start.11 = (bf16[32,3072]{1,0:T(8,128)(2,1)S(1)}, bf16[32,3072]{1,0:T(8,128)(2,1)S(1)}, u32[]{:S(2)}, u32[]{:S(2)}) collective-permute-start(bf16[32,3072]{1,0:T(8,128)(2,1)S(1)} %get-tuple-element.46), channel_id=1, source_target_pairs={{0,8},{8,0},{16,24},{24,16},{1,9},{9,1},{17,25},{25,17},{2,10},{10... | collective-permute-start | bytes 589832 | tf_op jit(solution)/shard_map/ppermute | solution.py:407
  38.1 1.7 %collective-permute-start.12 = (bf16[32,3072]{1,0:T(8,128)(2,1)S(1)}, bf16[32,3072]{1,0:T(8,128)(2,1)S(1)}, u32[]{:S(2)}, u32[]{:S(2)}) collective-permute-start(bf16[32,3072]{1,0:T(8,128)(2,1)S(1)} %get-tuple-element.47), channel_id=1, source_target_pairs={{0,8},{8,0},{16,24},{24,16},{1,9},{9,1},{17,25},{25,17},{2,10},{10... | collective-permute-start | bytes 589832 | tf_op jit(solution)/shard_map/ppermute | solution.py:407
  40.0 10.7 %collective-permute-start.13 = (bf16[16,3072]{1,0:T(8,128)(2,1)S(1)}, bf16[16,3072]{1,0:T(8,128)(2,1)S(1)}, u32[]{:S(2)}, u32[]{:S(2)}) collective-permute-start(bf16[16,3072]{1,0:T(8,128)(2,1)S(1)} %get-tuple-element.49), channel_id=1, source_target_pairs={{0,2},{1,3},{2,0},{3,1},{4,6},{5,7},{6,4},{7,5},{8,10},{9,11},{10,... | collective-permute-start | bytes 294920 | tf_op jit(solution)/shard_map/ppermute | solution.py:404
  41.6 9.1 %collective-permute-start.14 = (bf16[16,3072]{1,0:T(8,128)(2,1)S(1)}, bf16[16,3072]{1,0:T(8,128)(2,1)S(1)}, u32[]{:S(2)}, u32[]{:S(2)}) collective-permute-start(bf16[16,3072]{1,0:T(8,128)(2,1)S(1)} %get-tuple-element.50), channel_id=1, source_target_pairs={{0,1},{1,2},{2,3},{3,0},{4,5},{5,6},{6,7},{7,4},{8,9},{9,10},{10,1... | collective-permute-start | bytes 294920 | tf_op jit(solution)/shard_map/ppermute | solution.py:404
  43.6 7.9 %collective-permute-start.15 = (bf16[16,3072]{1,0:T(8,128)(2,1)S(1)}, bf16[16,3072]{1,0:T(8,128)(2,1)S(1)}, u32[]{:S(2)}, u32[]{:S(2)}) collective-permute-start(bf16[16,3072]{1,0:T(8,128)(2,1)S(1)} %get-tuple-element.51), channel_id=1, source_target_pairs={{0,3},{1,0},{2,1},{3,2},{4,7},{5,4},{6,5},{7,6},{8,11},{9,8},{10,9... | collective-permute-start | bytes 294920 | tf_op jit(solution)/shard_map/ppermute | solution.py:404
  45.4 9.5 %collective-permute-start.21 = (bf16[64,3072]{1,0:T(8,128)(2,1)S(1)}, bf16[64,3072]{1,0:T(8,128)(2,1)S(1)}, u32[]{:S(2)}, u32[]{:S(2)}) collective-permute-start(bf16[64,3072]{1,0:T(8,128)(2,1)S(1)} %collective-permute-done.17.refs_6_.refs_2_), channel_id=1, source_target_pairs={{0,8},{8,0},{16,24},{24,16},{1,9},{9,1},{17,25},{25,17},{2,10},{10... | collective-permute-start | bytes 1179656 | tf_op jit(solution)/shard_map/ppermute | solution.py:407
  49.1 8.9 %collective-permute-start.26 = (bf16[128,768]{1,0:T(8,128)(2,1)S(1)}, bf16[128,768]{1,0:T(8,128)(2,1)S(1)}, u32[]{:S(2)}, u32[]{:S(2)}) collective-permute-start(bf16[128,768]{1,0:T(8,128)(2,1)S(1)} %get-tuple-element.65), channel_id=1, source_target_pairs={{0,16},{8,24},{16,0},{24,8},{1,17},{9,25},{17,1},{25,9},{2,18},{10... | collective-permute-start | bytes 589832 | tf_op jit(solution)/shard_map/ppermute | solution.py:404
  50.6 1.7 %collective-permute-start.18 = (bf16[64,3072]{1,0:T(8,128)(2,1)S(1)}, bf16[64,3072]{1,0:T(8,128)(2,1)S(1)}, u32[]{:S(2)}, u32[]{:S(2)}) collective-permute-start(bf16[64,3072]{1,0:T(8,128)(2,1)S(1)} %get-tuple-element.57), channel_id=1, source_target_pairs={{0,8},{8,0},{16,24},{24,16},{1,9},{9,1},{17,25},{25,17},{2,10},{10... | collective-permute-start | bytes 1179656 | tf_op jit(solution)/shard_map/ppermute | solution.py:407
  50.7 9.9 %collective-permute-start.25 = (bf16[128,768]{1,0:T(8,128)(2,1)S(1)}, bf16[128,768]{1,0:T(8,128)(2,1)S(1)}, u32[]{:S(2)}, u32[]{:S(2)}) collective-permute-start(bf16[128,768]{1,0:T(8,128)(2,1)S(1)} %get-tuple-element.63), channel_id=1, source_target_pairs={{0,16},{8,24},{16,0},{24,8},{1,17},{9,25},{17,1},{25,9},{2,18},{10... | collective-permute-start | bytes 589832 | tf_op jit(solution)/shard_map/ppermute | solution.py:404
  51.5 3.4 %collective-permute-start.20 = (bf16[64,3072]{1,0:T(8,128)(2,1)S(1)}, bf16[64,3072]{1,0:T(8,128)(2,1)S(1)}, u32[]{:S(2)}, u32[]{:S(2)}) collective-permute-start(bf16[64,3072]{1,0:T(8,128)(2,1)S(1)} %collective-permute-done.19.refs_5_), channel_id=1, source_target_pairs={{0,8},{8,0},{16,24},{24,16},{1,9},{9,1},{17,25},{25,17},{2,10},{10... | collective-permute-start | bytes 1179656 | tf_op jit(solution)/shard_map/ppermute | solution.py:407
  51.6 12.5 %copy-start = (bf16[16,3072]{1,0:T(8,128)(2,1)}, bf16[16,3072]{1,0:T(8,128)(2,1)S(1)}, u32[]{:S(2)}) copy-start(bf16[16,3072]{1,0:T(8,128)(2,1)S(1)} %add_convert_fusion.1.refs_3_) | copy-start | bytes 294916
  52.4 10.9 %collective-permute-start.23 = (bf16[16,3072]{1,0:T(8,128)(2,1)S(1)}, bf16[16,3072]{1,0:T(8,128)(2,1)S(1)}, u32[]{:S(2)}, u32[]{:S(2)}) collective-permute-start(bf16[16,3072]{1,0:T(8,128)(2,1)S(1)} %grad_in_ahead.1), channel_id=1, source_target_pairs={{0,1},{1,2},{2,3},{3,0},{4,5},{5,6},{6,7},{7,4},{8,9},{9,10},{10,1... | collective-permute-start | bytes 294920 | tf_op jit(solution)/shard_map/ppermute | solution.py:404
  55.0 8.4 %collective-permute-start.22 = (bf16[16,3072]{1,0:T(8,128)(2,1)S(1)}, bf16[16,3072]{1,0:T(8,128)(2,1)S(1)}, u32[]{:S(2)}, u32[]{:S(2)}) collective-permute-start(bf16[16,3072]{1,0:T(8,128)(2,1)S(1)} %get-tuple-element.60), channel_id=1, source_target_pairs={{0,2},{1,3},{2,0},{3,1},{4,6},{5,7},{6,4},{7,5},{8,10},{9,11},{10,... | collective-permute-start | bytes 294920 | tf_op jit(solution)/shard_map/ppermute | solution.py:404
  56.6 6.9 %collective-permute-start.24 = (bf16[16,3072]{1,0:T(8,128)(2,1)S(1)}, bf16[16,3072]{1,0:T(8,128)(2,1)S(1)}, u32[]{:S(2)}, u32[]{:S(2)}) collective-permute-start(bf16[16,3072]{1,0:T(8,128)(2,1)S(1)} %get-tuple-element.61), channel_id=1, source_target_pairs={{0,3},{1,0},{2,1},{3,2},{4,7},{5,4},{6,5},{7,6},{8,11},{9,8},{10,9... | collective-permute-start | bytes 294920 | tf_op jit(solution)/shard_map/ppermute | solution.py:404

commit v7 on v6

--- a/solution.py
+++ b/solution.py
@@ -234,7 +234,7 @@
 
 def second_product(dims, vals, w, keep, sends):
     half, width = keep.shape
-    tile = tile_of(width, 512)
+    tile = tile_of(width, 1024)
     for at in range(0, width, tile):
         cut = slice(at, at + tile)
         if dims is NN:

time: 64.3 us -> 64.3 us (level)
  no operation moved by 1% of the time
where the time goes in v7:
time: 64.3 us; the launch traced here: 64.2 us
  starting transfers between devices  34 us (53%)
  Pallas kernels  22.9 us (36%)
  waiting for transfers between devices  5.64 us (9%)
  between operations  0.84 us (1%)
  other arithmetic  0.74 us (1%)
    ppermute x19, starting transfers between devices, shifted(): lax.ppermute(x, axis, [(i, (i + step) % count) for i in range(count)])  32.8 us
    pallas_call x15, Pallas kernels, call(): return lambda *args: kernel_call(*args, *after)  22.9 us
    ppermute x19, waiting for transfers between devices, shifted(): lax.ppermute(x, axis, [(i, (i + step) % count) for i in range(count)])  3.7 us
    ppermute x8, waiting for transfers between devices, across_cores(): return lax.ppermute(x, 'dp', [(i, i ^ 1) for i in range(dp)])  1.94 us
  transfers between devices with their start and end apart: 27, of which 9 were waited for; matrix products, arithmetic and copies ran while one was open for 0% of the time, Pallas kernels for 34%

profile of v7, /device:TPU:0, one launch (start us, length us, event | category | flops | bytes accessed | tf_op | source)
XLA Modules:
  0.0 64.2 jit_solution(2590583656945618779)
XLA Ops:
  0.6 1.0 %split_width.1 = (bf16[16,3072]{1,0:T(8,128)(2,1)S(1)}, bf16[8,3072]{1,0:T(8,128)(2,1)S(1)}, bf16[8,3072]{1,0:T(8,128)(2,1)S(1)}) custom-call(s32[1]{0:T(128)} %bitcast.1.refs_0_, bf16[8,6144]{1,0:T(8,128)(2,1)} %refs_1_.1, bf16[16,3072]{1,0:T(8,128)(2,1)} %refs_2_.1), custom_call_target="tpu_custom_call" | custom-call | tf_op jit(solution)/shard_map/split_width/pallas_call | solution.py:58
  1.6 3.0 %collective-permute-start = (bf16[8,3072]{1,0:T(8,128)(2,1)S(1)}, bf16[8,3072]{1,0:T(8,128)(2,1)S(1)}, u32[]{:S(2)}, u32[]{:S(2)}) collective-permute-start(bf16[8,3072]{1,0:T(8,128)(2,1)S(1)} %get-tuple-element.36), channel_id=1, source_target_pairs={{0,4},{4,0},{1,5},{5,1},{2,6},{6,2},{3,7},{7,3},{8,12},{12,8},{9,1... | collective-permute-start | bytes 147464 | tf_op jit(solution)/shard_map/ppermute | solution.py:404
  4.6 2.1 %collective-permute-done.refs_1_ = bf16[8,3072]{1,0:T(8,128)(2,1)S(1)} collective-permute-done((bf16[8,3072]{1,0:T(8,128)(2,1)S(1)}, bf16[8,3072]{1,0:T(8,128)(2,1)S(1)}, u32[]{:S(2)}, u32[]{:S(2)}) %collective-permute-start) | collective-permute-done | bytes 49184 | tf_op jit(solution)/shard_map/ppermute | solution.py:404
  6.7 2.2 %collective-permute-start.1 = (bf16[16,3072]{1,0:T(8,128)(2,1)S(1)}, bf16[16,3072]{1,0:T(8,128)(2,1)S(1)}, u32[]{:S(2)}, u32[]{:S(2)}) collective-permute-start(bf16[16,3072]{1,0:T(8,128)(2,1)S(1)} %get-tuple-element.38.refs_2_), channel_id=1, source_target_pairs={{0,1},{1,2},{2,3},{3,0},{4,5},{5,6},{6,7},{7,4},{8,9},{9,10},{10,1... | collective-permute-start | bytes 294920 | tf_op jit(solution)/shard_map/ppermute | solution.py:404
  8.9 2.6 %collective-permute-start.2 = (bf16[16,3072]{1,0:T(8,128)(2,1)S(1)}, bf16[16,3072]{1,0:T(8,128)(2,1)S(1)}, u32[]{:S(2)}, u32[]{:S(2)}) collective-permute-start(bf16[16,3072]{1,0:T(8,128)(2,1)S(1)} %get-tuple-element.38.refs_2_), channel_id=1, source_target_pairs={{0,2},{1,3},{2,0},{3,1},{4,6},{5,7},{6,4},{7,5},{8,10},{9,11},{10,... | collective-permute-start | bytes 294920 | tf_op jit(solution)/shard_map/ppermute | solution.py:404
  11.5 1.3 %collective-permute-start.3 = (bf16[16,3072]{1,0:T(8,128)(2,1)S(1)}, bf16[16,3072]{1,0:T(8,128)(2,1)S(1)}, u32[]{:S(2)}, u32[]{:S(2)}) collective-permute-start(bf16[16,3072]{1,0:T(8,128)(2,1)S(1)} %get-tuple-element.38.refs_2_), channel_id=1, source_target_pairs={{0,3},{1,0},{2,1},{3,2},{4,7},{5,4},{6,5},{7,6},{8,11},{9,8},{10,9... | collective-permute-start | bytes 294920 | tf_op jit(solution)/shard_map/ppermute | solution.py:404
  12.8 3.8 %load_first.1.refs_6_.refs_2_.refs_3_ = bf16[3072,1536]{1,0:T(8,128)(2,1)S(1)} custom-call(s32[1]{0:T(128)} %bitcast.2.refs_0_, bf16[3072,3072]{1,0:T(8,128)(2,1)} %bitcast.7, bf16[16,3072]{1,0:T(8,128)(2,1)S(1)} %get-tuple-element.38.refs_2_), custom_call_target="tpu_custom_call" | custom-call | tf_op jit(solution)/shard_map/load_first/pallas_call | solution.py:58
  17.3 2.3 %collective-permute-start.6 = (bf16[16,3072]{1,0:T(8,128)(2,1)S(1)}, bf16[16,3072]{1,0:T(8,128)(2,1)S(1)}, u32[]{:S(2)}, u32[]{:S(2)}) collective-permute-start(bf16[16,3072]{1,0:T(8,128)(2,1)S(1)} %get-tuple-element.41.refs_1_), channel_id=1, source_target_pairs={{0,1},{1,2},{2,3},{3,0},{4,5},{5,6},{6,7},{7,4},{8,9},{9,10},{10,1... | collective-permute-start | bytes 294920 | tf_op jit(solution)/shard_map/ppermute | solution.py:404
  19.7 1.8 %collective-permute-start.7 = (bf16[16,3072]{1,0:T(8,128)(2,1)S(1)}, bf16[16,3072]{1,0:T(8,128)(2,1)S(1)}, u32[]{:S(2)}, u32[]{:S(2)}) collective-permute-start(bf16[16,3072]{1,0:T(8,128)(2,1)S(1)} %get-tuple-element.41.refs_1_), channel_id=1, source_target_pairs={{0,2},{1,3},{2,0},{3,1},{4,6},{5,7},{6,4},{7,5},{8,10},{9,11},{10,... | collective-permute-start | bytes 294920 | tf_op jit(solution)/shard_map/ppermute | solution.py:404
  21.4 0.7 %collective-permute-start.8 = (bf16[16,3072]{1,0:T(8,128)(2,1)S(1)}, bf16[16,3072]{1,0:T(8,128)(2,1)S(1)}, u32[]{:S(2)}, u32[]{:S(2)}) collective-permute-start(bf16[16,3072]{1,0:T(8,128)(2,1)S(1)} %get-tuple-element.41.refs_1_), channel_id=1, source_target_pairs={{0,3},{1,0},{2,1},{3,2},{4,7},{5,4},{6,5},{7,6},{8,11},{9,8},{10,9... | collective-permute-start | bytes 294920 | tf_op jit(solution)/shard_map/ppermute | solution.py:404
  22.1 1.4 %preact_partial.1 = (f32[128,1536]{1,0:T(8,128)S(1)}, bf16[128,1536]{1,0:T(8,128)(2,1)S(1)}, bf16[64,3072]{1,0:T(8,128)(2,1)S(1)}) custom-call(bf16[64,3072]{1,0:T(8,128)(2,1)S(1)} %order_tokens.1.refs_0_, bf16[64,3072]{1,0:T(8,128)(2,1)S(1)} %collective-permute-done.4.refs_1_, bf16[3072,1536]{1,0:T(8,128)(2,1)S(1)} %load_first.1.refs_6_.refs_2_.refs_3_), custom_call_target="tpu_custom_call" | custom-call | tf_op jit(solution)/shard_map/preact_partial/pallas_call | solution.py:58
  23.5 1.6 %collective-permute-start.5 = (bf16[128,1536]{1,0:T(8,128)(2,1)S(1)}, bf16[128,1536]{1,0:T(8,128)(2,1)S(1)}, u32[]{:S(2)}, u32[]{:S(2)}) collective-permute-start(bf16[128,1536]{1,0:T(8,128)(2,1)S(1)} %get-tuple-element.40.refs_2_), channel_id=1, source_target_pairs={{0,4},{4,0},{1,5},{5,1},{2,6},{6,2},{3,7},{7,3},{8,12},{12,8},{9,1... | collective-permute-start | bytes 1179656 | tf_op jit(solution)/shard_map/ppermute | solution.py:404
  25.1 3.8 %load_second.1.refs_5_.refs_4_.refs_2_ = bf16[1536,3072]{1,0:T(8,128)(2,1)S(1)} custom-call(s32[1]{0:T(128)} %bitcast.2.refs_0_, bf16[3072,3072]{1,0:T(8,128)(2,1)} %bitcast.8, bf16[128,1536]{1,0:T(8,128)(2,1)S(1)} %get-tuple-element.40.refs_2_), custom_call_target="tpu_custom_call" | custom-call | tf_op jit(solution)/shard_map/load_second/pallas_call | solution.py:58
  29.6 1.5 %collective-permute-start.17 = (bf16[64,3072]{1,0:T(8,128)(2,1)S(1)}, bf16[64,3072]{1,0:T(8,128)(2,1)S(1)}, u32[]{:S(2)}, u32[]{:S(2)}) collective-permute-start(bf16[64,3072]{1,0:T(8,128)(2,1)S(1)} %get-tuple-element.55.refs_0_), channel_id=1, source_target_pairs={{0,16},{8,24},{16,0},{24,8},{1,17},{9,25},{17,1},{25,9},{2,18},{10... | collective-permute-start | bytes 1179656 | tf_op jit(solution)/shard_map/ppermute | solution.py:404
  31.1 2.7 %back_partial.1 = (f32[128,1536]{1,0:T(8,128)S(1)}, bf16[128,1536]{1,0:T(8,128)(2,1)S(1)}, bf16[64,3072]{1,0:T(8,128)(2,1)S(1)}) custom-call(bf16[32,3072]{1,0:T(8,128)(2,1)S(1)} %get-tuple-element.42.refs_0_, bf16[32,3072]{1,0:T(8,128)(2,1)S(1)} %get-tuple-element.43.refs_1_, bf16[32,3072]{1,0:T(8,128)(2,1)S(1)} %collective-permute-done.9.refs_2_.refs_3_, ...), custom_call_target="tpu_custom_call" | custom-call | tf_op jit(solution)/shard_map/back_partial/pallas_call | solution.py:58
  33.8 1.4 %collective-permute-start.16 = (bf16[128,1536]{1,0:T(8,128)(2,1)S(1)}, bf16[128,1536]{1,0:T(8,128)(2,1)S(1)}, u32[]{:S(2)}, u32[]{:S(2)}) collective-permute-start(bf16[128,1536]{1,0:T(8,128)(2,1)S(1)} %get-tuple-element.44.refs_3_), channel_id=1, source_target_pairs={{0,4},{4,0},{1,5},{5,1},{2,6},{6,2},{3,7},{7,3},{8,12},{12,8},{9,1... | collective-permute-start | bytes 1179656 | tf_op jit(solution)/shard_map/ppermute | solution.py:404
  35.2 1.2 %collective-permute-start.19 = (bf16[64,3072]{1,0:T(8,128)(2,1)S(1)}, bf16[64,3072]{1,0:T(8,128)(2,1)S(1)}, u32[]{:S(2)}, u32[]{:S(2)}) collective-permute-start(bf16[64,3072]{1,0:T(8,128)(2,1)S(1)} %get-tuple-element.58.refs_2_), channel_id=1, source_target_pairs={{0,16},{8,24},{16,0},{24,8},{1,17},{9,25},{17,1},{25,9},{2,18},{10... | collective-permute-start | bytes 1179656 | tf_op jit(solution)/shard_map/ppermute | solution.py:404
  36.4 1.6 %block_out_partial.1 = (f32[64,3072]{1,0:T(8,128)S(1)}, bf16[32,3072]{1,0:T(8,128)(2,1)S(1)}, bf16[32,3072]{1,0:T(8,128)(2,1)S(1)}, f32[128,1536]{1,0:T(8,128)S(...) custom-call(f32[128,1536]{1,0:T(8,128)S(1)} %get-tuple-element.39.refs_0_, ...), custom_call_target="tpu_custom_call" | custom-call | tf_op jit(solution)/shard_map/block_out_partial/pallas_call | solution.py:58
  38.6 0.9 %collective-permute-done.11.refs_2_ = bf16[32,3072]{1,0:T(8,128)(2,1)S(1)} collective-permute-done((bf16[32,3072]{1,0:T(8,128)(2,1)S(1)}, bf16[32,3072]{1,0:T(8,128)(2,1)S(1)}, u32[]{:S(2)}, u32[]{:S(2)}) %collective-permute-start.11) | collective-permute-done | bytes 196640 | tf_op jit(solution)/shard_map/ppermute | solution.py:407
  40.0 1.7 %collective-permute-start.13 = (bf16[16,3072]{1,0:T(8,128)(2,1)S(1)}, bf16[16,3072]{1,0:T(8,128)(2,1)S(1)}, u32[]{:S(2)}, u32[]{:S(2)}) collective-permute-start(bf16[16,3072]{1,0:T(8,128)(2,1)S(1)} %get-tuple-element.49), channel_id=1, source_target_pairs={{0,2},{1,3},{2,0},{3,1},{4,6},{5,7},{6,4},{7,5},{8,10},{9,11},{10,... | collective-permute-start | bytes 294920 | tf_op jit(solution)/shard_map/ppermute | solution.py:404
  41.6 2.0 %collective-permute-start.14 = (bf16[16,3072]{1,0:T(8,128)(2,1)S(1)}, bf16[16,3072]{1,0:T(8,128)(2,1)S(1)}, u32[]{:S(2)}, u32[]{:S(2)}) collective-permute-start(bf16[16,3072]{1,0:T(8,128)(2,1)S(1)} %get-tuple-element.50), channel_id=1, source_target_pairs={{0,1},{1,2},{2,3},{3,0},{4,5},{5,6},{6,7},{7,4},{8,9},{9,10},{10,1... | collective-permute-start | bytes 294920 | tf_op jit(solution)/shard_map/ppermute | solution.py:404
  43.6 1.8 %collective-permute-start.15 = (bf16[16,3072]{1,0:T(8,128)(2,1)S(1)}, bf16[16,3072]{1,0:T(8,128)(2,1)S(1)}, u32[]{:S(2)}, u32[]{:S(2)}) collective-permute-start(bf16[16,3072]{1,0:T(8,128)(2,1)S(1)} %get-tuple-element.51), channel_id=1, source_target_pairs={{0,3},{1,0},{2,1},{3,2},{4,7},{5,4},{6,5},{7,6},{8,11},{9,8},{10,9... | collective-permute-start | bytes 294920 | tf_op jit(solution)/shard_map/ppermute | solution.py:404
  45.4 2.7 %grad_in_partial.1 = (f32[64,3072]{1,0:T(8,128)S(1)}, bf16[64,3072]{1,0:T(8,128)(2,1)S(1)}, bf16[128,768]{1,0:T(8,128)(2,1)S(1)}, bf16[128,768]{1,0:T(8,128)(2,1)S(1)}, bf16[128,768]{1,0:T(8,128)(2,1)S(1)}) custom-call(f32[128,1536]{1,0:T(8,128)S(1)} %get-tuple-element.52.refs_0_, bf16[128,1536]{1,0:T(8,128)(2,1)S(1)} %collective-permute-done.16.refs_1_, ...), custom_call_target="tpu_custom_call" | custom-call | tf_op jit(solution)/shard_map/grad_in_partial/pallas_call | solution.py:58
  48.2 0.9 %collective-permute-done.19.refs_5_ = bf16[64,3072]{1,0:T(8,128)(2,1)S(1)} collective-permute-done((bf16[64,3072]{1,0:T(8,128)(2,1)S(1)}, bf16[64,3072]{1,0:T(8,128)(2,1)S(1)}, u32[]{:S(2)}, u32[]{:S(2)}) %collective-permute-start.19) | collective-permute-done | bytes 393248 | tf_op jit(solution)/shard_map/ppermute | solution.py:404
  49.1 1.5 %collective-permute-start.26 = (bf16[128,768]{1,0:T(8,128)(2,1)S(1)}, bf16[128,768]{1,0:T(8,128)(2,1)S(1)}, u32[]{:S(2)}, u32[]{:S(2)}) collective-permute-start(bf16[128,768]{1,0:T(8,128)(2,1)S(1)} %get-tuple-element.65), channel_id=1, source_target_pairs={{0,16},{8,24},{16,0},{24,8},{1,17},{9,25},{17,1},{25,9},{2,18},{10... | collective-permute-start | bytes 589832 | tf_op jit(solution)/shard_map/ppermute | solution.py:404
  50.7 0.8 %collective-permute-start.25 = (bf16[128,768]{1,0:T(8,128)(2,1)S(1)}, bf16[128,768]{1,0:T(8,128)(2,1)S(1)}, u32[]{:S(2)}, u32[]{:S(2)}) collective-permute-start(bf16[128,768]{1,0:T(8,128)(2,1)S(1)} %get-tuple-element.63), channel_id=1, source_target_pairs={{0,16},{8,24},{16,0},{24,8},{1,17},{9,25},{17,1},{25,9},{2,18},{10... | collective-permute-start | bytes 589832 | tf_op jit(solution)/shard_map/ppermute | solution.py:404
  51.6 0.7 %collective-permute-done.18.refs_2_ = bf16[64,3072]{1,0:T(8,128)(2,1)S(1)} collective-permute-done((bf16[64,3072]{1,0:T(8,128)(2,1)S(1)}, bf16[64,3072]{1,0:T(8,128)(2,1)S(1)}, u32[]{:S(2)}, u32[]{:S(2)}) %collective-permute-start.18) | collective-permute-done | bytes 393248 | tf_op jit(solution)/shard_map/ppermute | solution.py:407
  52.4 2.5 %collective-permute-start.23 = (bf16[16,3072]{1,0:T(8,128)(2,1)S(1)}, bf16[16,3072]{1,0:T(8,128)(2,1)S(1)}, u32[]{:S(2)}, u32[]{:S(2)}) collective-permute-start(bf16[16,3072]{1,0:T(8,128)(2,1)S(1)} %grad_in_ahead.1), channel_id=1, source_target_pairs={{0,1},{1,2},{2,3},{3,0},{4,5},{5,6},{6,7},{7,4},{8,9},{9,10},{10,1... | collective-permute-start | bytes 294920 | tf_op jit(solution)/shard_map/ppermute | solution.py:404
  55.0 1.5 %collective-permute-start.22 = (bf16[16,3072]{1,0:T(8,128)(2,1)S(1)}, bf16[16,3072]{1,0:T(8,128)(2,1)S(1)}, u32[]{:S(2)}, u32[]{:S(2)}) collective-permute-start(bf16[16,3072]{1,0:T(8,128)(2,1)S(1)} %get-tuple-element.60), channel_id=1, source_target_pairs={{0,2},{1,3},{2,0},{3,1},{4,6},{5,7},{6,4},{7,5},{8,10},{9,11},{10,... | collective-permute-start | bytes 294920 | tf_op jit(solution)/shard_map/ppermute | solution.py:404
  56.6 1.5 %collective-permute-start.24 = (bf16[16,3072]{1,0:T(8,128)(2,1)S(1)}, bf16[16,3072]{1,0:T(8,128)(2,1)S(1)}, u32[]{:S(2)}, u32[]{:S(2)}) collective-permute-start(bf16[16,3072]{1,0:T(8,128)(2,1)S(1)} %get-tuple-element.61), channel_id=1, source_target_pairs={{0,3},{1,0},{2,1},{3,2},{4,7},{5,4},{6,5},{7,6},{8,11},{9,8},{10,9... | collective-permute-start | bytes 294920 | tf_op jit(solution)/shard_map/ppermute | solution.py:404
  58.0 2.6 %grad_w_out.1 = bf16[768,3072]{1,0:T(8,128)(2,1)} custom-call(bf16[128,768]{1,0:T(8,128)(2,1)S(1)} %get-tuple-element.64.refs_0_, bf16[128,768]{1,0:T(8,128)(2,1)S(1)} %collective-permute-done.26.refs_1_, bf16[64,3072]{1,0:T(8,128)(2,1)S(1)} %get-tuple-element.58.refs_2_, bf16[32,3072]{1,0:T(8,128)(2,1)S(1)} %collective-permute-done.9.refs_2_.refs_3_, ...), custom_call_target="tpu_custom_call" | custom-call | tf_op jit(solution)/shard_map/grad_w_out/pallas_call | solution.py:58
  60.7 2.7 %grad_w_in.1 = bf16[3072,768]{1,0:T(8,128)(2,1)} custom-call(bf16[64,3072]{1,0:T(8,128)(2,1)S(1)} %get-tuple-element.55.refs_0_, bf16[64,3072]{1,0:T(8,128)(2,1)S(1)} %collective-permute-done.4.refs_1_, bf16[64,3072]{1,0:T(8,128)(2,1)S(1)} %collective-permute-done.17.refs_6_.refs_2_, bf16[64,3072]{1,0:T(8,128)(2,1)S(1)} %collective-permute-done.21.refs_5_.refs_3_, ...), custom_call_target="tpu_custom_call" | custom-call | tf_op jit(solution)/shard_map/grad_w_in/pallas_call | solution.py:58
  (41 shorter events, 3.5 us)
Async XLA Ops:
  1.6 5.1 %collective-permute-start = (bf16[8,3072]{1,0:T(8,128)(2,1)S(1)}, bf16[8,3072]{1,0:T(8,128)(2,1)S(1)}, u32[]{:S(2)}, u32[]{:S(2)}) collective-permute-start(bf16[8,3072]{1,0:T(8,128)(2,1)S(1)} %get-tuple-element.36), channel_id=1, source_target_pairs={{0,4},{4,0},{1,5},{5,1},{2,6},{6,2},{3,7},{7,3},{8,12},{12,8},{9,1... | collective-permute-start | bytes 147464 | tf_op jit(solution)/shard_map/ppermute | solution.py:404
  6.7 9.9 %collective-permute-start.1 = (bf16[16,3072]{1,0:T(8,128)(2,1)S(1)}, bf16[16,3072]{1,0:T(8,128)(2,1)S(1)}, u32[]{:S(2)}, u32[]{:S(2)}) collective-permute-start(bf16[16,3072]{1,0:T(8,128)(2,1)S(1)} %get-tuple-element.38.refs_2_), channel_id=1, source_target_pairs={{0,1},{1,2},{2,3},{3,0},{4,5},{5,6},{6,7},{7,4},{8,9},{9,10},{10,1... | collective-permute-start | bytes 294920 | tf_op jit(solution)/shard_map/ppermute | solution.py:404
  8.9 8.2 %collective-permute-start.2 = (bf16[16,3072]{1,0:T(8,128)(2,1)S(1)}, bf16[16,3072]{1,0:T(8,128)(2,1)S(1)}, u32[]{:S(2)}, u32[]{:S(2)}) collective-permute-start(bf16[16,3072]{1,0:T(8,128)(2,1)S(1)} %get-tuple-element.38.refs_2_), channel_id=1, source_target_pairs={{0,2},{1,3},{2,0},{3,1},{4,6},{5,7},{6,4},{7,5},{8,10},{9,11},{10,... | collective-permute-start | bytes 294920 | tf_op jit(solution)/shard_map/ppermute | solution.py:404
  11.5 5.7 %collective-permute-start.3 = (bf16[16,3072]{1,0:T(8,128)(2,1)S(1)}, bf16[16,3072]{1,0:T(8,128)(2,1)S(1)}, u32[]{:S(2)}, u32[]{:S(2)}) collective-permute-start(bf16[16,3072]{1,0:T(8,128)(2,1)S(1)} %get-tuple-element.38.refs_2_), channel_id=1, source_target_pairs={{0,3},{1,0},{2,1},{3,2},{4,7},{5,4},{6,5},{7,6},{8,11},{9,8},{10,9... | collective-permute-start | bytes 294920 | tf_op jit(solution)/shard_map/ppermute | solution.py:404
  17.3 4.9 %collective-permute-start.4 = (bf16[64,3072]{1,0:T(8,128)(2,1)S(1)}, bf16[64,3072]{1,0:T(8,128)(2,1)S(1)}, u32[]{:S(2)}, u32[]{:S(2)}) collective-permute-start(bf16[64,3072]{1,0:T(8,128)(2,1)S(1)} %order_tokens.1.refs_0_), channel_id=1, source_target_pairs={{0,8},{8,0},{16,24},{24,16},{1,9},{9,1},{17,25},{25,17},{2,10},{10... | collective-permute-start | bytes 1179656 | tf_op jit(solution)/shard_map/ppermute | solution.py:407
  17.3 11.6 %collective-permute-start.6 = (bf16[16,3072]{1,0:T(8,128)(2,1)S(1)}, bf16[16,3072]{1,0:T(8,128)(2,1)S(1)}, u32[]{:S(2)}, u32[]{:S(2)}) collective-permute-start(bf16[16,3072]{1,0:T(8,128)(2,1)S(1)} %get-tuple-element.41.refs_1_), channel_id=1, source_target_pairs={{0,1},{1,2},{2,3},{3,0},{4,5},{5,6},{6,7},{7,4},{8,9},{9,10},{10,1... | collective-permute-start | bytes 294920 | tf_op jit(solution)/shard_map/ppermute | solution.py:404
  19.7 9.2 %collective-permute-start.7 = (bf16[16,3072]{1,0:T(8,128)(2,1)S(1)}, bf16[16,3072]{1,0:T(8,128)(2,1)S(1)}, u32[]{:S(2)}, u32[]{:S(2)}) collective-permute-start(bf16[16,3072]{1,0:T(8,128)(2,1)S(1)} %get-tuple-element.41.refs_1_), channel_id=1, source_target_pairs={{0,2},{1,3},{2,0},{3,1},{4,6},{5,7},{6,4},{7,5},{8,10},{9,11},{10,... | collective-permute-start | bytes 294920 | tf_op jit(solution)/shard_map/ppermute | solution.py:404
  21.4 7.5 %collective-permute-start.8 = (bf16[16,3072]{1,0:T(8,128)(2,1)S(1)}, bf16[16,3072]{1,0:T(8,128)(2,1)S(1)}, u32[]{:S(2)}, u32[]{:S(2)}) collective-permute-start(bf16[16,3072]{1,0:T(8,128)(2,1)S(1)} %get-tuple-element.41.refs_1_), channel_id=1, source_target_pairs={{0,3},{1,0},{2,1},{3,2},{4,7},{5,4},{6,5},{7,6},{8,11},{9,8},{10,9... | collective-permute-start | bytes 294920 | tf_op jit(solution)/shard_map/ppermute | solution.py:404
  23.5 12.8 %collective-permute-start.5 = (bf16[128,1536]{1,0:T(8,128)(2,1)S(1)}, bf16[128,1536]{1,0:T(8,128)(2,1)S(1)}, u32[]{:S(2)}, u32[]{:S(2)}) collective-permute-start(bf16[128,1536]{1,0:T(8,128)(2,1)S(1)} %get-tuple-element.40.refs_2_), channel_id=1, source_target_pairs={{0,4},{4,0},{1,5},{5,1},{2,6},{6,2},{3,7},{7,3},{8,12},{12,8},{9,1... | collective-permute-start | bytes 1179656 | tf_op jit(solution)/shard_map/ppermute | solution.py:404
  29.0 2.1 %collective-permute-start.10 = (bf16[32,3072]{1,0:T(8,128)(2,1)S(1)}, bf16[32,3072]{1,0:T(8,128)(2,1)S(1)}, u32[]{:S(2)}, u32[]{:S(2)}) collective-permute-start(bf16[32,3072]{1,0:T(8,128)(2,1)S(1)} %get-tuple-element.43.refs_1_), channel_id=1, source_target_pairs={{0,8},{8,0},{16,24},{24,16},{1,9},{9,1},{17,25},{25,17},{2,10},{10... | collective-permute-start | bytes 589832 | tf_op jit(solution)/shard_map/ppermute | solution.py:407
  29.1 2.0 %collective-permute-start.9 = (bf16[32,3072]{1,0:T(8,128)(2,1)S(1)}, bf16[32,3072]{1,0:T(8,128)(2,1)S(1)}, u32[]{:S(2)}, u32[]{:S(2)}) collective-permute-start(bf16[32,3072]{1,0:T(8,128)(2,1)S(1)} %get-tuple-element.42.refs_0_), channel_id=1, source_target_pairs={{0,8},{8,0},{16,24},{24,16},{1,9},{9,1},{17,25},{25,17},{2,10},{10... | collective-permute-start | bytes 589832 | tf_op jit(solution)/shard_map/ppermute | solution.py:407
  29.6 14.0 %collective-permute-start.17 = (bf16[64,3072]{1,0:T(8,128)(2,1)S(1)}, bf16[64,3072]{1,0:T(8,128)(2,1)S(1)}, u32[]{:S(2)}, u32[]{:S(2)}) collective-permute-start(bf16[64,3072]{1,0:T(8,128)(2,1)S(1)} %get-tuple-element.55.refs_0_), channel_id=1, source_target_pairs={{0,16},{8,24},{16,0},{24,8},{1,17},{9,25},{17,1},{25,9},{2,18},{10... | collective-permute-start | bytes 1179656 | tf_op jit(solution)/shard_map/ppermute | solution.py:404
  33.8 11.6 %collective-permute-start.16 = (bf16[128,1536]{1,0:T(8,128)(2,1)S(1)}, bf16[128,1536]{1,0:T(8,128)(2,1)S(1)}, u32[]{:S(2)}, u32[]{:S(2)}) collective-permute-start(bf16[128,1536]{1,0:T(8,128)(2,1)S(1)} %get-tuple-element.44.refs_3_), channel_id=1, source_target_pairs={{0,4},{4,0},{1,5},{5,1},{2,6},{6,2},{3,7},{7,3},{8,12},{12,8},{9,1... | collective-permute-start | bytes 1179656 | tf_op jit(solution)/shard_map/ppermute | solution.py:404
  35.2 13.9 %collective-permute-start.19 = (bf16[64,3072]{1,0:T(8,128)(2,1)S(1)}, bf16[64,3072]{1,0:T(8,128)(2,1)S(1)}, u32[]{:S(2)}, u32[]{:S(2)}) collective-permute-start(bf16[64,3072]{1,0:T(8,128)(2,1)S(1)} %get-tuple-element.58.refs_2_), channel_id=1, source_target_pairs={{0,16},{8,24},{16,0},{24,8},{1,17},{9,25},{17,1},{25,9},{2,18},{10... | collective-permute-start | bytes 1179656 | tf_op jit(solution)/shard_map/ppermute | solution.py:404
  38.0 1.5 %collective-permute-start.11 = (bf16[32,3072]{1,0:T(8,128)(2,1)S(1)}, bf16[32,3072]{1,0:T(8,128)(2,1)S(1)}, u32[]{:S(2)}, u32[]{:S(2)}) collective-permute-start(bf16[32,3072]{1,0:T(8,128)(2,1)S(1)} %get-tuple-element.46), channel_id=1, source_target_pairs={{0,8},{8,0},{16,24},{24,16},{1,9},{9,1},{17,25},{25,17},{2,10},{10... | collective-permute-start | bytes 589832 | tf_op jit(solution)/shard_map/ppermute | solution.py:407
  38.1 1.7 %collective-permute-start.12 = (bf16[32,3072]{1,0:T(8,128)(2,1)S(1)}, bf16[32,3072]{1,0:T(8,128)(2,1)S(1)}, u32[]{:S(2)}, u32[]{:S(2)}) collective-permute-start(bf16[32,3072]{1,0:T(8,128)(2,1)S(1)} %get-tuple-element.47), channel_id=1, source_target_pairs={{0,8},{8,0},{16,24},{24,16},{1,9},{9,1},{17,25},{25,17},{2,10},{10... | collective-permute-start | bytes 589832 | tf_op jit(solution)/shard_map/ppermute | solution.py:407
  40.0 10.7 %collective-permute-start.13 = (bf16[16,3072]{1,0:T(8,128)(2,1)S(1)}, bf16[16,3072]{1,0:T(8,128)(2,1)S(1)}, u32[]{:S(2)}, u32[]{:S(2)}) collective-permute-start(bf16[16,3072]{1,0:T(8,128)(2,1)S(1)} %get-tuple-element.49), channel_id=1, source_target_pairs={{0,2},{1,3},{2,0},{3,1},{4,6},{5,7},{6,4},{7,5},{8,10},{9,11},{10,... | collective-permute-start | bytes 294920 | tf_op jit(solution)/shard_map/ppermute | solution.py:404
  41.6 9.1 %collective-permute-start.14 = (bf16[16,3072]{1,0:T(8,128)(2,1)S(1)}, bf16[16,3072]{1,0:T(8,128)(2,1)S(1)}, u32[]{:S(2)}, u32[]{:S(2)}) collective-permute-start(bf16[16,3072]{1,0:T(8,128)(2,1)S(1)} %get-tuple-element.50), channel_id=1, source_target_pairs={{0,1},{1,2},{2,3},{3,0},{4,5},{5,6},{6,7},{7,4},{8,9},{9,10},{10,1... | collective-permute-start | bytes 294920 | tf_op jit(solution)/shard_map/ppermute | solution.py:404
  43.6 7.9 %collective-permute-start.15 = (bf16[16,3072]{1,0:T(8,128)(2,1)S(1)}, bf16[16,3072]{1,0:T(8,128)(2,1)S(1)}, u32[]{:S(2)}, u32[]{:S(2)}) collective-permute-start(bf16[16,3072]{1,0:T(8,128)(2,1)S(1)} %get-tuple-element.51), channel_id=1, source_target_pairs={{0,3},{1,0},{2,1},{3,2},{4,7},{5,4},{6,5},{7,6},{8,11},{9,8},{10,9... | collective-permute-start | bytes 294920 | tf_op jit(solution)/shard_map/ppermute | solution.py:404
  45.4 9.5 %collective-permute-start.21 = (bf16[64,3072]{1,0:T(8,128)(2,1)S(1)}, bf16[64,3072]{1,0:T(8,128)(2,1)S(1)}, u32[]{:S(2)}, u32[]{:S(2)}) collective-permute-start(bf16[64,3072]{1,0:T(8,128)(2,1)S(1)} %collective-permute-done.17.refs_6_.refs_2_), channel_id=1, source_target_pairs={{0,8},{8,0},{16,24},{24,16},{1,9},{9,1},{17,25},{25,17},{2,10},{10... | collective-permute-start | bytes 1179656 | tf_op jit(solution)/shard_map/ppermute | solution.py:407
  49.1 8.9 %collective-permute-start.26 = (bf16[128,768]{1,0:T(8,128)(2,1)S(1)}, bf16[128,768]{1,0:T(8,128)(2,1)S(1)}, u32[]{:S(2)}, u32[]{:S(2)}) collective-permute-start(bf16[128,768]{1,0:T(8,128)(2,1)S(1)} %get-tuple-element.65), channel_id=1, source_target_pairs={{0,16},{8,24},{16,0},{24,8},{1,17},{9,25},{17,1},{25,9},{2,18},{10... | collective-permute-start | bytes 589832 | tf_op jit(solution)/shard_map/ppermute | solution.py:404
  50.6 1.7 %collective-permute-start.18 = (bf16[64,3072]{1,0:T(8,128)(2,1)S(1)}, bf16[64,3072]{1,0:T(8,128)(2,1)S(1)}, u32[]{:S(2)}, u32[]{:S(2)}) collective-permute-start(bf16[64,3072]{1,0:T(8,128)(2,1)S(1)} %get-tuple-element.57), channel_id=1, source_target_pairs={{0,8},{8,0},{16,24},{24,16},{1,9},{9,1},{17,25},{25,17},{2,10},{10... | collective-permute-start | bytes 1179656 | tf_op jit(solution)/shard_map/ppermute | solution.py:407
  50.7 9.9 %collective-permute-start.25 = (bf16[128,768]{1,0:T(8,128)(2,1)S(1)}, bf16[128,768]{1,0:T(8,128)(2,1)S(1)}, u32[]{:S(2)}, u32[]{:S(2)}) collective-permute-start(bf16[128,768]{1,0:T(8,128)(2,1)S(1)} %get-tuple-element.63), channel_id=1, source_target_pairs={{0,16},{8,24},{16,0},{24,8},{1,17},{9,25},{17,1},{25,9},{2,18},{10... | collective-permute-start | bytes 589832 | tf_op jit(solution)/shard_map/ppermute | solution.py:404
  51.5 3.4 %collective-permute-start.20 = (bf16[64,3072]{1,0:T(8,128)(2,1)S(1)}, bf16[64,3072]{1,0:T(8,128)(2,1)S(1)}, u32[]{:S(2)}, u32[]{:S(2)}) collective-permute-start(bf16[64,3072]{1,0:T(8,128)(2,1)S(1)} %collective-permute-done.19.refs_5_), channel_id=1, source_target_pairs={{0,8},{8,0},{16,24},{24,16},{1,9},{9,1},{17,25},{25,17},{2,10},{10... | collective-permute-start | bytes 1179656 | tf_op jit(solution)/shard_map/ppermute | solution.py:407
  51.6 12.5 %copy-start = (bf16[16,3072]{1,0:T(8,128)(2,1)}, bf16[16,3072]{1,0:T(8,128)(2,1)S(1)}, u32[]{:S(2)}) copy-start(bf16[16,3072]{1,0:T(8,128)(2,1)S(1)} %add_convert_fusion.1.refs_3_) | copy-start | bytes 294916
  52.4 10.9 %collective-permute-start.23 = (bf16[16,3072]{1,0:T(8,128)(2,1)S(1)}, bf16[16,3072]{1,0:T(8,128)(2,1)S(1)}, u32[]{:S(2)}, u32[]{:S(2)}) collective-permute-start(bf16[16,3072]{1,0:T(8,128)(2,1)S(1)} %grad_in_ahead.1), channel_id=1, source_target_pairs={{0,1},{1,2},{2,3},{3,0},{4,5},{5,6},{6,7},{7,4},{8,9},{9,10},{10,1... | collective-permute-start | bytes 294920 | tf_op jit(solution)/shard_map/ppermute | solution.py:404
  55.0 8.4 %collective-permute-start.22 = (bf16[16,3072]{1,0:T(8,128)(2,1)S(1)}, bf16[16,3072]{1,0:T(8,128)(2,1)S(1)}, u32[]{:S(2)}, u32[]{:S(2)}) collective-permute-start(bf16[16,3072]{1,0:T(8,128)(2,1)S(1)} %get-tuple-element.60), channel_id=1, source_target_pairs={{0,2},{1,3},{2,0},{3,1},{4,6},{5,7},{6,4},{7,5},{8,10},{9,11},{10,... | collective-permute-start | bytes 294920 | tf_op jit(solution)/shard_map/ppermute | solution.py:404
  56.6 6.9 %collective-permute-start.24 = (bf16[16,3072]{1,0:T(8,128)(2,1)S(1)}, bf16[16,3072]{1,0:T(8,128)(2,1)S(1)}, u32[]{:S(2)}, u32[]{:S(2)}) collective-permute-start(bf16[16,3072]{1,0:T(8,128)(2,1)S(1)} %get-tuple-element.61), channel_id=1, source_target_pairs={{0,3},{1,0},{2,1},{3,2},{4,7},{5,4},{6,5},{7,6},{8,11},{9,8},{10,9... | collective-permute-start | bytes 294920 | tf_op jit(solution)/shard_map/ppermute | solution.py:404
